TPU v7x, 32 devices: a whole 2x2x4 slice. The times are simulated.
32 devices in a mesh: dp: 4 (over y, core), fsdp: 8 (over z, x).
Axes of the slice: x: 2, y: 2, z: 4, core: 2. Of those that a mesh axis runs over, the one named last changes fastest.
Arguments:
- frames: bfloat16 [32, 256, 1024], P(('dp', 'fsdp')), may hold values from -6 to 6
- lengths: int32 [32], P(('dp', 'fsdp')), may hold values from 64 to 256
- cotangent: bfloat16 [32, 256, 1024], P(('dp', 'fsdp')), may hold values from -6 to 6
- panels: bfloat16 [23, 1024, 1024], P(None, 'fsdp')
- vectors: float32 [34, 1024], replicated
- vector_first: float32 [34, 1024], replicated, may hold values from -72.40774 to 72.40774
- vector_second: float32 [34, 1024], replicated, may hold values from 81.92 to 1228.8
- owners: int32 [23], replicated, may hold values from 0 to 7, as said below
- basis_left: float32 [24, 1024, 1024], P('fsdp'), may hold values from -0.1875 to 0.1875
- basis_right: float32 [24, 1024, 1024], P('fsdp'), may hold values from -0.1875 to 0.1875
- panel_first: float32 [1024, 24, 1024], P('dp', 'fsdp'), may hold values from -72.40774 to 72.40774
- panel_second: float32 [1024, 24, 1024], P('dp', 'fsdp'), may hold values from 81.92 to 1228.8
- panel_master: float32 [1024, 24, 1024], P('dp', 'fsdp'), may hold values from -0.1875 to 0.1875
Outputs:
- layer_out: bfloat16 [32, 256, 1024], P(('dp', 'fsdp'))
- frames_grad: bfloat16 [32, 256, 1024], P(('dp', 'fsdp'))
- panel_grads: float32 [23, 1024, 1024], P(None, 'fsdp', 'dp')
- vector_grads: float32 [34, 1024], replicated
- vector_first_new: float32 [34, 1024], replicated
- vector_second_new: float32 [34, 1024], replicated
- vectors_new: float32 [34, 1024], replicated
- panel_first_new: float32 [1024, 24, 1024], P('dp', 'fsdp')
- panel_second_new: float32 [1024, 24, 1024], P('dp', 'fsdp')
- panel_master_new: float32 [1024, 24, 1024], P('dp', 'fsdp')
Inputs may be any that keep to these rules, and one draw needn't show every extreme that they name: `owners`: every index along fsdp owns at most 3 panels, and some own exactly 3.
All inputs are finite; a program needn't handle non-finite values.
Results may differ from a plain program's by a relative error of at most 0.023.
Values may be sent and summed in bfloat16 or wider, within the bound.
No kernel may reach another device: no remote copies, remote signals or barrier semaphores. Data moves between devices by JAX's collectives and lax.ppermute only.
A program may use at most 384 MiB of HBM per device.

v0:
```python
import jax
import jax.numpy as jnp
from jax import lax
from jax.sharding import PartitionSpec as P

HEADS = 8
KERNEL = 5
STEPS = 4


norm_eps = 1e-05
adam_eps = 1e-08
beta_one = 0.5
beta_two = 0.5
learn_rate = 0.02
vector_rate = 0.25


def layer_norm(values, gain_row, shift_row):
    centred = values - jnp.mean(values, axis=-1, keepdims=True)
    inverse = lax.rsqrt(jnp.mean(centred * centred, axis=-1, keepdims=True) + norm_eps)
    return centred * inverse * gain_row + shift_row


def conv_piece(wide, kernel, conv_bias, gain_row, shift_row, frame_mask):
    gated = wide[:, :, 0] * jax.nn.sigmoid(wide[:, :, 1])
    gated = gated * frame_mask[:, :, None]
    seq_len = gated.shape[1]
    margin = KERNEL // 2
    padded = jnp.pad(gated, ((0, 0), (margin, margin), (0, 0)))
    depthwise = conv_bias + kernel[0] * padded[:, 0:seq_len]
    for tap_index in range(1, KERNEL):
        depthwise = depthwise + kernel[tap_index] * padded[:, tap_index : tap_index + seq_len]
    return jax.nn.silu(layer_norm(depthwise, gain_row, shift_row))


def adam_step(first_new, second_new):
    return (
        first_new
        / (1.0 - beta_one**STEPS)
        / (jnp.sqrt(second_new / (1.0 - beta_two**STEPS)) + adam_eps)
    )


def fetch_block(panel_rows):
    return lax.all_gather(panel_rows, "fsdp", axis=1, tiled=True)


def fetch_again(panel_rows):
    return lax.all_gather(panel_rows, "fsdp", axis=1, tiled=True)


def reduce_rows(matrices):
    return lax.psum_scatter(
        matrices.astype(jnp.bfloat16), "fsdp", scatter_dimension=1, tiled=True
    ).astype(jnp.float32)


def token_sum(values):
    return jnp.sum(values, axis=(0, 1), dtype=jnp.float32)


def norm_backward(residual, gain_row, shift_row, normed_grad):
    ignored, pull_back = jax.vjp(layer_norm, residual, gain_row, shift_row)
    return pull_back(normed_grad)


def ffn_forward(residual, weights, gain_row, shift_row, bias_in, bias_out):
    normed_low = layer_norm(residual, gain_row, shift_row).astype(jnp.bfloat16)
    hidden = (
        jnp.einsum("bld,pdc->blpc", normed_low, weights[0:4], preferred_element_type=jnp.float32)
        + bias_in
    )
    active_low = jax.nn.silu(hidden).astype(jnp.bfloat16)
    branch = (
        jnp.einsum("blpc,pcd->bld", active_low, weights[4:8], preferred_element_type=jnp.float32)
        + bias_out
    )
    return (residual + 0.5 * branch, (normed_low, hidden, active_low))


def ffn_backward(grad_out, residual, weights, gain_row, shift_row, kept):
    normed_low, hidden, active_low = kept
    branch_grad = (0.5 * grad_out).astype(jnp.bfloat16)
    out_matrix = jnp.einsum(
        "blpc,bld->pcd", active_low, branch_grad, preferred_element_type=jnp.float32
    )
    active_grad = jnp.einsum(
        "bld,pcd->blpc", branch_grad, weights[4:8], preferred_element_type=jnp.float32
    )
    sigmoid_values = jax.nn.sigmoid(hidden)
    hidden_grad = (active_grad * sigmoid_values * (1.0 + hidden * (1.0 - sigmoid_values))).astype(
        jnp.bfloat16
    )
    in_matrix = jnp.einsum(
        "bld,blpc->pdc", normed_low, hidden_grad, preferred_element_type=jnp.float32
    )
    normed_grad = jnp.einsum(
        "blpc,pdc->bld", hidden_grad, weights[0:4], preferred_element_type=jnp.float32
    )
    residual_grad, gain_grad, shift_grad = norm_backward(residual, gain_row, shift_row, normed_grad)
    matrices = jnp.concatenate([in_matrix, out_matrix], axis=0)
    row_grads = [gain_grad, shift_grad, token_sum(hidden_grad), token_sum(branch_grad)]
    return (grad_out + residual_grad, matrices, row_grads)


def split_heads(projected):
    seq_count, seq_len = (projected.shape[0], projected.shape[1])
    heads = projected.reshape(seq_count, seq_len, 3, HEADS, -1)
    return (heads[:, :, 0], heads[:, :, 1], heads[:, :, 2])


def masked_scores(queries, key_heads, frame_mask, score_scale):
    scores = (
        jnp.einsum("blhe,bmhe->bhlm", queries, key_heads, preferred_element_type=jnp.float32)
        * score_scale
    )
    return jnp.where(frame_mask[:, None, None, :] > 0, scores, -1000000000.0)


def attention_forward(residual, weights, vectors, frame_mask):
    seq_count, seq_len, model_width = residual.shape
    score_scale = (model_width // HEADS) ** (-0.5)
    normed_low = layer_norm(residual, vectors[2], vectors[3]).astype(jnp.bfloat16)
    biases = jnp.stack([vectors[22], jnp.zeros_like(vectors[22]), vectors[23]])
    projected = (
        jnp.einsum("bld,pdc->blpc", normed_low, weights[0:3], preferred_element_type=jnp.float32)
        + biases
    )
    projected = projected.astype(jnp.bfloat16)
    queries, key_heads, value_heads = split_heads(projected)
    scores = masked_scores(queries, key_heads, frame_mask, score_scale)
    log_total = jax.nn.logsumexp(scores, axis=-1)
    soft_low = jnp.exp(scores - log_total[..., None]).astype(jnp.bfloat16)
    mixed = jnp.einsum("bhlm,bmhe->blhe", soft_low, value_heads, preferred_element_type=jnp.float32)
    mixed_low = mixed.reshape(seq_count, seq_len, model_width).astype(jnp.bfloat16)
    branch = (
        jnp.einsum("bld,dc->blc", mixed_low, weights[3], preferred_element_type=jnp.float32)
        + vectors[24]
    )
    return (residual + branch, (normed_low, projected, log_total, mixed_low))


def attention_backward(grad_out, residual, weights, vectors, kept, frame_mask):
    seq_count, seq_len, model_width = residual.shape
    score_scale = (model_width // HEADS) ** (-0.5)
    normed_low, projected, log_total, mixed_low = kept
    branch_grad = grad_out.astype(jnp.bfloat16)
    out_matrix = jnp.einsum(
        "bld,blc->dc", mixed_low, branch_grad, preferred_element_type=jnp.float32
    )
    mixed_grad = jnp.einsum(
        "blc,dc->bld", branch_grad, weights[3], preferred_element_type=jnp.float32
    )
    mixed_grad = mixed_grad.astype(jnp.bfloat16).reshape(seq_count, seq_len, HEADS, -1)
    queries, key_heads, value_heads = split_heads(projected)
    scores = masked_scores(queries, key_heads, frame_mask, score_scale)
    soft = jnp.exp(scores - log_total[..., None])
    soft_grad = jnp.einsum(
        "blhe,bmhe->bhlm", mixed_grad, value_heads, preferred_element_type=jnp.float32
    )
    value_grad = jnp.einsum(
        "bhlm,blhe->bmhe", soft.astype(jnp.bfloat16), mixed_grad, preferred_element_type=jnp.float32
    )
    score_grad = (soft * (soft_grad - jnp.sum(soft_grad * soft, axis=-1, keepdims=True))).astype(
        jnp.bfloat16
    )
    query_grad = (
        jnp.einsum("bhlm,bmhe->blhe", score_grad, key_heads, preferred_element_type=jnp.float32)
        * score_scale
    )
    key_grad = (
        jnp.einsum("bhlm,blhe->bmhe", score_grad, queries, preferred_element_type=jnp.float32)
        * score_scale
    )
    projected_grad = jnp.stack([query_grad, key_grad, value_grad], axis=2)
    projected_grad = projected_grad.reshape(seq_count, seq_len, 3, model_width).astype(jnp.bfloat16)
    in_matrix = jnp.einsum(
        "bld,blpc->pdc", normed_low, projected_grad, preferred_element_type=jnp.float32
    )
    normed_grad = jnp.einsum(
        "blpc,pdc->bld", projected_grad, weights[0:3], preferred_element_type=jnp.float32
    )
    residual_grad, gain_grad, shift_grad = norm_backward(
        residual, vectors[2], vectors[3], normed_grad
    )
    projected_sums = token_sum(projected_grad)
    matrices = jnp.concatenate([in_matrix, out_matrix[None]], axis=0)
    row_grads = [
        gain_grad,
        shift_grad,
        projected_sums[0],
        projected_sums[2],
        token_sum(branch_grad),
    ]
    return (grad_out + residual_grad, matrices, row_grads)


def conv_forward(residual, weights, vectors, frame_mask):
    normed_low = layer_norm(residual, vectors[4], vectors[5]).astype(jnp.bfloat16)
    wide = (
        jnp.einsum("bld,pdc->blpc", normed_low, weights[0:2], preferred_element_type=jnp.float32)
        + vectors[25:27]
    )
    active_low = conv_piece(
        wide, vectors[28:33], vectors[27], vectors[6], vectors[7], frame_mask
    ).astype(jnp.bfloat16)
    branch = (
        jnp.einsum("bld,dc->blc", active_low, weights[2], preferred_element_type=jnp.float32)
        + vectors[33]
    )
    return (residual + branch, (normed_low, wide, active_low))


def conv_backward(grad_out, residual, weights, vectors, kept, frame_mask):
    normed_low, wide, active_low = kept
    branch_grad = grad_out.astype(jnp.bfloat16)
    out_matrix = jnp.einsum(
        "bld,blc->dc", active_low, branch_grad, preferred_element_type=jnp.float32
    )
    active_grad = jnp.einsum(
        "blc,dc->bld", branch_grad, weights[2], preferred_element_type=jnp.float32
    )

    def local_piece(wide_in, kernel, conv_bias, gain_row, shift_row):
        return conv_piece(wide_in, kernel, conv_bias, gain_row, shift_row, frame_mask)

    ignored, pull_back = jax.vjp(
        local_piece, wide, vectors[28:33], vectors[27], vectors[6], vectors[7]
    )
    wide_grad, kernel_grad, bias_grad, norm_gain_grad, norm_shift_grad = pull_back(active_grad)
    wide_low = wide_grad.astype(jnp.bfloat16)
    in_matrix = jnp.einsum(
        "bld,blpc->pdc", normed_low, wide_low, preferred_element_type=jnp.float32
    )
    normed_grad = jnp.einsum(
        "blpc,pdc->bld", wide_low, weights[0:2], preferred_element_type=jnp.float32
    )
    residual_grad, gain_grad, shift_grad = norm_backward(
        residual, vectors[4], vectors[5], normed_grad
    )
    matrices = jnp.concatenate([in_matrix, out_matrix[None]], axis=0)
    row_grads = [
        gain_grad,
        shift_grad,
        norm_gain_grad,
        norm_shift_grad,
        token_sum(wide_low),
        bias_grad,
        kernel_grad,
        token_sum(branch_grad),
    ]
    return (grad_out + residual_grad, matrices, row_grads)


def on_device(
    frames,
    lengths,
    cotangent,
    panels,
    vectors,
    vector_first,
    vector_second,
    owners,
    basis_left,
    basis_right,
    panel_first,
    panel_second,
    panel_master,
):
    seq_count, seq_len, model_width = frames.shape
    positions = lax.broadcasted_iota(jnp.int32, (seq_count, seq_len), 1)
    frame_mask = (positions < lengths[:, None]).astype(jnp.float32)
    ffn_first = fetch_block(panels[0:8])
    after_first, kept_first = ffn_forward(
        frames.astype(jnp.float32), ffn_first, vectors[0], vectors[1], vectors[12:16], vectors[16]
    )
    attn_weights = fetch_block(panels[8:12])
    after_attn, kept_attn = attention_forward(after_first, attn_weights, vectors, frame_mask)
    conv_weights = fetch_block(panels[12:15])
    after_conv, kept_conv = conv_forward(after_attn, conv_weights, vectors, frame_mask)
    ffn_second = fetch_block(panels[15:23])
    after_second, kept_second = ffn_forward(
        after_conv, ffn_second, vectors[8], vectors[9], vectors[17:21], vectors[21]
    )
    layer_out = layer_norm(after_second, vectors[10], vectors[11]).astype(jnp.bfloat16)
    out_grad = cotangent.astype(jnp.float32) * frame_mask[:, :, None]
    grad_flow, final_gain, final_shift = norm_backward(
        after_second, vectors[10], vectors[11], out_grad
    )
    ffn_second = fetch_again(panels[15:23])
    conv_weights = fetch_again(panels[12:15])
    attn_weights = fetch_again(panels[8:12])
    ffn_first = fetch_again(panels[0:8])
    grad_flow, second_mats, second_rows = ffn_backward(
        grad_flow, after_conv, ffn_second, vectors[8], vectors[9], kept_second
    )
    second_shard = reduce_rows(second_mats)
    grad_flow, conv_mats, conv_rows = conv_backward(
        grad_flow, after_attn, conv_weights, vectors, kept_conv, frame_mask
    )
    conv_shard = reduce_rows(conv_mats)
    grad_flow, attn_mats, attn_rows = attention_backward(
        grad_flow, after_first, attn_weights, vectors, kept_attn, frame_mask
    )
    attn_shard = reduce_rows(attn_mats)
    grad_flow, first_mats, first_rows = ffn_backward(
        grad_flow, frames.astype(jnp.float32), ffn_first, vectors[0], vectors[1], kept_first
    )
    first_shard = reduce_rows(first_mats)
    frames_grad = grad_flow.astype(jnp.bfloat16)
    vector_grad = jnp.concatenate(
        [
            first_rows[0][None],
            first_rows[1][None],
            attn_rows[0][None],
            attn_rows[1][None],
            conv_rows[0][None],
            conv_rows[1][None],
            conv_rows[2][None],
            conv_rows[3][None],
            second_rows[0][None],
            second_rows[1][None],
            final_gain[None],
            final_shift[None],
            first_rows[2],
            first_rows[3][None],
            second_rows[2],
            second_rows[3][None],
            attn_rows[2][None],
            attn_rows[3][None],
            attn_rows[4][None],
            conv_rows[4],
            conv_rows[5][None],
            conv_rows[6],
            conv_rows[7][None],
        ],
        axis=0,
    )
    vector_grads = lax.psum(vector_grad, ("dp", "fsdp"))
    vector_first_new = beta_one * vector_first + (1.0 - beta_one) * vector_grads
    vector_second_new = beta_two * vector_second + (1.0 - beta_two) * vector_grads * vector_grads
    vectors_new = vectors - vector_rate * adam_step(vector_first_new, vector_second_new)
    row_shards = jnp.concatenate([first_shard, attn_shard, conv_shard, second_shard], axis=0)
    dp_count = lax.axis_size("dp")
    dp_rank = lax.axis_index("dp")
    col_count = model_width // dp_count
    panel_grads = lax.psum_scatter(
        row_shards.astype(jnp.bfloat16), "dp", scatter_dimension=2, tiled=True
    ).astype(jnp.float32)
    fsdp_count = lax.axis_size("fsdp")
    fsdp_rank = lax.axis_index("fsdp")
    slot_count = panel_first.shape[1]
    panel_count = owners.shape[0]
    panel_index = jnp.arange(panel_count, dtype=jnp.int32)
    same_owner = owners[:, None] == owners[None, :]
    earlier = panel_index[None, :] < panel_index[:, None]
    slot_of = jnp.sum((same_owner & earlier).astype(jnp.int32), axis=1)
    target = owners * slot_count + slot_of
    slot_hit = target[:, None] == jnp.arange(fsdp_count * slot_count, dtype=jnp.int32)[None, :]
    source = jnp.sum(slot_hit.astype(jnp.int32) * panel_index[:, None], axis=0)
    filled = jnp.any(slot_hit, axis=0)
    source_order = source.reshape(fsdp_count, slot_count).T.reshape(-1)
    filled_order = filled.reshape(fsdp_count, slot_count).T.reshape(-1)
    outgoing = jnp.where(
        filled_order[:, None, None], jnp.take(panel_grads, source_order, axis=0), 0.0
    )
    outgoing = outgoing.reshape(slot_count, fsdp_count, panel_grads.shape[1], col_count)
    incoming = lax.all_to_all(
        outgoing.astype(jnp.bfloat16), "fsdp", split_axis=1, concat_axis=1, tiled=True
    ).astype(outgoing.dtype)
    whole_grads = incoming.reshape(slot_count, model_width, col_count)
    mine = lax.dynamic_slice_in_dim(filled, fsdp_rank * slot_count, slot_count)
    turned = jnp.einsum("srk,src->skc", basis_left, whole_grads, precision=lax.Precision.HIGHEST)
    right_rows = lax.dynamic_slice_in_dim(basis_right, dp_rank * col_count, col_count, 1)
    part_rows = turned
    rotated = lax.psum_scatter(
        jnp.einsum("skc,scx->ksx", part_rows, right_rows, precision=lax.Precision.HIGHEST).astype(
            jnp.bfloat16
        ),
        "dp",
        scatter_dimension=0,
        tiled=True,
    ).astype(jnp.float32)
    first_new = beta_one * panel_first + (1.0 - beta_one) * rotated
    second_new = beta_two * panel_second + (1.0 - beta_two) * rotated * rotated
    step_values = adam_step(first_new, second_new)
    back_turn = jnp.einsum(
        "rsc,sxc->rsx", step_values, basis_right, precision=lax.Precision.HIGHEST
    )
    left_cols = lax.dynamic_slice_in_dim(basis_left, dp_rank * col_count, col_count, 2)
    part_rows = left_cols
    update = lax.psum_scatter(
        jnp.einsum("sak,ksx->asx", part_rows, back_turn, precision=lax.Precision.HIGHEST).astype(
            jnp.bfloat16
        ),
        "dp",
        scatter_dimension=0,
        tiled=True,
    ).astype(jnp.float32)
    keep_slot = mine[None, :, None]
    master_new = jnp.where(keep_slot, panel_master - learn_rate * update, 0.0)
    first_new = jnp.where(keep_slot, first_new, 0.0)
    second_new = jnp.where(keep_slot, second_new, 0.0)
    return (
        layer_out,
        frames_grad,
        panel_grads,
        vector_grads,
        vector_first_new,
        vector_second_new,
        vectors_new,
        first_new,
        second_new,
        master_new,
    )


def solution(mesh):
    return jax.shard_map(
        on_device,
        mesh=mesh,
        in_specs=(
            P(("dp", "fsdp"), None, None),
            P(("dp", "fsdp")),
            P(("dp", "fsdp"), None, None),
            P(None, "fsdp", None),
            P(),
            P(),
            P(),
            P(),
            P("fsdp", None, None),
            P("fsdp", None, None),
            P("dp", "fsdp", None),
            P("dp", "fsdp", None),
            P("dp", "fsdp", None),
        ),
        out_specs=(
            P(("dp", "fsdp"), None, None),
            P(("dp", "fsdp"), None, None),
            P(None, "fsdp", "dp"),
            P(),
            P(),
            P(),
            P(),
            P("dp", "fsdp", None),
            P("dp", "fsdp", None),
            P("dp", "fsdp", None),
        ),
        check_vma=False,
    )
```

profile of v0, /device:TPU:1, one launch (start us, length us, event | category | flops | bytes accessed | tf_op | source)
XLA Modules:
  0.0 2024.8 jit_solution(4223456331468071224)
XLA Ops:
  7.2 4.8 fusion.180
  19.3 222.2 %all-gather.5.cloned.1.call-done = bf16[8,1024,1024]{2,1,0:T(8,128)(2,1)} async-done(((bf16[8,128,1024]{2,1,0:T(8,128)(2,1)}), bf16[8,1024,1024]{2,1,0:T(8,128)(2,1)}) %all-gather.5.cloned.1.call-update) | async-done | bytes 16777232 | tf_op jit(solution)/shard_map/all_gather | solution.py:46
  241.5 5.8 fusion.14
  247.4 8.2 fusion.186
  255.9 111.5 %all-gather.7.cloned.1.call-done = bf16[4,1024,1024]{2,1,0:T(8,128)(2,1)} async-done(((bf16[4,128,1024]{2,1,0:T(8,128)(2,1)}), bf16[4,1024,1024]{2,1,0:T(8,128)(2,1)}) %all-gather.7.cloned.1.call-update) | async-done | bytes 8388624 | tf_op jit(solution)/shard_map/all_gather | solution.py:46
  367.4 4.7 add_convert_fusion
  379.6 87.1 %all-gather.9.cloned.1.call-done = bf16[3,1024,1024]{2,1,0:T(8,128)(2,1)} async-done(((bf16[3,128,1024]{2,1,0:T(8,128)(2,1)}), bf16[3,1024,1024]{2,1,0:T(8,128)(2,1)}) %all-gather.9.cloned.1.call-update) | async-done | bytes 6291472 | tf_op jit(solution)/shard_map/all_gather | solution.py:46
  477.3 218.0 %all-gather.11.cloned.1.call-done = bf16[8,1024,1024]{2,1,0:T(8,128)(2,1)} async-done(((bf16[8,128,1024]{2,1,0:T(8,128)(2,1)}), bf16[8,1024,1024]{2,1,0:T(8,128)(2,1)}) %all-gather.11.cloned.1.call-update) | async-done | bytes 16777232 | tf_op jit(solution)/shard_map/all_gather | solution.py:46
  695.3 6.2 fusion.6
  701.5 7.5 fusion.190
  712.6 7.6 convert_reduce_fusion
  720.2 7.3 fusion.112
  743.8 14.4 copy.198
  758.2 10.2 copy.211
  768.7 4.9 fusion.113
  792.0 4.7 convert_bitcast_fusion.4
  796.7 6.9 pad_maximum_fusion.2
  803.6 15.3 copy.196
  819.0 12.1 copy.210
  832.3 4.2 convert_bitcast_fusion
  836.6 5.0 convolution_convert_fusion
  841.6 6.7 pad_maximum_fusion.1
  848.3 24.0 %copy.200 = bf16[8,1024,1024]{2,0,1:T(8,128)(2,1)} copy(bf16[8,1024,1024]{1,2,0:T(8,128)(2,1)} %pad_maximum_fusion.1) | data formatting | bytes 33554432
  872.3 18.7 copy.212
  891.1 5.0 fusion.114
  899.3 6.9 convert_reduce_fusion.1
  910.2 5.0 convolution_convert_fusion.1
  915.2 6.8 pad_maximum_fusion
  922.0 24.1 %copy.194 = bf16[8,1024,1024]{2,0,1:T(8,128)(2,1)} copy(bf16[8,1024,1024]{1,2,0:T(8,128)(2,1)} %pad_maximum_fusion) | data formatting | bytes 33554432
  946.1 18.8 copy.208
  968.6 68.2 %reduce-scatter.24.cloned.1.call-done = bf16[128,4096]{1,0:T(8,128)(2,1)} async-done(((bf16[1024,4096]{1,0:T(8,128)(2,1)}), bf16[128,4096]{1,0:T(8,128)(2,1)}) %reduce-scatter.24.cloned.1.call-update) | async-done | bytes 1048592
  1040.4 282.5 %reduce-scatter.28.cloned.1.call-done = bf16[128,8192]{1,0:T(8,128)(2,1)} async-done(((bf16[1024,8192]{1,0:T(8,128)(2,1)}), bf16[128,8192]{1,0:T(8,128)(2,1)}) %reduce-scatter.28.cloned.1.call-update) | async-done | bytes 2097168
  1328.7 279.7 %reduce-scatter.22.cloned.1.call-done = bf16[128,8192]{1,0:T(8,128)(2,1)} async-done(((bf16[1024,8192]{1,0:T(8,128)(2,1)}), bf16[128,8192]{1,0:T(8,128)(2,1)}) %reduce-scatter.22.cloned.1.call-update) | async-done | bytes 2097168
  1614.2 5.9 pad_maximum_fusion.4
  1621.5 54.4 %reduce-scatter.16.cloned.1.call-done = bf16[23,128,256]{1,2,0:T(8,128)(2,1)} async-done(((bf16[23,128,1024]{1,2,0:T(8,128)(2,1)}), bf16[23,128,256]{1,2,0:T(8,128)(2,1)}) %reduce-scatter.16.cloned.1.call-update) | async-done | bytes 1507344 | tf_op jit(solution)/shard_map/reduce_scatter | solution.py:348
  1682.8 5.2 all-to-all-start
  1688.1 36.1 %all-to-all-done = bf16[3,8,128,256]{3,2,0,1:T(8,128)(2,1)S(1)} async-done(((bf16[3,8,128,256]{3,2,0,1:T(8,128)(2,1)}), bf16[3,8,128,256]{3,2,0,1:T(8,128)(2,1)S(1)}, u32[]{:S(2)}, u32[]{:S(2)}) %all-to-all-start) | async-done | bytes 1572896 | tf_op jit(solution)/shard_map/all_to_all | solution.py:369
  1724.3 10.5 fusion.191
  1734.8 14.6 convert_bitcast_fusion.3
  1753.2 4.3 copy.160
  1761.9 6.0 fusion.102
  1768.8 5.4 concatenate.41
  1774.3 32.9 %reduce-scatter.18.cloned.1.call-done = bf16[256,3,1024]{0,2,1:T(8,128)(2,1)} async-done(((bf16[1024,3,1024]{0,2,1:T(8,128)(2,1)}), bf16[256,3,1024]{0,2,1:T(8,128)(2,1)}) %reduce-scatter.18.cloned.1.call-update) | async-done | bytes 1572880 | tf_op jit(solution)/shard_map/reduce_scatter | solution.py:377
  1807.2 25.6 %fusion.27 = f32[3,256,1024]{2,1,0:T(8,128)S(1)} fusion(f32[3,1024,1024]{2,1,0:T(8,128)} %param.22, bf16[256,3,1024]{0,2,1:T(8,128)(2,1)} %reduce-scatter.18.cloned.1.call-done, f32[256,3,1024]{0,2,1:T(8,128)} %copy.160, f32[256,3,1024]{0,2,1:T(8,128)} %copy.166), kind=kOutput, calls=%fused_computation.52 | convolution fusion | flops 9672327168 | bytes 23592960 | tf_op jit(solution)/shard_map/rsc,sxc->rsx/dot_general | solution.py:388
  1832.8 24.7 %convert_bitcast_fusion.2 = bf16[1024,3,1024]{0,2,1:T(8,128)(2,1)} fusion(f32[3,256,1024]{2,1,0:T(8,128)S(1)} %fusion.27, f32[3,1024,1024]{2,1,0:T(8,128)} %param.21, s32[]{:T(128)S(6)} %select_n.66), kind=kOutput, calls=%fused_computation.25 | convolution fusion | flops 9666822144 | bytes 12582916 | tf_op jit(solution)/shard_map/sak,ksx->asx/dot_general | solution.py:394
  1862.4 74.3 %all-reduce.15.cloned.1.call-done = f32[34,1024]{1,0:T(8,128)} async-done(((f32[34,1024]{1,0:T(8,128)}), f32[34,1024]{1,0:T(8,128)}) %all-reduce.15.cloned.1.call-update) | async-done | bytes 139280 | tf_op jit(solution)/shard_map/psum | solution.py:340
  1941.8 57.3 %reduce-scatter.20.cloned.1.call-done = bf16[256,3,1024]{0,2,1:T(8,128)(2,1)} async-done(((bf16[1024,3,1024]{0,2,1:T(8,128)(2,1)}), bf16[256,3,1024]{0,2,1:T(8,128)(2,1)}) %reduce-scatter.20.cloned.1.call-update) | async-done | bytes 1572880 | tf_op jit(solution)/shard_map/reduce_scatter | solution.py:393
  1999.1 8.2 fusion.46
  (328 shorter events, 127.6 us)
Async XLA Ops:
  7.2 234.3 %all-gather.5.cloned.1.call-start = ((), (), s32[]{:S(2)}) async-start(), calls=%async_computation.8 | async-start | bytes 18874368 | tf_op jit(solution)/shard_map/all_gather | solution.py:46
  12.1 355.3 %all-gather.7.cloned.1.call-start = ((), (), s32[]{:S(2)}) async-start(), calls=%async_computation.9 | async-start | bytes 9437184 | tf_op jit(solution)/shard_map/all_gather | solution.py:46
  14.4 452.3 %all-gather.9.cloned.1.call-start = ((), (), s32[]{:S(2)}) async-start(), calls=%async_computation.10 | async-start | bytes 7077888 | tf_op jit(solution)/shard_map/all_gather | solution.py:46
  16.7 678.6 %all-gather.11.cloned.1.call-start = ((), (), s32[]{:S(2)}) async-start(), calls=%async_computation.11 | async-start | bytes 18874368 | tf_op jit(solution)/shard_map/all_gather | solution.py:46
  17.3 947.7 %reduce-scatter.26.cloned.1.call-start = ((), (), s32[]{:S(2)}) async-start(), calls=%async_computation.18 | async-start | bytes 7077888
  18.2 229.1 %copy-start.59 = (f32[256]{0:T(256)}, f32[256]{0:T(256)S(1)}, u32[]{:S(2)}) copy-start(f32[256]{0:T(256)S(1)} %broadcast_multiply_fusion.10) | copy-start | bytes 3076
  19.1 228.2 %copy-start.57 = (f32[256]{0:T(256)}, f32[256]{0:T(256)S(1)}, u32[]{:S(2)}) copy-start(f32[256]{0:T(256)S(1)} %fusion.145) | copy-start | bytes 3076
  19.3 228.1 %copy-start.55 = (f32[1,1024]{1,0:T(1,128)}, f32[1,1024]{1,0:T(1,128)S(1)}, u32[]{:S(2)}) copy-start(f32[1,1024]{1,0:T(1,128)S(1)} %get-tuple-element.131) | copy-start | bytes 12292
  19.3 228.1 %copy-start.75 = (f32[1,1024]{1,0:T(1,128)}, f32[1,1024]{1,0:T(1,128)S(1)}, u32[]{:S(2)}) copy-start(f32[1,1024]{1,0:T(1,128)S(1)} %get-tuple-element.130) | copy-start | bytes 12292
  19.3 228.1 %copy-start.73 = (f32[4,1024]{1,0:T(4,128)}, f32[4,1024]{1,0:T(4,128)S(1)}, u32[]{:S(2)}) copy-start(f32[4,1024]{1,0:T(4,128)S(1)} %get-tuple-element.133) | copy-start | bytes 49156
  247.4 8.2 copy-start.87
  255.6 116.5 %copy-start.20 = (f32[1,256,1024]{2,1,0:T(8,128)}, f32[1,256,1024]{2,1,0:T(8,128)S(1)}, u32[]{:S(2)}) copy-start(f32[1,256,1024]{2,1,0:T(8,128)S(1)} %get-tuple-element.138) | copy-start | bytes 3145732
  255.9 116.2 %copy-start.79 = (f32[256]{0:T(256)}, f32[256]{0:T(256)S(1)}, u32[]{:S(2)}) copy-start(f32[256]{0:T(256)S(1)} %multiply_reduce_fusion.14) | copy-start | bytes 3076
  695.3 6.2 copy-start.11
  701.5 11.1 copy-start.86
  701.5 7.8 copy-start.42
  712.6 7.6 copy-start.52
  720.2 7.3 copy-start.25
  768.4 268.4 %reduce-scatter.24.cloned.1.call-start = ((), (), s32[]{:S(2)}) async-start(), calls=%async_computation.17 | async-start | bytes 9437184
  788.9 7.9 copy-start.31
  831.1 491.7 %reduce-scatter.28.cloned.1.call-start = ((), (), s32[]{:S(2)}) async-start(), calls=%async_computation.19 | async-start | bytes 18874368
  891.0 717.4 %reduce-scatter.22.cloned.1.call-start = ((), (), s32[]{:S(2)}) async-start(), calls=%async_computation.16 | async-start | bytes 18874368
  898.3 11.9 copy-start.35
  899.3 8.3 copy-start.3
  899.3 8.3 copy-start.56
  899.3 8.3 copy-start.58
  899.3 8.3 copy-start.60
  899.3 8.3 copy-start.76
  964.9 711.0 %reduce-scatter.16.cloned.1.call-start = ((), (), s32[]{:S(2)}) async-start(), calls=%async_computation.12 | async-start | bytes 7536640 | tf_op jit(solution)/shard_map/reduce_scatter | solution.py:348
  1682.8 41.3 %all-to-all-start = ((bf16[3,8,128,256]{3,2,0,1:T(8,128)(2,1)}), bf16[3,8,128,256]{3,2,0,1:T(8,128)(2,1)S(1)}, u32[]{:S(2)}, u32[]{:S(2)}) async-start(bf16[3,8,128,256]{3,2,0,1:T(8,128)(2,1)} %select_convert_fusion), calls=%async_computation.1 | async-start | bytes 3145728 | tf_op jit(solution)/shard_map/all_to_all | solution.py:369
  1688.0 119.1 %reduce-scatter.18.cloned.1.call-start = ((), (), s32[]{:S(2)}) async-start(), calls=%async_computation.14 | async-start | bytes 7864320 | tf_op jit(solution)/shard_map/reduce_scatter | solution.py:377
  1749.4 187.3 %all-reduce.15.cloned.1.call-start = ((), (), s32[]{:S(2)}) async-start(), calls=%async_computation.13 | async-start | bytes 327680 | tf_op jit(solution)/shard_map/psum | solution.py:340
  1761.8 6.2 copy-start.78
  1761.8 6.9 copy-start.61
  1761.8 6.8 copy-start.62
  1761.8 6.8 copy-start.63
  1761.8 6.8 copy-start.64
  1761.8 6.8 copy-start.65
  1761.9 6.8 copy-start.66
  1761.9 6.8 copy-start.72
  1761.9 6.8 copy-start.81
  1761.9 6.8 copy-start.82
  1761.9 6.8 copy-start.83
  1761.9 6.8 copy-start.84
  1774.2 224.9 %reduce-scatter.20.cloned.1.call-start = ((), (), s32[]{:S(2)}) async-start(), calls=%async_computation.15 | async-start | bytes 7864320 | tf_op jit(solution)/shard_map/reduce_scatter | solution.py:393
  1861.2 75.5 %copy-start.48 = (f32[34,1024]{1,0:T(8,128)S(1)}, f32[34,1024]{1,0:T(8,128)}, u32[]{:S(2)}) copy-start(f32[34,1024]{1,0:T(8,128)} %param.17) | copy-start | bytes 417796
  1861.2 75.5 %copy-start.54 = (f32[34,1024]{1,0:T(8,128)S(1)}, f32[34,1024]{1,0:T(8,128)}, u32[]{:S(2)}) copy-start(f32[34,1024]{1,0:T(8,128)} %param.19) | copy-start | bytes 417796
  1862.4 136.7 %copy-start.4 = (f32[256,3,1024]{0,2,1:T(8,128)S(1)}, f32[256,3,1024]{0,2,1:T(8,128)}, u32[]{:S(2)}) copy-start(f32[256,3,1024]{0,2,1:T(8,128)} %copy.166) | copy-start | bytes 9437188
  (54 other events, 150.2 us)
Sparse Core Ops, SparseCore 0:
  12.2 229.2 all-gather.4
  244.3 123.0 all-gather.6
  369.6 97.0 all-gather.8
  469.3 225.8 all-gather.10
  768.5 115.7 reduce-scatter.25
  887.8 148.9 reduce-scatter.23
  1041.1 281.7 reduce-scatter.27
  1326.6 281.7 reduce-scatter.21
  1620.2 55.6 reduce-scatter.15
  1749.5 57.6 reduce-scatter.17
  1814.2 122.4 all-reduce.14
  1939.3 59.7 reduce-scatter.19
where the time goes:
time: 2040 us; the launch traced here: 2020 us
  waiting for transfers between devices  1520 us (75%)
  local copies, waits for them, and re-layouts  222 us (11%)
  matrix products  194 us (10%)
  other arithmetic  61.2 us (3%)
    all_gather x4, waiting for transfers between devices, fetch_block(): return lax.all_gather(panel_rows, 'fsdp', axis=1, tiled=True)  639 us
    unnamed x16, waiting for transfers between devices  631 us
    unnamed x204, local copies, waits for them, and re-layouts  197 us
    psum x1, waiting for transfers between devices, on_device(): vector_grads = lax.psum(vector_grad, ('dp', 'fsdp'))  74.3 us
    reduce_scatter x1, waiting for transfers between devices, on_device(): lax.psum_scatter(jnp.einsum('sak,ksx->asx', part_rows, back_turn, precisi...  57.3 us
    reduce_scatter x1, waiting for transfers between devices, on_device(): lax.psum_scatter(row_shards.astype(jnp.bfloat16), 'dp', scatter_dimension...  54.4 us
  transfers between devices with their start and end apart: 13, of which 12 were waited for; matrix products, arithmetic and copies ran while one was open for 16% of the time, Pallas kernels for 0%

commit v1 on v0

v1 whole, which is shorter than its diff:
```python
import functools

import jax
import jax.numpy as jnp
from jax import lax
from jax.experimental import pallas as pl
from jax.experimental.pallas import tpu as pltpu
from jax.sharding import Mesh
from jax.sharding import PartitionSpec as P

HEADS = 8
KERNEL = 5
STEPS = 4


norm_eps = 1e-05
adam_eps = 1e-08
beta_one = 0.5
beta_two = 0.5
learn_rate = 0.02
vector_rate = 0.25

bf16 = jnp.bfloat16
f32 = jnp.float32
ANY = pl.ANY
VMEM = pltpu.VMEM
SMEM = pltpu.SMEM
SWAP = [(0, 1), (1, 0)]
TILE = 256
tie = lax.optimization_barrier
VMEM_LIMIT = 56 * 1024 * 1024


def layer_norm(values, gain_row, shift_row):
    centred = values - jnp.mean(values, axis=-1, keepdims=True)
    inverse = lax.rsqrt(jnp.mean(centred * centred, axis=-1, keepdims=True) + norm_eps)
    return centred * inverse * gain_row + shift_row


def norm_backward(residual, gain_row, shift_row, normed_grad):
    ignored, pull_back = jax.vjp(layer_norm, residual, gain_row, shift_row)
    return pull_back(normed_grad)


def adam_step(first_new, second_new):
    return (
        first_new
        / (1.0 - beta_one**STEPS)
        / (jnp.sqrt(second_new / (1.0 - beta_two**STEPS)) + adam_eps)
    )


def token_sum(values):
    return jnp.sum(values, axis=0, dtype=f32)


def dot(left, right):
    return lax.dot_general(left, right, (((1,), (0,)), ((), ())), preferred_element_type=f32)


def dot_nt(left, right):
    return lax.dot_general(left, right, (((1,), (1,)), ((), ())), preferred_element_type=f32)


def dot_tn(left, right):
    return lax.dot_general(left, right, (((0,), (0,)), ((), ())), preferred_element_type=f32)


class Cell:
    def __init__(self, value):
        self.value = value


def bind(*cells):
    for cell, value in zip(cells, tie(tuple(cell.value for cell in cells))):
        cell.value = value


class Wires:
    def __init__(self, outer, owners_count):
        self.outer, self.count = outer, owners_count
        walk = list(range(0, owners_count, 2)) + list(range(owners_count - 1, 0, -2))
        onward = [(walk[i], walk[(i + 1) % owners_count]) for i in range(owners_count)]
        self.routes = {
            "onward": ("f", onward),
            "back": ("f", [(b, a) for a, b in onward]),
            "chip": ("o", [(i, i ^ 1) for i in range(outer)]),
            "core": ("c", SWAP),
        }
        for name, count in (("o", outer), ("f", owners_count)):
            step = 1
            while step < count:
                self.routes[f"{name}{step}"] = (name, [(i, i ^ step) for i in range(count)])
                step *= 2
        index = lax.axis_index("f")
        self.place = jnp.where(index % 2 == 0, index // 2, owners_count - 1 - index // 2)
        self.past = []

    def start(self, *groups, after=()):
        sends = [send for group in groups for send in group]
        came = []
        for value, route, take in sends:
            if after:
                value = tie((value, *[cell.value for cell in after]))[0]
            axis, pairs = self.routes[route]
            came.append(Cell(lax.ppermute(value, axis, pairs)))
            take(came[-1])
        return came

    def slot(self, *groups):
        came = self.start(*groups, after=self.past[-2] if len(self.past) >= 2 else ())
        if came:
            self.past.append(came)
        return came

    def index_at(self, steps):
        spot = (self.place + steps + self.count) % self.count
        return jnp.where(spot < self.count // 2, 2 * spot, 2 * (self.count - 1 - spot) + 1)

    def reach(self, turn):
        half = self.count // 2
        return (half, half - 1) if turn == 0 else (half - 1, half)


class Gather:
    def __init__(self, wires, unit, turn):
        self.wires = wires
        self.left = list(wires.reach(turn))
        self.pieces = [Cell(unit)]
        self.origin = [wires.index_at(0)]
        self.moving = [self.pieces[0], self.pieces[0]]
        self.hops = 0

    def hop(self):
        self.hops += 1
        sends = []
        for way, (route, sign) in enumerate((("onward", -1), ("back", 1))):
            if self.left[way]:
                self.left[way] -= 1
                self.origin.append(self.wires.index_at(sign * self.hops))

                def take(cell, way=way):
                    self.moving[way] = cell
                    self.pieces.append(cell)

                sends.append((self.moving[way].value, route, take))
        return sends

    def spots(self):
        return jnp.stack(self.origin).astype(jnp.int32)


class Reduce:
    def __init__(self, wires, part_of, turn):
        self.wires, self.part_of = wires, part_of
        self.left = list(wires.reach(turn))
        self.moving = [None, None]

    def hop(self):
        sends = []
        for way, (route, sign) in enumerate((("onward", 1), ("back", -1))):
            if self.left[way]:
                value = self.part_of(self.wires.index_at(sign * self.left[way]))
                if self.moving[way] is not None:
                    value = value.astype(f32) + self.moving[way].value.astype(f32)

                def take(cell, way=way):
                    self.moving[way] = cell

                sends.append((value.astype(bf16), route, take))
                self.left[way] -= 1
        return sends

    def total(self):
        while any(self.left):
            self.wires.slot(self.hop())
        own = self.part_of(self.wires.index_at(0)).astype(f32)
        return own + self.moving[0].value.astype(f32) + self.moving[1].value.astype(f32)


class AllSum:
    def __init__(self, wires, value):
        self.wires, self.value = wires, Cell(value)
        self.todo = ["core"] + [name for name in wires.routes if name[1:].isdigit()]
        self.came = None

    def hop(self):
        if not self.todo:
            return []
        self.settle()
        return [(self.value.value, self.todo.pop(0), self.take)]

    def take(self, cell):
        self.came = cell

    def settle(self):
        if self.came is not None:
            self.value = Cell(self.value.value + self.came.value)
            self.came = None

    def total(self):
        while self.todo:
            self.wires.slot(self.hop())
        self.settle()
        return self.value.value


class ChipSum:
    def __init__(self, wires, blocks=None, here=None, there=None):
        self.wires, self.blocks = wires, blocks
        if blocks is not None and wires.outer == 2:
            index = lax.axis_index("o")
            here = lax.dynamic_index_in_dim(blocks, index, 0, keepdims=False)
            there = [lax.dynamic_index_in_dim(blocks, 1 - index, 0, keepdims=False)]
        self.here, self.there, self.came = here, list(there or []), []

    def send(self):
        if not self.there:
            return []
        return [(self.there.pop(0).astype(bf16), "chip", self.came.append)]

    def total(self):
        if self.here is None:
            low = self.blocks.astype(bf16)
            low = lax.psum_scatter(low, "o", scatter_dimension=0, tiled=True)
            return low[0].astype(f32)
        while self.there:
            self.wires.slot(self.send())
        came = [cell.value for cell in self.came]
        came = came[0] if len(came) == 1 else jnp.stack(came)
        return self.here.astype(f32) + came.astype(f32)


def swap_cores(values):
    return lax.ppermute(values, "c", SWAP)


def row_parts(depth, *matrices):
    def part_of(index):
        parts = [lax.dynamic_slice_in_dim(m, index * depth, depth, m.ndim - 2) for m in matrices]
        return jnp.concatenate(parts, axis=-3) if len(parts) > 1 else parts[0]

    return part_of


def gather_blocks(values, name, count):
    if count == 2:
        index = lax.axis_index(name)
        other = lax.ppermute(values, name, SWAP)
        first = jnp.where(index == 0, values, other)
        second = jnp.where(index == 0, other, values)
        return jnp.stack([first, second])
    return lax.all_gather(values, name)


def trade_blocks(values, name, count):
    if count == 2:
        index = lax.axis_index(name)
        there = lax.dynamic_index_in_dim(values, 1 - index, 0, keepdims=False)
        here = lax.dynamic_index_in_dim(values, index, 0, keepdims=False)
        came = lax.ppermute(there, name, SWAP)
        return jnp.stack([jnp.where(index == 0, here, came), jnp.where(index == 0, came, here)])
    return lax.all_to_all(values, name, split_axis=0, concat_axis=0, tiled=True)


def pick_kernel(slots, source, grads, out, sems):
    copies = [
        pltpu.make_async_copy(grads.at[source[i]], out.at[i], sems.at[i]) for i in range(slots)
    ]
    for copy in copies:
        copy.start()
    for copy in copies:
        copy.wait()


def pick(grads, source):
    slots = source.shape[0]
    return pl.pallas_call(
        functools.partial(pick_kernel, slots),
        out_shape=jax.ShapeDtypeStruct((slots,) + grads.shape[1:], grads.dtype),
        in_specs=[pl.BlockSpec(memory_space=SMEM), pl.BlockSpec(memory_space=ANY)],
        out_specs=pl.BlockSpec(memory_space=VMEM),
        scratch_shapes=[pltpu.SemaphoreType.DMA((slots,))],
        name="pick",
    )(source, grads)


def load_share(mine, other, spots, depth, first, weights, sems):
    copies = []
    for i in range(len(mine)):
        row = pl.multiple_of(spots[i] * depth, depth)
        for side, pieces in enumerate((mine, other)):
            copies.append(
                pltpu.make_async_copy(
                    pieces[i].at[first],
                    weights.at[2 * first + side, pl.ds(row, depth)],
                    sems.at[first, side, i],
                )
            )
    return copies


def ffn_forward_kernel(count, meta, normed, bias, *refs):
    mine, other = refs[:count], refs[count : 2 * count]
    hidden, active, branch, away, weights, sems = refs[2 * count :]
    depth, width = mine[0].shape[1:]
    tokens = branch.shape[0]
    ins = load_share(mine, other, meta, depth, 0, weights, sems)
    outs = load_share(mine, other, meta, depth, 1, weights, sems)
    start_all(ins + outs)
    wait_all(ins)
    for p in range(2):

        @column_loop(width)
        def columns(cols):
            value = dot(normed[...], weights[p, :, cols]) + bias[p, :, cols]
            hidden[p, :, cols] = value
            active[p, :, cols] = (value * jax.nn.sigmoid(value)).astype(bf16)

    wait_all(outs)

    @column_loop(width)
    def out_columns(cols):
        total = dot(active[0], weights[2, :, cols]) + dot(active[1], weights[3, :, cols])
        branch[:, cols] = total[:tokens]
        away[:, cols] = total[tokens:].astype(bf16)


def ffn_forward_call(normed, bias, mine, other, meta):
    tokens, width = normed.shape
    count = len(mine)
    return pl.pallas_call(
        functools.partial(ffn_forward_kernel, count),
        out_shape=[
            jax.ShapeDtypeStruct((2, tokens, width), f32),
            jax.ShapeDtypeStruct((2, tokens, width), bf16),
            jax.ShapeDtypeStruct((tokens // 2, width), f32),
            jax.ShapeDtypeStruct((tokens // 2, width), bf16),
        ],
        in_specs=[
            pl.BlockSpec(memory_space=SMEM),
            pl.BlockSpec(memory_space=VMEM),
            pl.BlockSpec(memory_space=VMEM),
        ]
        + [pl.BlockSpec(memory_space=ANY)] * (2 * count),
        out_specs=[pl.BlockSpec(memory_space=VMEM)] * 4,
        scratch_shapes=[
            VMEM((4, width, width), bf16),
            pltpu.SemaphoreType.DMA((2, 2, count)),
        ],
        compiler_params=pltpu.CompilerParams(vmem_limit_bytes=VMEM_LIMIT),
        cost_estimate=pl.CostEstimate(
            flops=8 * tokens * width * width,
            bytes_accessed=8 * width * width + tokens * width * 18,
            transcendentals=2 * tokens * width,
        ),
        name="ffn_forward",
    )(meta, normed, bias, *mine, *other)


def ffn_out_backward_kernel(count, bias, blocks, meta, hidden, active, grad, had, *refs):
    mine, other = refs[:count], refs[count : 2 * count]
    low, sums, *matrices, weights, sems = refs[2 * count :]
    depth, width = mine[0].shape[1:]
    outer, ways = blocks
    parity, core = meta[count], meta[count + 1]
    store = share_store(ways, meta[count + 2], matrices)
    sums[...] = had[...]
    copies = load_share(mine, other, meta, depth, 1, weights, sems)
    start_all(copies)
    for p in range(2):
        put_blocks(store, p ^ parity, active.at[p], grad, outer)
    wait_all(copies)
    for p in range(2):
        row = bias + 2 * core + (p ^ parity)

        @column_loop(width)
        def rows(cols):
            value = hidden[p, :, cols]
            share = jax.nn.sigmoid(value)
            slope = share * (1.0 + value * (1.0 - share))
            part = (dot_nt(grad[...], weights[2 + p, cols, :]) * slope).astype(bf16)
            low[p, :, cols] = part
            sums[pl.ds(row, 1), cols] = jnp.sum(part.astype(f32), axis=0, keepdims=True)


def ffn_in_backward_kernel(count, bias, blocks, meta, normed, low, *refs):
    mine, other = refs[:count], refs[count : 2 * count]
    normed_grad, away, *matrices, weights, sems = refs[2 * count :]
    tokens = away.shape[0]
    depth, width = mine[0].shape[1:]
    outer, ways = blocks
    parity = meta[count]
    store = share_store(ways, meta[count + 2], matrices)
    copies = load_share(mine, other, meta, depth, 0, weights, sems)
    start_all(copies)
    for p in range(2):
        put_blocks(store, p ^ parity, normed, low.at[p], outer)
    wait_all(copies)

    @column_loop(width)
    def back(cols):
        total = dot_nt(low[0], weights[0, cols, :]) + dot_nt(low[1], weights[1, cols, :])
        normed_grad[:, cols] = total[:tokens]
        away[:, cols] = total[tokens:].astype(bf16)


def share_store(ways, chip, matrices):
    if ways:
        return store_by_chip(chip, matrices[0], matrices[1:])
    return store_all(matrices[0])


def ffn_backward_call(kernel, name, bias, outer, ways, meta, arrays, mine, other, outs):
    width = mine[0].shape[-1]
    tokens = arrays[0].shape[-2]
    count = len(mine)
    quarter = width // (2 * outer)
    if ways:
        part = jax.ShapeDtypeStruct((2, width, quarter), bf16)
        blocks = [jax.ShapeDtypeStruct((2, 2, width, quarter), bf16), part, part]
    else:
        blocks = [jax.ShapeDtypeStruct((outer, 2, 2, width, quarter), bf16)]
    return pl.pallas_call(
        functools.partial(kernel, count, bias, (outer, ways)),
        out_shape=[*outs, *blocks],
        in_specs=[pl.BlockSpec(memory_space=SMEM)]
        + [pl.BlockSpec(memory_space=VMEM)] * len(arrays)
        + [pl.BlockSpec(memory_space=ANY)] * (2 * count),
        out_specs=[pl.BlockSpec(memory_space=VMEM)] * (len(outs) + len(blocks)),
        scratch_shapes=[
            VMEM((4, width, width), bf16),
            pltpu.SemaphoreType.DMA((2, 2, count)),
        ],
        compiler_params=pltpu.CompilerParams(vmem_limit_bytes=VMEM_LIMIT),
        cost_estimate=pl.CostEstimate(
            flops=8 * tokens * width * width,
            bytes_accessed=8 * width * width + tokens * width * 16,
            transcendentals=tokens * width,
        ),
        name=name,
    )(meta, *arrays, *mine, *other)


def norm_parts(values):
    centred = values - jnp.mean(values, axis=-1, keepdims=True)
    inverse = lax.rsqrt(jnp.mean(centred * centred, axis=-1, keepdims=True) + norm_eps)
    return centred * inverse, inverse


def norm_pull(normed, inverse, gain_row, grad):
    scaled = grad * gain_row
    along = jnp.mean(scaled * normed, axis=-1, keepdims=True)
    return inverse * (scaled - jnp.mean(scaled, axis=-1, keepdims=True) - normed * along)


def column_sum(values):
    return jnp.sum(values, axis=0, keepdims=True)


def halves_to_panels(first, last, own, other, spots, core, weights, sems):
    depth, half = own[0].shape[1:]
    copies = []
    for i in range(len(own)):
        row = pl.multiple_of(spots[i] * depth, depth)
        for side, pieces in ((core, own), (1 - core, other)):
            col = pl.multiple_of(side * half, half)
            copies.append(
                pltpu.make_async_copy(
                    pieces[i].at[pl.ds(first, last - first)],
                    weights.at[pl.ds(0, last - first), pl.ds(row, depth), pl.ds(col, half)],
                    sems.at[len(copies)],
                )
            )
    return copies


def start_all(copies):
    for copy in copies:
        copy.start()


def wait_all(copies):
    for copy in copies:
        copy.wait()


def column_loop(width):
    def run(body):
        @pl.loop(0, width // TILE)
        def step(j):
            body(pl.ds(pl.multiple_of(j * TILE, TILE), TILE))

    return run


def put_blocks(store, panel, left, right, outer):
    quarter = right.shape[-1] // (2 * outer)

    @column_loop(left.shape[1])
    def rows(part):
        value = dot_tn(left[:, part], right[...]).astype(bf16)
        for o in range(outer):
            for c in range(2):
                at = (2 * o + c) * quarter
                store(o, c, panel, part, value[:, at : at + quarter])


def store_all(blocks):
    def store(o, c, panel, part, value):
        blocks[o, c, panel, part, :] = value

    return store


def store_by_core(core, here, there):
    def store(o, c, panel, part, value):
        @pl.when(c == core)
        def kept():
            here[o, panel, part, :] = value

        @pl.when(c != core)
        def sent():
            there[o, panel, part, :] = value

    return store


def store_by_chip(chip, here, there):
    def store(o, c, panel, part, value):
        @pl.when(o == chip)
        def kept():
            here[c, panel, part, :] = value

        @pl.when(o != chip)
        def sent():
            there[c][panel, part, :] = value

    return store


def attend(queries, keys, head, size, length, score_scale):
    cols = slice(head * size, (head + 1) * size)
    scores = dot_nt(queries[:, cols], keys[:, cols]) * score_scale
    spot = lax.broadcasted_iota(jnp.int32, scores.shape, 1)
    scores = jnp.where(spot < length, scores, -1000000000.0)
    peak = jnp.max(scores, axis=-1, keepdims=True)
    raised = jnp.exp(scores - peak)
    return raised * (1.0 / jnp.sum(raised, axis=-1, keepdims=True)), cols


def attention_forward_kernel(count, meta, stream, rows, *refs):
    own, other = refs[:count], refs[count : 2 * count]
    out, normed, queries, keys, values, mixed, weights, sems = refs[2 * count :]
    core, length = meta[count], meta[count + 1]
    width = stream.shape[1]
    size = width // HEADS
    copies = halves_to_panels(0, 4, own, other, meta, core, weights, sems)
    start_all(copies)
    inside, ignored = norm_parts(stream[...])
    normed[...] = (inside * rows[2:3] + rows[3:4]).astype(bf16)
    wait_all(copies)

    @column_loop(width)
    def project(cols):
        low = normed[...]
        queries[:, cols] = (dot(low, weights[0, :, cols]) + rows[22:23, cols]).astype(bf16)
        keys[:, cols] = dot(low, weights[1, :, cols]).astype(bf16)
        values[:, cols] = (dot(low, weights[2, :, cols]) + rows[23:24, cols]).astype(bf16)

    for head in range(HEADS):
        soft, cols = attend(queries, keys, head, size, length, size ** (-0.5))
        mixed[:, cols] = dot(soft.astype(bf16), values[:, cols]).astype(bf16)

    @column_loop(width)
    def branch(cols):
        out[:, cols] = (
            stream[:, cols] + dot(mixed[...], weights[3, :, cols]) + rows[24:25, cols]
        )


def attention_heads_backward_kernel(
    count, meta, grad, queries, keys, values, mixed, had, *refs
):
    own, other = refs[:count], refs[count : 2 * count]
    lows, here, there, sums, weights, branch_grad, low_mixed, sems = refs[2 * count :]
    store = store_by_core(meta[count], here, there)
    sums[...] = had[...]
    core, length = meta[count], meta[count + 1]
    width = grad.shape[1]
    size = width // HEADS
    score_scale = size ** (-0.5)
    copies = halves_to_panels(3, 4, own, other, meta, core, weights, sems)
    start_all(copies)
    branch_grad[...] = grad[...].astype(bf16)
    sums[24:25] = column_sum(branch_grad[...].astype(f32))
    put_blocks(store, 0, mixed, branch_grad, here.shape[0])
    wait_all(copies)

    @column_loop(width)
    def through(cols):
        low_mixed[:, cols] = dot_nt(branch_grad[...], weights[0, cols, :]).astype(bf16)

    for head in range(HEADS):
        soft, cols = attend(queries, keys, head, size, length, score_scale)
        low = low_mixed[:, cols]
        soft_grad = dot_nt(low, values[:, cols])
        lows[2, :, cols] = dot_tn(soft.astype(bf16), low).astype(bf16)
        along = jnp.sum(soft_grad * soft, axis=-1, keepdims=True)
        score_grad = (soft * (soft_grad - along)).astype(bf16)
        lows[0, :, cols] = (dot(score_grad, keys[:, cols]) * score_scale).astype(bf16)
        lows[1, :, cols] = (dot_tn(score_grad, queries[:, cols]) * score_scale).astype(bf16)

    sums[22:23] = column_sum(lows[0].astype(f32))
    sums[23:24] = column_sum(lows[2].astype(f32))


def attention_in_backward_kernel(count, meta, grad, stream, normed, lows, rows, had, *refs):
    own, other = refs[:count], refs[count : 2 * count]
    out, here, there, sums, half_low, weights, normed_grad, sems = refs[2 * count :]
    core = meta[count]
    store = store_by_core(core, here, there)
    sums[...] = had[...]
    width = stream.shape[1]
    copies = halves_to_panels(0, 3, own, other, meta, core, weights, sems)
    start_all(copies)
    for i in range(3):
        put_blocks(store, i, normed, lows.at[i], here.shape[0])
    wait_all(copies)

    @column_loop(width)
    def back(cols):
        total = dot_nt(lows[0], weights[0, cols, :])
        total = total + dot_nt(lows[1], weights[1, cols, :])
        normed_grad[:, cols] = total + dot_nt(lows[2], weights[2, cols, :])

    inside, inverse = norm_parts(stream[...])
    pulled = normed_grad[...]
    sums[2:3] = column_sum(pulled * inside)
    sums[3:4] = column_sum(pulled)
    flow = grad[...] + norm_pull(inside, inverse, rows[2:3], pulled)
    out[...] = flow
    half_low[...] = (0.5 * flow).astype(bf16)
    sums[16:17] = column_sum(half_low[...].astype(f32))


def moved(values, steps):
    if steps == 0:
        return values
    tall = values.shape[0]
    spot = lax.broadcasted_iota(jnp.int32, values.shape, 0) + steps
    return jnp.where((spot >= 0) & (spot < tall), pltpu.roll(values, (-steps) % tall, 0), 0.0)


def gated_depth(wide, rows, length):
    value, gate = wide[0], wide[1]
    open_gate = jax.nn.sigmoid(gate)
    inside = lax.broadcasted_iota(jnp.int32, value.shape, 0) < length
    gated = jnp.where(inside, value * open_gate, 0.0)
    depth = rows[27:28] + rows[28:29] * moved(gated, -(KERNEL // 2))
    for tap in range(1, KERNEL):
        depth = depth + rows[28 + tap : 29 + tap] * moved(gated, tap - KERNEL // 2)
    return value, open_gate, inside, gated, depth


def conv_forward_kernel(count, meta, stream, rows, *refs):
    own, other = refs[:count], refs[count : 2 * count]
    out, normed, wide, active, weights, sems = refs[2 * count :]
    core, length = meta[count], meta[count + 1]
    width = stream.shape[1]
    copies = halves_to_panels(4, 7, own, other, meta, core, weights, sems)
    start_all(copies)
    inside, ignored = norm_parts(stream[...])
    normed[...] = (inside * rows[4:5] + rows[5:6]).astype(bf16)
    wait_all(copies)

    @column_loop(width)
    def project(cols):
        for i in range(2):
            wide[i, :, cols] = dot(normed[...], weights[i, :, cols]) + rows[25 + i : 26 + i, cols]

    depth = gated_depth(wide, rows, length)[-1]
    inside, ignored = norm_parts(depth)
    shifted = inside * rows[6:7] + rows[7:8]
    active[...] = (shifted * jax.nn.sigmoid(shifted)).astype(bf16)

    @column_loop(width)
    def branch(cols):
        out[:, cols] = (
            stream[:, cols] + dot(active[...], weights[2, :, cols]) + rows[33:34, cols]
        )


def conv_out_backward_kernel(count, meta, grad, wide, active, rows, had, *refs):
    own, other = refs[:count], refs[count : 2 * count]
    lows, here, there, sums, weights, full, sems = refs[2 * count :]
    core, length = meta[count], meta[count + 1]
    store = store_by_core(core, here, there)
    sums[...] = had[...]
    width = grad.shape[1]
    copies = halves_to_panels(6, 7, own, other, meta, core, weights, sems)
    start_all(copies)
    branch_grad = grad[...].astype(bf16)
    lows[0] = branch_grad
    sums[33:34] = column_sum(branch_grad.astype(f32))
    put_blocks(store, 0, active, lows.at[0], here.shape[0])
    wait_all(copies)

    @column_loop(width)
    def through(cols):
        full[:, cols] = dot_nt(lows[0], weights[0, cols, :])

    value, open_gate, valid, gated, depth = gated_depth(wide, rows, length)
    inside, inverse = norm_parts(depth)
    shifted = inside * rows[6:7] + rows[7:8]
    share = jax.nn.sigmoid(shifted)
    outer_grad = full[...] * share * (1.0 + shifted * (1.0 - share))
    sums[6:7] = column_sum(outer_grad * inside)
    sums[7:8] = column_sum(outer_grad)
    depth_grad = norm_pull(inside, inverse, rows[6:7], outer_grad)
    sums[27:28] = column_sum(depth_grad)
    gated_grad = jnp.zeros_like(depth_grad)
    for tap in range(KERNEL):
        off = tap - KERNEL // 2
        sums[28 + tap : 29 + tap] = column_sum(depth_grad * moved(gated, off))
        gated_grad = gated_grad + rows[28 + tap : 29 + tap] * moved(depth_grad, -off)
    gated_grad = jnp.where(valid, gated_grad, 0.0)
    lows[0] = (gated_grad * open_gate).astype(bf16)
    lows[1] = (gated_grad * value * open_gate * (1.0 - open_gate)).astype(bf16)
    for i in range(2):
        sums[25 + i : 26 + i] = column_sum(lows[i].astype(f32))


def conv_in_backward_kernel(count, meta, grad, stream, normed, lows, rows, had, *refs):
    own, other = refs[:count], refs[count : 2 * count]
    out, here, there, sums, weights, full, sems = refs[2 * count :]
    core = meta[count]
    store = store_by_core(core, here, there)
    sums[...] = had[...]
    width = stream.shape[1]
    copies = halves_to_panels(4, 6, own, other, meta, core, weights, sems)
    start_all(copies)
    for i in range(2):
        put_blocks(store, i, normed, lows.at[i], here.shape[0])
    wait_all(copies)

    @column_loop(width)
    def back(cols):
        full[:, cols] = dot_nt(lows[0], weights[0, cols, :]) + dot_nt(lows[1], weights[1, cols, :])

    inside, inverse = norm_parts(stream[...])
    pulled = full[...]
    sums[4:5] = column_sum(pulled * inside)
    sums[5:6] = column_sum(pulled)
    out[...] = grad[...] + norm_pull(inside, inverse, rows[4:5], pulled)


def pull_kernel(gain, grad, stream, mine, came, rows, had, out, sums):
    sums[...] = had[...]
    inside, inverse = norm_parts(stream[...])
    pulled = mine[...] + came[...].astype(f32)
    sums[gain : gain + 1] = column_sum(pulled * inside)
    sums[gain + 1 : gain + 2] = column_sum(pulled)
    flow = grad[...] + norm_pull(inside, inverse, rows[gain : gain + 1], pulled)
    out[...] = flow.astype(out.dtype)


def pull_call(gain, grad, stream, mine, came, rows, had, dtype):
    return pl.pallas_call(
        functools.partial(pull_kernel, gain),
        out_shape=[
            jax.ShapeDtypeStruct(grad.shape, dtype),
            jax.ShapeDtypeStruct(had.shape, f32),
        ],
        cost_estimate=pl.CostEstimate(
            flops=20 * grad.size, bytes_accessed=16 * grad.size, transcendentals=0
        ),
        compiler_params=pltpu.CompilerParams(vmem_limit_bytes=VMEM_LIMIT),
        name="norm_pull",
    )(grad, stream, mine, came, rows, had)


def turn_kernel(meta, stream, mine, came, cotangent, rows, layer_out, out, half_low, sums):
    last = stream[...] + 0.5 * (mine[...] + came[...].astype(f32) + rows[21:22])
    inside, inverse = norm_parts(last)
    layer_out[...] = (inside * rows[10:11] + rows[11:12]).astype(bf16)
    spot = lax.broadcasted_iota(jnp.int32, last.shape, 0)
    grad = jnp.where(spot < meta[0], cotangent[...].astype(f32), 0.0)
    sums[...] = jnp.zeros_like(sums)
    sums[10:11] = column_sum(grad * inside)
    sums[11:12] = column_sum(grad)
    flow = norm_pull(inside, inverse, rows[10:11], grad)
    out[...] = flow
    half_low[...] = (0.5 * flow).astype(bf16)
    sums[21:22] = column_sum(half_low[...].astype(f32))


def turn_call(length, stream, mine, came, cotangent, rows):
    return pl.pallas_call(
        turn_kernel,
        in_specs=[pl.BlockSpec(memory_space=SMEM)] + [pl.BlockSpec(memory_space=VMEM)] * 5,
        out_shape=[
            jax.ShapeDtypeStruct(stream.shape, bf16),
            jax.ShapeDtypeStruct(stream.shape, f32),
            jax.ShapeDtypeStruct(stream.shape, bf16),
            jax.ShapeDtypeStruct(rows.shape, f32),
        ],
        cost_estimate=pl.CostEstimate(
            flops=30 * stream.size, bytes_accessed=20 * stream.size, transcendentals=0
        ),
        compiler_params=pltpu.CompilerParams(vmem_limit_bytes=VMEM_LIMIT),
        name="turn",
    )(length, stream, mine, came, cotangent, rows)


def panel_call(kernel, name, panels, meta, blocks, own, other, outs, scratch, flops):
    count = len(own)
    width = blocks[0].shape[1]
    return pl.pallas_call(
        functools.partial(kernel, count),
        out_shape=outs,
        in_specs=[pl.BlockSpec(memory_space=SMEM)]
        + [pl.BlockSpec(memory_space=VMEM)] * len(blocks)
        + [pl.BlockSpec(memory_space=ANY)] * (2 * count),
        out_specs=[pl.BlockSpec(memory_space=VMEM)] * len(outs),
        scratch_shapes=[VMEM((panels, width, width), bf16)]
        + scratch
        + [pltpu.SemaphoreType.DMA((2 * count,))],
        compiler_params=pltpu.CompilerParams(vmem_limit_bytes=VMEM_LIMIT),
        cost_estimate=pl.CostEstimate(
            flops=flops,
            bytes_accessed=panels * width * width * 2 + 8 * blocks[0].size * 4,
            transcendentals=2 * blocks[0].size,
        ),
        name=name,
    )(meta, *blocks, *own, *other)


def both_cores(values):
    return jnp.concatenate([values, swap_cores(values)], axis=0)


def on_device(
    outer,
    owners_count,
    frames,
    lengths,
    cotangent,
    panels,
    vectors,
    vector_first,
    vector_second,
    owners,
    basis_left,
    basis_right,
    panel_first,
    panel_second,
    panel_master,
):
    seq_count, seq_len, width = frames.shape
    tokens = seq_count * seq_len
    depth = panels.shape[1]
    half = width // 2
    quarter = width // (2 * outer)
    core = lax.axis_index("c")
    parity = lax.axis_index("o") % 2
    wires = Wires(outer, owners_count)
    shape = jax.ShapeDtypeStruct

    def chip_share(first, side):
        panel = 2 * core + side
        ins = lax.dynamic_slice_in_dim(panels, first + panel, 1, 0)
        outs = lax.dynamic_slice_in_dim(panels, first + 4 + panel, 1, 0)
        return jnp.concatenate([ins, outs], axis=0)

    first = Gather(wires, chip_share(0, parity), 0)
    middle = Gather(wires, lax.dynamic_slice_in_dim(panels[8:15], core * half, half, 2), 1)
    second = Gather(wires, chip_share(15, parity), 0)
    first_other = [Cell(chip_share(0, 1 - parity))]
    second_other = [Cell(chip_share(15, 1 - parity))]
    middle_other = []

    class Passing:
        def __init__(self, gather, route, store, start):
            self.gather, self.route, self.store, self.next = gather, route, store, start

        def more(self, most=1):
            sends = []
            while most and self.next < len(self.gather.pieces):
                sends.append((self.gather.pieces[self.next].value, self.route, self.store.append))
                self.next += 1
                most -= 1
            return sends

    to_chip = Passing(first, "chip", first_other, 1)
    to_chip_too = Passing(second, "chip", second_other, 1)
    to_core = Passing(middle, "core", middle_other, 0)
    slot = wires.slot

    def values(cells):
        return [cell.value for cell in cells]

    def core_rows(first):
        rows = lax.dynamic_slice_in_dim(vectors, first + 2 * core, 2, 0)
        rows = jnp.where(parity == 0, rows, rows[::-1])
        return rows[:, None, :]

    def meta_of(gather, *more):
        return jnp.concatenate([gather.spots(), jnp.stack(more).astype(jnp.int32)])

    low_stream = shape((tokens, width), bf16)
    stream = shape((tokens, width), f32)

    left = Cell(basis_left.astype(bf16))
    right = Cell(basis_right.astype(bf16))
    start = Cell(frames.reshape(tokens, width).astype(f32))
    normed = Cell(
        both_cores(layer_norm(start.value, vectors[0], vectors[1]).astype(bf16))
    )
    bias_first, bias_second = Cell(core_rows(12)), Cell(core_rows(17))
    ready = [start, normed, bias_first, bias_second, *first_other, *second_other]
    came = slot(first.hop(), to_core.more())
    bind(*ready, *came)
    slot(first.hop(), to_chip.more())
    slot(middle.hop(), to_chip.more(2))
    slot(first.hop(), to_chip.more(), to_core.more(2))
    slot(second.hop(), to_chip.more())
    slot(first.hop(), to_chip.more())
    came = slot(middle.hop(), to_chip.more(), to_chip_too.more())
    bind(left, right, *wires.past[-2])
    while any(first.left):
        came = slot(first.hop())
    while to_chip.next < len(first.pieces):
        came = slot(to_chip.more(2))
    came = slot(second.hop(), to_chip_too.more(), to_core.more(2))
    bind(normed, *wires.past[-2])
    slot(middle.hop(), to_chip_too.more(2))
    hidden, active, mine, away = ffn_forward_call(
        normed.value, bias_first.value, values(first.pieces), values(first_other),
        meta_of(first, parity),
    )
    after_first = Cell(
        start.value + 0.5 * (mine + swap_cores(away).astype(f32) + vectors[16])
    )
    kept_first = (normed.value, hidden, active)
    bind(after_first, *wires.past[-1], *wires.past[-2])
    slot(second.hop(), to_core.more(2))
    slot(middle.hop(), second.hop(), to_chip_too.more(2))
    while any(middle.left) or any(second.left):
        slot(middle.hop(), second.hop(), to_chip_too.more(2), to_core.more(2))
    came = wires.start(to_core.more(2), to_chip_too.more(), after=wires.past[-1])
    while to_core.next < len(middle.pieces):
        came += slot(to_core.more(2))
    middle_meta = meta_of(middle, core, lengths[0])
    bind(after_first, *wires.past[-1])
    after_attn, attn_normed, queries, keys, values_, mixed = panel_call(
        attention_forward_kernel,
        "attention_forward",
        4,
        middle_meta,
        [after_first.value, vectors],
        values(middle.pieces),
        values(middle_other),
        [stream] + [low_stream] * 5,
        [],
        8 * tokens * width * width,
    )
    after_attn = Cell(after_attn)
    bind(after_attn, *came)
    came = []
    while to_chip_too.next < len(second.pieces):
        came += wires.start(to_chip_too.more(2), after=[after_attn])
    after_conv, conv_normed, wide, conv_active = panel_call(
        conv_forward_kernel,
        "conv_forward",
        3,
        middle_meta,
        [after_attn.value, vectors],
        values(middle.pieces),
        values(middle_other),
        [stream, low_stream, shape((2, tokens, width), f32), low_stream],
        [],
        6 * tokens * width * width,
    )
    normed = both_cores(layer_norm(after_conv, vectors[8], vectors[9]).astype(bf16))
    hidden, active, mine, away = ffn_forward_call(
        normed, bias_second.value, values(second.pieces), values(second_other),
        meta_of(second, parity),
    )
    kept_second = (normed, hidden, active)
    layer_out, grad_flow, half_low, sums = turn_call(
        lengths, after_conv, mine, swap_cores(away), cotangent.reshape(tokens, width), vectors
    )

    def ring_of(turn, *matrices):
        return Reduce(wires, row_parts(depth, *matrices), turn)

    class Share:
        def __init__(self, here, there):
            self.here, self.there = here, there

        def hop(self):
            return [(self.there, "core", self.take)]

        def take(self, cell):
            self.came = cell

        def total(self):
            return (self.here.astype(f32) + self.came.value.astype(f32)).astype(bf16)

    def trade_cores(block):
        there = lax.dynamic_index_in_dim(block, 1 - core, 0, keepdims=False)
        here = lax.dynamic_index_in_dim(block, core, 0, keepdims=False)
        came = swap_cores(there.astype(bf16)).astype(f32)
        return jnp.where(
            core == 0, jnp.concatenate([here, came]), jnp.concatenate([came, here])
        )

    chip = lax.axis_index("o")
    pairs = outer == 2

    def ffn_backward_out(half_low, gather, other, kept, bias, sums, ways):
        normed, hidden, active = kept
        return ffn_backward_call(
            ffn_out_backward_kernel,
            "ffn_out_backward",
            bias,
            outer,
            ways,
            meta_of(gather, parity, core, chip),
            [hidden, active, both_cores(half_low), sums],
            values(gather.pieces),
            values(other),
            [shape((2, 2 * tokens, width), bf16), shape(vectors.shape, f32)],
        )

    def ffn_backward_in(low, gather, other, kept, ways):
        return ffn_backward_call(
            ffn_in_backward_kernel,
            "ffn_in_backward",
            0,
            outer,
            ways,
            meta_of(gather, parity, core, chip),
            [kept[0], low],
            values(gather.pieces),
            values(other),
            [shape((tokens, width), f32), shape((tokens, width), bf16)],
        )

    def middle_call(kernel, name, used, arrays, outs, scratch, flops):
        block_shape = shape((outer, used, width, quarter), bf16)
        return panel_call(
            kernel,
            name,
            used,
            middle_meta,
            arrays,
            values(middle.pieces),
            values(middle_other),
            [outs[0], block_shape, block_shape, shape(vectors.shape, f32), *outs[1:]],
            scratch,
            flops * tokens * width * width,
        )

    class Part:
        def __init__(self, matrices, turn):
            self.turn = turn
            self.ring = None
            if len(matrices) == 3:
                self.chips = ChipSum(wires, here=matrices[0], there=matrices[1:])
            else:
                self.chips = None
                self.ring = ring_of(turn, *matrices)

        def send(self):
            return self.chips.send()

        def hop(self):
            if self.ring is None:
                self.ring = ring_of(self.turn, self.chips.total().astype(bf16))
            return self.ring.hop()

        def finish(self):
            if self.chips is not None:
                return []
            self.chips = ChipSum(wires, blocks=self.ring.total())
            self.late = True
            return self.chips.send()

        def total(self):
            if self.chips is None:
                slot(self.finish())
            return self.chips.total() if hasattr(self, "late") else self.ring.total()

    begin = wires.start
    low, sums, *matrices = ffn_backward_out(
        half_low, second, second_other, kept_second, 17, sums, False
    )
    second_out = Part(matrices, 0)
    low = Cell(low)
    came = begin(second_out.hop(), after=[low])
    mine, away, *matrices = ffn_backward_in(
        low.value, second, second_other, kept_second, pairs
    )
    mine = Cell(mine)
    bind(mine, *came)
    second_in = Part(matrices, 1)
    came = begin(second_out.hop(), second_in.send() if pairs else [], after=[mine])
    grad_flow, sums = pull_call(
        8, grad_flow, after_conv, mine.value, swap_cores(away), vectors, sums, f32
    )
    lows, here, there, sums = middle_call(
        conv_out_backward_kernel,
        "conv_out_backward",
        1,
        [grad_flow, wide, conv_active, vectors, sums],
        [shape((2, tokens, width), bf16)],
        [VMEM((tokens, width), f32)],
        4,
    )
    lows = Cell(lows)
    bind(lows, *came)
    conv_out = Share(here, there)
    came = begin(
        second_out.hop(), second_in.send() if pairs else [], conv_out.hop(), after=[lows]
    )
    flow, here, there, sums = middle_call(
        conv_in_backward_kernel,
        "conv_in_backward",
        2,
        [grad_flow, after_attn.value, conv_normed, lows.value, vectors, sums],
        [stream],
        [VMEM((tokens, width), f32)],
        8,
    )
    flow = Cell(flow)
    conv_in = Share(here, there)
    lows, here, there, sums = middle_call(
        attention_heads_backward_kernel,
        "attention_heads_backward",
        1,
        [flow.value, queries, keys, values_, mixed, sums],
        [shape((3, tokens, width), bf16)],
        [VMEM((tokens, width), bf16), VMEM((tokens, width), bf16)],
        6,
    )
    lows = Cell(lows)
    bind(lows, *came)
    attn_out = Share(here, there)
    came = begin(
        second_out.hop(), second_in.hop(), conv_in.hop(), attn_out.hop(), after=[lows]
    )
    flow.value, here, there, sums, half_low = middle_call(
        attention_in_backward_kernel,
        "attention_in_backward",
        3,
        [flow.value, after_first.value, attn_normed, lows.value, vectors, sums],
        [stream, low_stream],
        [VMEM((tokens, width), f32)],
        12,
    )
    half_low = Cell(half_low)
    bind(half_low, *came)
    attn_in = Share(here, there)
    conv_part = ring_of(0, conv_in.total(), conv_out.total())
    came = begin(
        conv_part.hop(), second_in.hop(), attn_in.hop(), second_out.finish(), after=[half_low]
    )
    low, sums, *matrices = ffn_backward_out(
        half_low.value, first, first_other, kept_first, 12, sums, pairs
    )
    first_out = Part(matrices, 1)
    low = Cell(low)
    bind(low, *came)
    attn_in_total, attn_out_total = attn_in.total(), attn_out.total()
    if pairs:
        attn_chips = ChipSum(
            wires, blocks=jnp.concatenate([attn_in_total, attn_out_total], axis=1)
        )
        attn_sends = attn_chips.send()
    else:
        attn_part, attn_sends = ring_of(1, attn_in_total, attn_out_total), []
    came = begin(conv_part.hop(), second_in.hop(), attn_sends, after=[low])
    mine, away, *matrices = ffn_backward_in(low.value, first, first_other, kept_first, False)
    first_in = Part(matrices, 0)
    mine = Cell(mine)
    bind(mine, *came)
    wires.past = [came]
    slot(first_in.hop(), conv_part.hop(), first_out.send() if pairs else [])
    frames_grad, sums = pull_call(
        0, flow.value, start.value, mine.value, swap_cores(away), vectors, sums, bf16
    )
    frames_grad, sums = Cell(frames_grad), Cell(sums)
    bind(sums, frames_grad, *came)
    vector_sum = AllSum(wires, sums.value)
    if pairs:
        attn_part = ring_of(1, attn_chips.total().astype(bf16))
    slot(first_in.hop(), attn_part.hop(), first_out.send() if pairs else [], vector_sum.hop())
    slot(first_in.hop(), conv_part.hop(), second_in.hop(), vector_sum.hop())
    slot(first_in.hop(), attn_part.hop(), vector_sum.hop())
    conv_chips = ChipSum(wires, blocks=conv_part.total())
    slot(attn_part.hop(), first_out.hop(), conv_chips.send(), vector_sum.hop())
    slot(attn_part.hop(), first_out.hop(), first_in.finish(), vector_sum.hop())
    early = [trade_cores(second_in.total()), trade_cores(second_out.total()), conv_chips.total()]
    early = [Cell(part) for part in early]
    slot(first_out.hop())
    slot(first_out.hop())
    late = [trade_cores(first_in.total()), attn_part.total()]
    if not pairs:
        late[1] = ChipSum(wires, blocks=late[1]).total()
    late = [Cell(part) for part in late]
    vector_grads = Cell(vector_sum.total())
    bind(vector_grads, *early, *late, *wires.past[-2])
    vector_grads = vector_grads.value
    panel_grads = jnp.concatenate(
        [
            late[0].value,
            trade_cores(first_out.total()),
            late[1].value,
            early[2].value,
            early[0].value,
            early[1].value,
        ],
        axis=0,
    )
    vector_first_new = beta_one * vector_first + (1.0 - beta_one) * vector_grads
    vector_second_new = beta_two * vector_second + (1.0 - beta_two) * vector_grads * vector_grads
    vectors_new = vectors - vector_rate * adam_step(vector_first_new, vector_second_new)
    panel_grads = Cell(panel_grads)
    updated = [Cell(vector_first_new), Cell(vector_second_new), Cell(vectors_new)]
    bind(panel_grads, frames_grad, *updated)
    panel_grads = panel_grads.value

    slot_count = panel_first.shape[1]
    panel_count = owners.shape[0]
    panel_index = jnp.arange(panel_count, dtype=jnp.int32)
    same_owner = owners[:, None] == owners[None, :]
    earlier = panel_index[None, :] < panel_index[:, None]
    slot_of = jnp.sum((same_owner & earlier).astype(jnp.int32), axis=1)
    target = owners * slot_count + slot_of
    slot_hit = target[:, None] == jnp.arange(owners_count * slot_count, dtype=jnp.int32)[None, :]
    source = jnp.sum(slot_hit.astype(jnp.int32) * panel_index[:, None], axis=0)
    filled = jnp.any(slot_hit, axis=0)
    mine = lax.dynamic_slice_in_dim(filled, lax.axis_index("f") * slot_count, slot_count)

    outgoing = pick(panel_grads.astype(bf16), source)
    outgoing = outgoing.reshape(owners_count, slot_count, depth, quarter)
    incoming = lax.all_to_all(outgoing, "f", split_axis=0, concat_axis=0, tiled=True)
    block = lax.axis_index("o") * 2 + core
    left_rows = lax.dynamic_slice_in_dim(left.value, block * quarter, quarter, 1)
    results = []
    for s in range(slot_count):
        turned = dot_tn(left.value[s], incoming[:, s].reshape(width, quarter)).astype(bf16)
        turned = trade_blocks(turned.reshape(outer, 2 * quarter, quarter), "o", outer)
        turned = turned.reshape(outer, 2, quarter, quarter).transpose(1, 0, 2, 3)
        turned = trade_blocks(turned, "c", 2)
        turned = turned.transpose(2, 1, 0, 3).reshape(quarter, width)
        rotated = dot(turned, right.value[s])
        first_new = beta_one * panel_first[:, s] + (1.0 - beta_one) * rotated
        second_new = beta_two * panel_second[:, s] + (1.0 - beta_two) * rotated * rotated
        step_values = adam_step(first_new, second_new).astype(bf16)
        back_turn = dot_nt(step_values, right.value[s]).astype(bf16)
        back_turn = gather_blocks(back_turn, "o", outer)
        back_turn = gather_blocks(back_turn, "c", 2)
        back_turn = back_turn.transpose(1, 0, 2, 3).reshape(width, width)
        update = dot(left_rows[s], back_turn)
        results.append(
            (
                jnp.where(mine[s], first_new, 0.0),
                jnp.where(mine[s], second_new, 0.0),
                jnp.where(mine[s], panel_master[:, s] - learn_rate * update, 0.0),
            )
        )
    first_new, second_new, master_new = [jnp.stack(part, axis=1) for part in zip(*results)]
    return (
        layer_out.reshape(frames.shape),
        frames_grad.value.reshape(frames.shape),
        panel_grads,
        vector_grads,
        *values(updated),
        first_new,
        second_new,
        master_new,
    )


def solution(mesh):
    outer = mesh.shape["dp"] // 2
    owners_count = mesh.shape["fsdp"]
    split = Mesh(mesh.devices.reshape(outer, 2, owners_count), ("o", "c", "f"))
    every = P(("o", "c", "f"), None, None)
    state = P(("o", "c"), "f", None)
    return jax.shard_map(
        functools.partial(on_device, outer, owners_count),
        mesh=split,
        in_specs=(
            every,
            P(("o", "c", "f")),
            every,
            P(None, "f", None),
            P(),
            P(),
            P(),
            P(),
            P("f", None, None),
            P("f", None, None),
            state,
            state,
            state,
        ),
        out_specs=(
            every,
            every,
            P(None, "f", ("o", "c")),
            P(),
            P(),
            P(),
            P(),
            state,
            state,
            state,
        ),
        check_vma=False,
    )
```

time: 2040 us -> 741 us (0.36)
  waiting for transfers between devices: 1520 us -> 257 us
  local copies, waits for them, and re-layouts: 222 us -> 36.3 us
  matrix products: 194 us -> 25.5 us
  Pallas kernels: 0 us -> 159 us
  starting transfers between devices: 5.91 us -> 162 us
  other arithmetic: 61.2 us -> 89.6 us
    all_gather x4 -> x0, waiting for transfers between devices: 639 us -> none  [fetch_block(): return lax.all_gather(panel_rows, 'fsdp', axis=1, tiled=True)]
    unnamed x16 -> x0, waiting for transfers between devices: 631 us -> none
    ppermute x0 -> x126, waiting for transfers between devices: none -> 221 us  [the longest x102 188 us: start(): came.append(Cell(lax.ppermute(value, axis, pairs)))]
    unnamed x204 -> x180, local copies, waits for them, and re-layouts: 197 us -> 11.2 us
    dot_general x34 -> x12, matrix products: 194 us -> 25.5 us  [the longest x6 15.5 us: dot(): lax.dot_general(left, right, (((1,), (0,)), ((), ())), preferred_element_...]
    pallas_call x0 -> x16, Pallas kernels: none -> 159 us  [the longest x6 66 us: panel_call(): pl.pallas_call(functools.partial(kernel, count), out_shape=outs, in_specs...]
    ppermute x0 -> x126, starting transfers between devices: none -> 157 us  [the longest x102 102 us: start(): came.append(Cell(lax.ppermute(value, axis, pairs)))]
    reduce_scatter x3 -> x0, waiting for transfers between devices: 145 us -> none  [the longest x1 57.3 us: on_device(): lax.psum_scatter(jnp.einsum('sak,ksx->asx', part_rows, back_turn, precisi...]
  transfers between devices with their start and end apart: 13 -> 127, of which waited for: 12 -> 46; matrix products, arithmetic and copies ran while one was open for 16% -> 14% of each run, Pallas kernels for 0% -> 16%
where the time goes in v1:
time: 741 us; the launch traced here: 732 us
  waiting for transfers between devices  257 us (35%)
  starting transfers between devices  162 us (22%)
  Pallas kernels  159 us (21%)
  other arithmetic  89.6 us (12%)
  local copies, waits for them, and re-layouts  36.3 us (5%)
  matrix products  25.5 us (3%)
    ppermute x102, waiting for transfers between devices, start(): came.append(Cell(lax.ppermute(value, axis, pairs)))  188 us
    ppermute x102, starting transfers between devices, start(): came.append(Cell(lax.ppermute(value, axis, pairs)))  102 us
    pallas_call x6, Pallas kernels, panel_call(): pl.pallas_call(functools.partial(kernel, count), out_shape=outs, in_specs...  66 us
    pallas_call x4, Pallas kernels, ffn_backward_call(): pl.pallas_call(functools.partial(kernel, count, bias, (outer, ways)), out...  51.9 us
    ppermute x12, starting transfers between devices, swap_cores(): return lax.ppermute(values, 'c', SWAP)  36.7 us
    all_to_all x1, waiting for transfers between devices, on_device(): lax.all_to_all(outgoing, 'f', split_axis=0, concat_axis=0, tiled=True)  35.7 us
    pallas_call x2, Pallas kernels, ffn_forward_call(): pl.pallas_call(functools.partial(ffn_forward_kernel, count), out_shape=[j...  25.6 us
    ppermute x6, waiting for transfers between devices, gather_blocks(): other = lax.ppermute(values, name, SWAP)  22.6 us
  transfers between devices with their start and end apart: 127, of which 46 were waited for; matrix products, arithmetic and copies ran while one was open for 14% of the time, Pallas kernels for 16%

profile of v1, /device:TPU:1, one launch (start us, length us, event | category | flops | bytes accessed | tf_op | source)
XLA Modules:
  0.0 731.6 jit_solution(14350626862633824110)
XLA Ops:
  26.0 9.1 %collective-permute-done.7.refs_3_ = bf16[2,128,1024]{2,1,0:T(8,128)(2,1)S(1)} collective-permute-done((bf16[2,128,1024]{2,1,0:T(8,128)(2,1)}, bf16[2,128,1024]{2,1,0:T(8,128)(2,1)S(1)}, u32[]{:S(2)}, u32[]{:S(2)}) %collective-permute-start.7) | collective-permute-done | bytes 524320 | tf_op jit(solution)/shard_map/ppermute | solution.py:106
  38.7 16.2 %collective-permute-done.4.refs_1_ = bf16[7,128,512]{2,1,0:T(8,128)(2,1)S(1)} collective-permute-done((bf16[7,128,512]{2,1,0:T(8,128)(2,1)S(1)}, bf16[7,128,512]{2,1,0:T(8,128)(2,1)S(1)}, u32[]{:S(2)}, u32[]{:S(2)}) %collective-permute-start.4) | collective-permute-done | bytes 917536 | tf_op jit(solution)/shard_map/ppermute | solution.py:106
  73.6 5.2 collective-permute-done.9.refs_1_
  85.9 4.1 collective-permute-done.21.refs_7_
  91.1 8.2 %convert_element_type.511 = bf16[3,1024,1024]{2,1,0:T(8,128)(2,1)} convert(f32[3,1024,1024]{2,1,0:T(8,128)} %param.21) | non-fusion elementwise | flops 3145728 | bytes 18874368 | tf_op jit(solution)/shard_map/convert_element_type | solution.py:914
  99.3 8.2 %convert_element_type.512 = bf16[3,1024,1024]{2,1,0:T(8,128)(2,1)} convert(f32[3,1024,1024]{2,1,0:T(8,128)} %param.22) | non-fusion elementwise | flops 3145728 | bytes 18874368 | tf_op jit(solution)/shard_map/convert_element_type | solution.py:915
  110.8 6.7 collective-permute-done.22.refs_15_
  117.4 12.8 %ffn_forward.2 = (f32[2,512,1024]{2,1,0:T(8,128)}, bf16[2,512,1024]{2,1,0:T(8,128)(2,1)}, f32[256,1024]{1,0:T(8,128)}, bf16[256,1024]{1,0:T(8,128)(2,1)}) custom-call(s32[9]{0:T(128)} %concatenate.99.meta, bf16[512,1024]{1,0:T(8,128)(2,1)} %pad_maximum_fusion.3.normed, f32[2,1,1024]{2,1,0:T(1,128)} %copy.49.bias, ...), custom_call_target="tpu_custom_call" | custom-call | flops 4294967296 | bytes 17825792 | tf_op jit(solution)/shard_map/ffn_forward/pallas_call | solution.py:332
  130.3 7.9 %collective-permute-start.25 = (bf16[256,1024]{1,0:T(8,128)(2,1)}, bf16[256,1024]{1,0:T(8,128)(2,1)S(1)}, u32[]{:S(2)}, u32[]{:S(2)}) collective-permute-start(bf16[256,1024]{1,0:T(8,128)(2,1)} %get-tuple-element.268), channel_id=1, source_target_pairs={{0,8},{8,0},{1,9},{9,1},{2,10},{10,2},{3,11},{11,3},{4,12},{12,4},... | collective-permute-start | bytes 1572872 | tf_op jit(solution)/shard_map/ppermute | solution.py:235
  141.3 10.4 %collective-permute-done.29.refs_11_ = bf16[2,128,1024]{2,1,0:T(8,128)(2,1)S(1)} collective-permute-done((bf16[2,128,1024]{2,1,0:T(8,128)(2,1)S(1)}, bf16[2,128,1024]{2,1,0:T(8,128)(2,1)S(1)}, u32[]{:S(2)}, u32[]{:S(2)}) %collective-permute-start.29) | collective-permute-done | bytes 524320 | tf_op jit(solution)/shard_map/ppermute | solution.py:106
  155.4 9.0 %collective-permute-done.31.refs_12_ = bf16[2,128,1024]{2,1,0:T(8,128)(2,1)S(1)} collective-permute-done((bf16[2,128,1024]{2,1,0:T(8,128)(2,1)S(1)}, bf16[2,128,1024]{2,1,0:T(8,128)(2,1)S(1)}, u32[]{:S(2)}, u32[]{:S(2)}) %collective-permute-start.31) | collective-permute-done | bytes 524320 | tf_op jit(solution)/shard_map/ppermute | solution.py:106
  167.1 9.2 %collective-permute-done.36.refs_5_ = bf16[2,128,1024]{2,1,0:T(8,128)(2,1)S(1)} collective-permute-done((bf16[2,128,1024]{2,1,0:T(8,128)(2,1)S(1)}, bf16[2,128,1024]{2,1,0:T(8,128)(2,1)S(1)}, u32[]{:S(2)}, u32[]{:S(2)}) %collective-permute-start.36) | collective-permute-done | bytes 524320 | tf_op jit(solution)/shard_map/ppermute | solution.py:106
  179.2 4.9 collective-permute-start.41
  184.0 12.8 %collective-permute-done.35.refs_7_ = bf16[7,128,512]{2,1,0:T(8,128)(2,1)S(1)} collective-permute-done((bf16[7,128,512]{2,1,0:T(8,128)(2,1)}, bf16[7,128,512]{2,1,0:T(8,128)(2,1)S(1)}, u32[]{:S(2)}, u32[]{:S(2)}) %collective-permute-start.35) | collective-permute-done | bytes 917536 | tf_op jit(solution)/shard_map/ppermute | solution.py:106
  205.9 11.6 %attention_forward.1 = (f32[256,1024]{1,0:T(8,128)}, bf16[256,1024]{1,0:T(8,128)(2,1)}, bf16[256,1024]{1,0:T(8,128)(2,1)}, bf16[256,1024]{1,0:T(8,128)(2,1)}, bf...) custom-call(s32[10]{0:T(128)} %concatenate.94.meta, f32[256,1024]{1,0:T(8,128)} %multiply_add_fusion.3.stream, ...), custom_call_target="tpu_custom_call" | custom-call | flops 2147483648 | bytes 16777216 | tf_op jit(solution)/shard_map/attention_forward/pallas_call | solution.py:819
  217.5 10.5 %conv_forward.1 = (f32[256,1024]{1,0:T(8,128)}, bf16[256,1024]{1,0:T(8,128)(2,1)}, f32[2,256,1024]{2,1,0:T(8,128)}, bf16[256,1024]{1,0:T(8,128)(2,1)}) custom-call(s32[10]{0:T(128)} %concatenate.94.meta, f32[256,1024]{1,0:T(8,128)} %get-tuple-element.302.stream, f32[34,1024]{1,0:T(8,128)} %rows.15, bf16[7,128,512]{2,1,0:T(8,128)(2,1)} %copy-done, ...), custom_call_target="tpu_custom_call" | custom-call | flops 1610612736 | bytes 14680064 | tf_op jit(solution)/shard_map/conv_forward/pallas_call | solution.py:819
  236.0 12.8 %ffn_forward.3 = (f32[2,512,1024]{2,1,0:T(8,128)}, bf16[2,512,1024]{2,1,0:T(8,128)(2,1)}, f32[256,1024]{1,0:T(8,128)}, bf16[256,1024]{1,0:T(8,128)(2,1)}) custom-call(s32[9]{0:T(128)} %concatenate.99.meta, bf16[512,1024]{1,0:T(8,128)(2,1)} %pad_maximum_fusion.4.normed, f32[2,1,1024]{2,1,0:T(1,128)} %broadcast_in_dim.30.bias, ...), custom_call_target="tpu_custom_call" | custom-call | flops 4294967296 | bytes 17825792 | tf_op jit(solution)/shard_map/ffn_forward/pallas_call | solution.py:332
  251.8 4.2 turn.1
  260.2 14.0 %ffn_out_backward.2 = (bf16[2,512,1024]{2,1,0:T(8,128)(2,1)}, f32[34,1024]{1,0:T(8,128)}, bf16[2,2,2,1024,256]{4,3,2,1,0:T(8,128)(2,1)}) custom-call(s32[11]{0:T(128)} %concatenate.102.meta, f32[2,512,1024]{2,1,0:T(8,128)} %get-tuple-element.315.hidden, bf16[2,512,1024]{2,1,0:T(8,128)(2,1)} %get-tuple-element.316.active, ...), custom_call_target="tpu_custom_call" | custom-call | flops 4294967296 | bytes 16777216 | tf_op jit(solution)/shard_map/ffn_out_backward/pallas_call | solution.py:424
  277.5 11.9 %ffn_in_backward.2 = (f32[256,1024]{1,0:T(8,128)}, bf16[256,1024]{1,0:T(8,128)(2,1)}, bf16[2,2,1024,256]{3,2,1,0:T(8,128)(2,1)}, bf16[2,1024,256]{2,1,0:T(8,128)(2,1)}, bf16[2,1024,256]{2,1,0:T(8,128)(2,1)}) custom-call(s32[11]{0:T(128)} %concatenate.102.meta, bf16[512,1024]{1,0:T(8,128)(2,1)} %pad_maximum_fusion.4.normed, ...), custom_call_target="tpu_custom_call" | custom-call | flops 4294967296 | bytes 16777216 | tf_op jit(solution)/shard_map/ffn_in_backward/pallas_call | solution.py:424
  296.5 3.9 norm_pull.2
  300.3 11.2 %conv_out_backward.1 = (bf16[2,256,1024]{2,1,0:T(8,128)(2,1)}, bf16[2,1,1024,256]{3,2,1,0:T(8,128)(2,1)}, bf16[2,1,1024,256]{3,2,1,0:T(8,128)(2,1)}, f32[34,1024]{1,0:T(8,128)}) custom-call(s32[10]{0:T(128)} %concatenate.94.meta, f32[256,1024]{1,0:T(8,128)} %get-tuple-element.327.grad, f32[2,256,1024]{2,1,0:T(8,128)} %get-tuple-element.329.wide, ...), custom_call_target="tpu_custom_call" | custom-call | flops 1073741824 | bytes 10485760 | tf_op jit(solution)/shard_map/conv_out_backward/pallas_call | solution.py:819
  320.4 9.5 %conv_in_backward.1 = (f32[256,1024]{1,0:T(8,128)}, bf16[2,2,1024,256]{3,2,1,0:T(8,128)(2,1)}, bf16[2,2,1024,256]{3,2,1,0:T(8,128)(2,1)}, f32[34,1024]{1,0:T(8,128)}) custom-call(s32[10]{0:T(128)} %concatenate.94.meta, f32[256,1024]{1,0:T(8,128)} %get-tuple-element.327.grad, f32[256,1024]{1,0:T(8,128)} %get-tuple-element.302.stream, ...), custom_call_target="tpu_custom_call" | custom-call | flops 2147483648 | bytes 12582912 | tf_op jit(solution)/shard_map/conv_in_backward/pallas_call | solution.py:819
  329.8 10.6 %attention_heads_backward.1 = (bf16[3,256,1024]{2,1,0:T(8,128)(2,1)}, bf16[2,1,1024,256]{3,2,1,0:T(8,128)(2,1)}, bf16[2,1,1024,256]{3,2,1,0:T(8,128)(2,1)}, f32[34,1024]{1,0:T(8,128)}) custom-call(s32[10]{0:T(128)} %concatenate.94.meta, f32[256,1024]{1,0:T(8,128)} %get-tuple-element.341.grad, bf16[256,1024]{1,0:T(8,128)(2,1)} %get-tuple-element.343.queries, ...), custom_call_target="tpu_custom_call" | custom-call | flops 1610612736 | bytes 10485760 | tf_op jit(solution)/shard_map/attention_heads_backward/pallas_call | solution.py:819
  348.7 12.6 %attention_in_backward.1 = (f32[256,1024]{1,0:T(8,128)}, bf16[2,3,1024,256]{3,2,1,0:T(8,128)(2,1)}, bf16[2,3,1024,256]{3,2,1,0:T(8,128)(2,1)}, f32[34,1024]{1,0:T(8,128)}, bf16[256,1024]{1,0:T(8,128)(2,1)}) custom-call(s32[10]{0:T(128)} %concatenate.94.meta, f32[256,1024]{1,0:T(8,128)} %get-tuple-element.341.grad, f32[256,1024]{1,0:T(8,128)} %multiply_add_fusion.3.stream, ...), custom_call_target="tpu_custom_call" | custom-call | flops 3221225472 | bytes 14680064 | tf_op jit(solution)/shard_map/attention_in_backward/pallas_call | solution.py:819
  380.0 6.3 collective-permute-done.66
  387.2 14.5 %ffn_out_backward.3 = (bf16[2,512,1024]{2,1,0:T(8,128)(2,1)}, f32[34,1024]{1,0:T(8,128)}, bf16[2,2,1024,256]{3,2,1,0:T(8,128)(2,1)}, bf16[2,1024,256]{2,1,0:T(8,128)(2,1)}, bf16[2,1024,256]{2,1,0:T(8,128)(2,1)}) custom-call(s32[11]{0:T(128)} %concatenate.102.meta, f32[2,512,1024]{2,1,0:T(8,128)} %get-tuple-element.360.hidden, ...), custom_call_target="tpu_custom_call" | custom-call | flops 4294967296 | bytes 16777216 | tf_op jit(solution)/shard_map/ffn_out_backward/pallas_call | solution.py:424
  414.1 11.5 %ffn_in_backward.3 = (f32[256,1024]{1,0:T(8,128)}, bf16[256,1024]{1,0:T(8,128)(2,1)}, bf16[2,2,2,1024,256]{4,3,2,1,0:T(8,128)(2,1)}) custom-call(s32[11]{0:T(128)} %concatenate.102.meta, bf16[512,1024]{1,0:T(8,128)(2,1)} %pad_maximum_fusion.3.normed, bf16[2,512,1024]{2,1,0:T(8,128)(2,1)} %get-tuple-element.392.low, ...), custom_call_target="tpu_custom_call" | custom-call | flops 4294967296 | bytes 16777216 | tf_op jit(solution)/shard_map/ffn_in_backward/pallas_call | solution.py:424
  436.2 10.6 %collective-permute-done.73 = bf16[2,2,128,256]{3,2,1,0:T(8,128)(2,1)} collective-permute-done((bf16[2,2,128,256]{3,2,1,0:T(8,128)(2,1)}, bf16[2,2,128,256]{3,2,1,0:T(8,128)(2,1)}, u32[]{:S(2)}, u32[]{:S(2)}) %collective-permute-start.73) | collective-permute-done | bytes 262176 | tf_op jit(solution)/shard_map/ppermute | solution.py:106
  456.3 4.8 collective-permute-start.76
  467.1 8.0 %collective-permute-done.81 = bf16[2,1024,256]{2,1,0:T(8,128)(2,1)} collective-permute-done((bf16[2,1024,256]{2,1,0:T(8,128)(2,1)}, bf16[2,1024,256]{2,1,0:T(8,128)(2,1)}, u32[]{:S(2)}, u32[]{:S(2)}) %collective-permute-start.81) | collective-permute-done | bytes 1048608 | tf_op jit(solution)/shard_map/ppermute | solution.py:106
  483.3 5.4 collective-permute-done.86
  500.7 4.2 collective-permute-done.82
  506.5 7.5 %collective-permute-done.84 = bf16[2,2,2,128,256]{4,3,2,1,0:T(8,128)(2,1)S(1)} collective-permute-done((bf16[2,2,2,128,256]{4,3,2,1,0:T(8,128)(2,1)S(1)}, bf16[2,2,2,128,256]{4,3,2,1,0:T(8,128)(2,1)S(1)}, u32[]{:S(2)}, u32[]{:S(2)}) %collective-permute-start.84) | collective-permute-done | bytes 524320 | tf_op jit(solution)/shard_map/ppermute | solution.py:106
  520.3 16.3 %collective-permute-done.95 = bf16[4,128,256]{2,1,0:T(8,128)(2,1)S(1)} collective-permute-done((bf16[4,128,256]{2,1,0:T(8,128)(2,1)S(1)}, bf16[4,128,256]{2,1,0:T(8,128)(2,1)S(1)}, u32[]{:S(2)}, u32[]{:S(2)}) %collective-permute-start.95) | collective-permute-done | bytes 262176 | tf_op jit(solution)/shard_map/ppermute | solution.py:106
  537.9 7.3 collective-permute-done.108
  551.3 4.6 collective-permute-done.104
  556.0 9.5 %collective-permute-start.102 = (bf16[2,128,256]{2,1,0:T(8,128)(2,1)S(1)}, bf16[2,128,256]{2,1,0:T(8,128)(2,1)S(1)}, u32[]{:S(2)}, u32[]{:S(2)}) collective-permute-start(bf16[2,128,256]{2,1,0:T(8,128)(2,1)S(1)} %fusion.90), channel_id=1, source_target_pairs={{0,8},{8,0},{1,9},{9,1},{2,10},{10,2},{3,11},{11,3},{4,12},{12,4},... | collective-permute-start | bytes 393224 | tf_op jit(solution)/shard_map/ppermute | solution.py:235
  575.1 5.6 collective-permute-done.109
  582.1 8.3 %collective-permute-start.113 = (bf16[2,128,256]{2,1,0:T(8,128)(2,1)S(1)}, bf16[2,128,256]{2,1,0:T(8,128)(2,1)S(1)}, u32[]{:S(2)}, u32[]{:S(2)}) collective-permute-start(bf16[2,128,256]{2,1,0:T(8,128)(2,1)S(1)} %fusion.91), channel_id=1, source_target_pairs={{0,8},{8,0},{1,9},{9,1},{2,10},{10,2},{3,11},{11,3},{4,12},{12,4},... | collective-permute-start | bytes 393224 | tf_op jit(solution)/shard_map/ppermute | solution.py:235
  597.9 4.6 all-to-all-start
  603.4 35.7 %all-to-all-done = bf16[8,3,128,256]{3,2,1,0:T(8,128)(2,1)} async-done(((bf16[8,3,128,256]{3,2,1,0:T(8,128)(2,1)}), bf16[8,3,128,256]{3,2,1,0:T(8,128)(2,1)}, u32[]{:S(2)}, u32[]{:S(2)}) %all-to-all-start) | async-done | bytes 1572896 | tf_op jit(solution)/shard_map/all_to_all | solution.py:1249
  649.9 4.0 collective-permute-start.115
  655.5 4.0 collective-permute-start.119
  684.6 3.8 select_bitcast_fusion.11
  688.4 4.8 collective-permute-done.124
  696.5 7.9 %collective-permute-done.122 = bf16[256,1024]{1,0:T(8,128)(2,1)S(1)} collective-permute-done((bf16[256,1024]{1,0:T(8,128)(2,1)S(1)}, bf16[256,1024]{1,0:T(8,128)(2,1)S(1)}, u32[]{:S(2)}, u32[]{:S(2)}) %collective-permute-start.122) | collective-permute-done | bytes 524320 | tf_op jit(solution)/shard_map/ppermute | solution.py:249
  705.9 9.8 %collective-permute-done.120 = bf16[256,1024]{1,0:T(8,128)(2,1)S(1)} collective-permute-done((bf16[256,1024]{1,0:T(8,128)(2,1)S(1)}, bf16[256,1024]{1,0:T(8,128)(2,1)S(1)}, u32[]{:S(2)}, u32[]{:S(2)}) %collective-permute-start.120) | collective-permute-done | bytes 524320 | tf_op jit(solution)/shard_map/ppermute | solution.py:249
  (569 shorter events, 291.5 us)
Async XLA Ops:
  23.2 31.8 %collective-permute-start.4 = (bf16[7,128,512]{2,1,0:T(8,128)(2,1)S(1)}, bf16[7,128,512]{2,1,0:T(8,128)(2,1)S(1)}, u32[]{:S(2)}, u32[]{:S(2)}) collective-permute-start(bf16[7,128,512]{2,1,0:T(8,128)(2,1)S(1)} %constant_dynamic-slice_fusion.28.refs_0_), channel_id=1, source_target_pairs={{0,2},{2,4},{4,6},{6,7},{7,5},{5,3},{3,1},{1,0},{8,10},{10,12},{12... | collective-permute-start | bytes 2752520 | tf_op jit(solution)/shard_map/ppermute | solution.py:106
  24.6 31.6 %collective-permute-start.5 = (bf16[7,128,512]{2,1,0:T(8,128)(2,1)S(1)}, bf16[7,128,512]{2,1,0:T(8,128)(2,1)}, u32[]{:S(2)}, u32[]{:S(2)}) collective-permute-start(bf16[7,128,512]{2,1,0:T(8,128)(2,1)S(1)} %constant_dynamic-slice_fusion.28.refs_0_), channel_id=1, source_target_pairs={{2,0},{4,2},{6,4},{7,6},{5,7},{3,5},{1,3},{0,1},{10,8},{12,10},{14... | collective-permute-start | bytes 2752520 | tf_op jit(solution)/shard_map/ppermute | solution.py:106
  35.2 22.3 %collective-permute-start.6 = (bf16[2,128,1024]{2,1,0:T(8,128)(2,1)}, bf16[2,128,1024]{2,1,0:T(8,128)(2,1)S(1)}, u32[]{:S(2)}, u32[]{:S(2)}) collective-permute-start(bf16[2,128,1024]{2,1,0:T(8,128)(2,1)} %collective-permute-done.2.refs_2_), channel_id=1, source_target_pairs={{0,16},{16,0},{1,17},{17,1},{2,18},{18,2},{3,19},{19,3},{4,20},{20... | collective-permute-start | bytes 1572872 | tf_op jit(solution)/shard_map/ppermute | solution.py:106
  36.4 23.5 %collective-permute-start.8 = (bf16[2,128,1024]{2,1,0:T(8,128)(2,1)S(1)}, bf16[2,128,1024]{2,1,0:T(8,128)(2,1)}, u32[]{:S(2)}, u32[]{:S(2)}) collective-permute-start(bf16[2,128,1024]{2,1,0:T(8,128)(2,1)S(1)} %collective-permute-done.7.refs_3_), channel_id=1, source_target_pairs={{0,16},{16,0},{1,17},{17,1},{2,18},{18,2},{3,19},{19,3},{4,20},{20... | collective-permute-start | bytes 1572872 | tf_op jit(solution)/shard_map/ppermute | solution.py:106
  37.4 28.7 %collective-permute-start.13 = (bf16[2,128,1024]{2,1,0:T(8,128)(2,1)S(1)}, bf16[2,128,1024]{2,1,0:T(8,128)(2,1)S(1)}, u32[]{:S(2)}, u32[]{:S(2)}) collective-permute-start(bf16[2,128,1024]{2,1,0:T(8,128)(2,1)S(1)} %collective-permute-done.7.refs_3_), channel_id=1, source_target_pairs={{0,2},{2,4},{4,6},{6,7},{7,5},{5,3},{3,1},{1,0},{8,10},{10,12},{12... | collective-permute-start | bytes 1572872 | tf_op jit(solution)/shard_map/ppermute | solution.py:106
  83.0 27.2 %collective-permute-start.15 = (bf16[7,128,512]{2,1,0:T(8,128)(2,1)S(1)}, bf16[7,128,512]{2,1,0:T(8,128)(2,1)S(1)}, u32[]{:S(2)}, u32[]{:S(2)}) collective-permute-start(bf16[7,128,512]{2,1,0:T(8,128)(2,1)S(1)} %collective-permute-done.4.refs_1_), channel_id=1, source_target_pairs={{0,2},{2,4},{4,6},{6,7},{7,5},{5,3},{3,1},{1,0},{8,10},{10,12},{12... | collective-permute-start | bytes 2752520 | tf_op jit(solution)/shard_map/ppermute | solution.py:106
  83.8 27.0 %collective-permute-start.16 = (bf16[7,128,512]{2,1,0:T(8,128)(2,1)}, bf16[7,128,512]{2,1,0:T(8,128)(2,1)}, u32[]{:S(2)}, u32[]{:S(2)}) collective-permute-start(bf16[7,128,512]{2,1,0:T(8,128)(2,1)} %collective-permute-done.5.refs_2_), channel_id=1, source_target_pairs={{2,0},{4,2},{6,4},{7,6},{5,7},{3,5},{1,3},{0,1},{10,8},{12,10},{14... | collective-permute-start | bytes 2752520 | tf_op jit(solution)/shard_map/ppermute | solution.py:106
  84.4 24.3 %collective-permute-start.24 = (bf16[2,128,1024]{2,1,0:T(8,128)(2,1)}, bf16[2,128,1024]{2,1,0:T(8,128)(2,1)}, u32[]{:S(2)}, u32[]{:S(2)}) collective-permute-start(bf16[2,128,1024]{2,1,0:T(8,128)(2,1)} %collective-permute-done.17.refs_6_), channel_id=1, source_target_pairs={{0,16},{16,0},{1,17},{17,1},{2,18},{18,2},{3,19},{19,3},{4,20},{20... | collective-permute-start | bytes 1572872 | tf_op jit(solution)/shard_map/ppermute | solution.py:106
  85.2 24.7 %collective-permute-start.23 = (bf16[2,128,1024]{2,1,0:T(8,128)(2,1)}, bf16[2,128,1024]{2,1,0:T(8,128)(2,1)}, u32[]{:S(2)}, u32[]{:S(2)}) collective-permute-start(bf16[2,128,1024]{2,1,0:T(8,128)(2,1)} %collective-permute-done.9.refs_1_), channel_id=1, source_target_pairs={{0,16},{16,0},{1,17},{17,1},{2,18},{18,2},{3,19},{19,3},{4,20},{20... | collective-permute-start | bytes 1572872 | tf_op jit(solution)/shard_map/ppermute | solution.py:106
  90.0 27.4 %collective-permute-start.22 = (bf16[2,128,1024]{2,1,0:T(8,128)(2,1)}, bf16[2,128,1024]{2,1,0:T(8,128)(2,1)}, u32[]{:S(2)}, u32[]{:S(2)}) collective-permute-start(bf16[2,128,1024]{2,1,0:T(8,128)(2,1)} %collective-permute-done.21.refs_7_), channel_id=1, source_target_pairs={{0,16},{16,0},{1,17},{17,1},{2,18},{18,2},{3,19},{19,3},{4,20},{20... | collective-permute-start | bytes 1572872 | tf_op jit(solution)/shard_map/ppermute | solution.py:106
  108.7 30.9 %collective-permute-start.30 = (bf16[2,128,1024]{2,1,0:T(8,128)(2,1)}, bf16[2,128,1024]{2,1,0:T(8,128)(2,1)S(1)}, u32[]{:S(2)}, u32[]{:S(2)}) collective-permute-start(bf16[2,128,1024]{2,1,0:T(8,128)(2,1)} %copy-done.73), channel_id=1, source_target_pairs={{2,0},{4,2},{6,4},{7,6},{5,7},{3,5},{1,3},{0,1},{10,8},{12,10},{14... | collective-permute-start | bytes 1572872 | tf_op jit(solution)/shard_map/ppermute | solution.py:106
  109.9 29.9 %collective-permute-start.32 = (bf16[2,128,1024]{2,1,0:T(8,128)(2,1)}, bf16[2,128,1024]{2,1,0:T(8,128)(2,1)S(1)}, u32[]{:S(2)}, u32[]{:S(2)}) collective-permute-start(bf16[2,128,1024]{2,1,0:T(8,128)(2,1)} %copy-done.73), channel_id=1, source_target_pairs={{0,16},{16,0},{1,17},{17,1},{2,18},{18,2},{3,19},{19,3},{4,20},{20... | collective-permute-start | bytes 1572872 | tf_op jit(solution)/shard_map/ppermute | solution.py:106
  110.2 28.0 %collective-permute-start.28 = (bf16[2,128,1024]{2,1,0:T(8,128)(2,1)}, bf16[2,128,1024]{2,1,0:T(8,128)(2,1)S(1)}, u32[]{:S(2)}, u32[]{:S(2)}) collective-permute-start(bf16[2,128,1024]{2,1,0:T(8,128)(2,1)} %collective-permute-done.9.refs_1_), channel_id=1, source_target_pairs={{0,2},{2,4},{4,6},{6,7},{7,5},{5,3},{3,1},{1,0},{8,10},{10,12},{12... | collective-permute-start | bytes 1572872 | tf_op jit(solution)/shard_map/ppermute | solution.py:106
  139.3 25.2 %collective-permute-start.33 = (bf16[7,128,512]{2,1,0:T(8,128)(2,1)S(1)}, bf16[7,128,512]{2,1,0:T(8,128)(2,1)S(1)}, u32[]{:S(2)}, u32[]{:S(2)}) collective-permute-start(bf16[7,128,512]{2,1,0:T(8,128)(2,1)S(1)} %collective-permute-done.15.refs_3_), channel_id=1, source_target_pairs={{0,8},{8,0},{1,9},{9,1},{2,10},{10,2},{3,11},{11,3},{4,12},{12,4},... | collective-permute-start | bytes 2752520 | tf_op jit(solution)/shard_map/ppermute | solution.py:106
  139.7 24.8 %collective-permute-start.34 = (bf16[7,128,512]{2,1,0:T(8,128)(2,1)}, bf16[7,128,512]{2,1,0:T(8,128)(2,1)S(1)}, u32[]{:S(2)}, u32[]{:S(2)}) collective-permute-start(bf16[7,128,512]{2,1,0:T(8,128)(2,1)} %collective-permute-done.16.refs_4_), channel_id=1, source_target_pairs={{0,8},{8,0},{1,9},{9,1},{2,10},{10,2},{3,11},{11,3},{4,12},{12,4},... | collective-permute-start | bytes 2752520 | tf_op jit(solution)/shard_map/ppermute | solution.py:106
  139.8 24.7 %collective-permute-start.26 = (bf16[7,128,512]{2,1,0:T(8,128)(2,1)S(1)}, bf16[7,128,512]{2,1,0:T(8,128)(2,1)}, u32[]{:S(2)}, u32[]{:S(2)}) collective-permute-start(bf16[7,128,512]{2,1,0:T(8,128)(2,1)S(1)} %collective-permute-done.15.refs_3_), channel_id=1, source_target_pairs={{0,2},{2,4},{4,6},{6,7},{7,5},{5,3},{3,1},{1,0},{8,10},{10,12},{12... | collective-permute-start | bytes 2752520 | tf_op jit(solution)/shard_map/ppermute | solution.py:106
  141.2 23.3 %collective-permute-start.27 = (bf16[7,128,512]{2,1,0:T(8,128)(2,1)}, bf16[7,128,512]{2,1,0:T(8,128)(2,1)}, u32[]{:S(2)}, u32[]{:S(2)}) collective-permute-start(bf16[7,128,512]{2,1,0:T(8,128)(2,1)} %collective-permute-done.16.refs_4_), channel_id=1, source_target_pairs={{2,0},{4,2},{6,4},{7,6},{5,7},{3,5},{1,3},{0,1},{10,8},{12,10},{14... | collective-permute-start | bytes 2752520 | tf_op jit(solution)/shard_map/ppermute | solution.py:106
  166.0 30.9 %collective-permute-start.35 = (bf16[7,128,512]{2,1,0:T(8,128)(2,1)}, bf16[7,128,512]{2,1,0:T(8,128)(2,1)S(1)}, u32[]{:S(2)}, u32[]{:S(2)}) collective-permute-start(bf16[7,128,512]{2,1,0:T(8,128)(2,1)} %collective-permute-done.27.refs_6_), channel_id=1, source_target_pairs={{2,0},{4,2},{6,4},{7,6},{5,7},{3,5},{1,3},{0,1},{10,8},{12,10},{14... | collective-permute-start | bytes 2752520 | tf_op jit(solution)/shard_map/ppermute | solution.py:106
  176.3 23.4 %collective-permute-start.37 = (bf16[2,128,1024]{2,1,0:T(8,128)(2,1)S(1)}, bf16[2,128,1024]{2,1,0:T(8,128)(2,1)}, u32[]{:S(2)}, u32[]{:S(2)}) collective-permute-start(bf16[2,128,1024]{2,1,0:T(8,128)(2,1)S(1)} %collective-permute-done.36.refs_5_), channel_id=1, source_target_pairs={{0,2},{2,4},{4,6},{6,7},{7,5},{5,3},{3,1},{1,0},{8,10},{10,12},{12... | collective-permute-start | bytes 1572872 | tf_op jit(solution)/shard_map/ppermute | solution.py:106
  177.7 22.1 %collective-permute-start.38 = (bf16[2,128,1024]{2,1,0:T(8,128)(2,1)S(1)}, bf16[2,128,1024]{2,1,0:T(8,128)(2,1)S(1)}, u32[]{:S(2)}, u32[]{:S(2)}) collective-permute-start(bf16[2,128,1024]{2,1,0:T(8,128)(2,1)S(1)} %collective-permute-done.36.refs_5_), channel_id=1, source_target_pairs={{0,16},{16,0},{1,17},{17,1},{2,18},{18,2},{3,19},{19,3},{4,20},{20... | collective-permute-start | bytes 1572872 | tf_op jit(solution)/shard_map/ppermute | solution.py:106
  178.9 20.8 %collective-permute-start.40 = (bf16[2,128,1024]{2,1,0:T(8,128)(2,1)S(1)}, bf16[2,128,1024]{2,1,0:T(8,128)(2,1)S(1)}, u32[]{:S(2)}, u32[]{:S(2)}) collective-permute-start(bf16[2,128,1024]{2,1,0:T(8,128)(2,1)S(1)} %collective-permute-done.39.refs_6_), channel_id=1, source_target_pairs={{0,16},{16,0},{1,17},{17,1},{2,18},{18,2},{3,19},{19,3},{4,20},{20... | collective-permute-start | bytes 1572872 | tf_op jit(solution)/shard_map/ppermute | solution.py:106
  179.2 26.7 %collective-permute-start.41 = (bf16[7,128,512]{2,1,0:T(8,128)(2,1)}, bf16[7,128,512]{2,1,0:T(8,128)(2,1)}, u32[]{:S(2)}, u32[]{:S(2)}) collective-permute-start(bf16[7,128,512]{2,1,0:T(8,128)(2,1)} %collective-permute-done.26.refs_5_), channel_id=1, source_target_pairs={{0,8},{8,0},{1,9},{9,1},{2,10},{10,2},{3,11},{11,3},{4,12},{12,4},... | collective-permute-start | bytes 2752520 | tf_op jit(solution)/shard_map/ppermute | solution.py:106
  290.1 23.3 %collective-permute-start.53 = (bf16[2,1024,256]{2,1,0:T(8,128)(2,1)}, bf16[2,1024,256]{2,1,0:T(8,128)(2,1)S(1)}, u32[]{:S(2)}, u32[]{:S(2)}) collective-permute-start(bf16[2,1024,256]{2,1,0:T(8,128)(2,1)} %get-tuple-element.338), channel_id=1, source_target_pairs={{0,16},{16,0},{1,17},{17,1},{2,18},{18,2},{3,19},{19,3},{4,20},{20... | collective-permute-start | bytes 3145736 | tf_op jit(solution)/shard_map/ppermute | solution.py:106
  313.4 27.1 %collective-permute-start.56 = (bf16[2,1024,256]{2,1,0:T(8,128)(2,1)}, bf16[2,1024,256]{2,1,0:T(8,128)(2,1)S(1)}, u32[]{:S(2)}, u32[]{:S(2)}) collective-permute-start(bf16[2,1024,256]{2,1,0:T(8,128)(2,1)} %get-tuple-element.354), channel_id=1, source_target_pairs={{0,16},{16,0},{1,17},{17,1},{2,18},{18,2},{3,19},{19,3},{4,20},{20... | collective-permute-start | bytes 3145736 | tf_op jit(solution)/shard_map/ppermute | solution.py:106
  314.1 26.4 %collective-permute-start.57 = (bf16[2,1,1024,256]{3,2,1,0:T(8,128)(2,1)}, bf16[2,1,1024,256]{3,2,1,0:T(8,128)(2,1)S(1)}, u32[]{:S(2)}, u32[]{:S(2)}) collective-permute-start(bf16[2,1,1024,256]{3,2,1,0:T(8,128)(2,1)} %get-tuple-element.356), channel_id=1, source_target_pairs={{0,8},{8,0},{1,9},{9,1},{2,10},{10,2},{3,11},{11,3},{4,12},{12,4},... | collective-permute-start | bytes 3145736 | tf_op jit(solution)/shard_map/ppermute | solution.py:106
  318.7 21.7 %collective-permute-start.54 = (bf16[2,2,2,128,256]{4,3,2,1,0:T(8,128)(2,1)S(1)}, bf16[2,2,2,128,256]{4,3,2,1,0:T(8,128)(2,1)S(1)}, u32[]{:S(2)}, u32[]{:S(2)}) collective-permute-start(bf16[2,2,2,128,256]{4,3,2,1,0:T(8,128)(2,1)S(1)} %get-tuple-element.350), channel_id=1, source_target_pairs={{0,2},{2,4},{4,6},{6,7},{7,5},{5,3},{3,1},{1,0},{8,10},{10,12},{12... | collective-permute-start | bytes 1572872 | tf_op jit(solution)/shard_map/ppermute | solution.py:106
  320.0 20.4 %collective-permute-start.55 = (bf16[2,2,2,128,256]{4,3,2,1,0:T(8,128)(2,1)S(1)}, bf16[2,2,2,128,256]{4,3,2,1,0:T(8,128)(2,1)S(1)}, u32[]{:S(2)}, u32[]{:S(2)}) collective-permute-start(bf16[2,2,2,128,256]{4,3,2,1,0:T(8,128)(2,1)S(1)} %get-tuple-element.352), channel_id=1, source_target_pairs={{2,0},{4,2},{6,4},{7,6},{5,7},{3,5},{1,3},{0,1},{10,8},{12,10},{14... | collective-permute-start | bytes 1572872 | tf_op jit(solution)/shard_map/ppermute | solution.py:106
  341.5 21.5 %collective-permute-start.61 = (bf16[2,2,1024,256]{3,2,1,0:T(8,128)(2,1)}, bf16[2,2,1024,256]{3,2,1,0:T(8,128)(2,1)}, u32[]{:S(2)}, u32[]{:S(2)}) collective-permute-start(bf16[2,2,1024,256]{3,2,1,0:T(8,128)(2,1)} %get-tuple-element.371), channel_id=1, source_target_pairs={{0,8},{8,0},{1,9},{9,1},{2,10},{10,2},{3,11},{11,3},{4,12},{12,4},... | collective-permute-start | bytes 6291464 | tf_op jit(solution)/shard_map/ppermute | solution.py:106
  342.1 20.8 %collective-permute-start.62 = (bf16[2,1,1024,256]{3,2,1,0:T(8,128)(2,1)}, bf16[2,1,1024,256]{3,2,1,0:T(8,128)(2,1)}, u32[]{:S(2)}, u32[]{:S(2)}) collective-permute-start(bf16[2,1,1024,256]{3,2,1,0:T(8,128)(2,1)} %get-tuple-element.373), channel_id=1, source_target_pairs={{0,8},{8,0},{1,9},{9,1},{2,10},{10,2},{3,11},{11,3},{4,12},{12,4},... | collective-permute-start | bytes 3145736 | tf_op jit(solution)/shard_map/ppermute | solution.py:106
  363.1 38.6 %collective-permute-start.68 = (bf16[2,3,1024,256]{3,2,1,0:T(8,128)(2,1)}, bf16[2,3,1024,256]{3,2,1,0:T(8,128)(2,1)}, u32[]{:S(2)}, u32[]{:S(2)}) collective-permute-start(bf16[2,3,1024,256]{3,2,1,0:T(8,128)(2,1)} %get-tuple-element.388), channel_id=1, source_target_pairs={{0,8},{8,0},{1,9},{9,1},{2,10},{10,2},{3,11},{11,3},{4,12},{12,4},... | collective-permute-start | bytes 9437192 | tf_op jit(solution)/shard_map/ppermute | solution.py:106
  370.4 31.3 %collective-permute-start.64 = (bf16[2,3,128,256]{3,2,1,0:T(8,128)(2,1)S(1)}, bf16[2,3,128,256]{3,2,1,0:T(8,128)(2,1)}, u32[]{:S(2)}, u32[]{:S(2)}) collective-permute-start(bf16[2,3,128,256]{3,2,1,0:T(8,128)(2,1)S(1)} %pad_maximum_fusion.14), channel_id=1, source_target_pairs={{0,2},{2,4},{4,6},{6,7},{7,5},{5,3},{3,1},{1,0},{8,10},{10,12},{12... | collective-permute-start | bytes 1179656 | tf_op jit(solution)/shard_map/ppermute | solution.py:106
  371.8 29.9 %collective-permute-start.65 = (bf16[2,3,128,256]{3,2,1,0:T(8,128)(2,1)S(1)}, bf16[2,3,128,256]{3,2,1,0:T(8,128)(2,1)S(1)}, u32[]{:S(2)}, u32[]{:S(2)}) collective-permute-start(bf16[2,3,128,256]{3,2,1,0:T(8,128)(2,1)S(1)} %pad_maximum_fusion.15), channel_id=1, source_target_pairs={{2,0},{4,2},{6,4},{7,6},{5,7},{3,5},{1,3},{0,1},{10,8},{12,10},{14... | collective-permute-start | bytes 1179656 | tf_op jit(solution)/shard_map/ppermute | solution.py:106
  378.8 22.9 %collective-permute-start.67 = (bf16[2,2,128,256]{3,2,1,0:T(8,128)(2,1)}, bf16[2,2,128,256]{3,2,1,0:T(8,128)(2,1)S(1)}, u32[]{:S(2)}, u32[]{:S(2)}) collective-permute-start(bf16[2,2,128,256]{3,2,1,0:T(8,128)(2,1)} %get-tuple-element.386), channel_id=1, source_target_pairs={{2,0},{4,2},{6,4},{7,6},{5,7},{3,5},{1,3},{0,1},{10,8},{12,10},{14... | collective-permute-start | bytes 786440 | tf_op jit(solution)/shard_map/ppermute | solution.py:106
  406.8 45.8 %collective-permute-start.74 = (bf16[4,1024,256]{2,1,0:T(8,128)(2,1)}, bf16[4,1024,256]{2,1,0:T(8,128)(2,1)}, u32[]{:S(2)}, u32[]{:S(2)}) collective-permute-start(bf16[4,1024,256]{2,1,0:T(8,128)(2,1)} %fusion.4), channel_id=1, source_target_pairs={{0,16},{16,0},{1,17},{17,1},{2,18},{18,2},{3,19},{19,3},{4,20},{20... | collective-permute-start | bytes 6291464 | tf_op jit(solution)/shard_map/ppermute | solution.py:106
  409.4 38.2 %collective-permute-start.70 = (bf16[2,3,128,256]{3,2,1,0:T(8,128)(2,1)}, bf16[2,3,128,256]{3,2,1,0:T(8,128)(2,1)}, u32[]{:S(2)}, u32[]{:S(2)}) collective-permute-start(bf16[2,3,128,256]{3,2,1,0:T(8,128)(2,1)} %add_convert_fusion.22), channel_id=1, source_target_pairs={{0,2},{2,4},{4,6},{6,7},{7,5},{5,3},{3,1},{1,0},{8,10},{10,12},{12... | collective-permute-start | bytes 1179656 | tf_op jit(solution)/shard_map/ppermute | solution.py:106
  425.5 27.0 %collective-permute-start.75 = (bf16[256,1024]{1,0:T(8,128)(2,1)}, bf16[256,1024]{1,0:T(8,128)(2,1)}, u32[]{:S(2)}, u32[]{:S(2)}) collective-permute-start(bf16[256,1024]{1,0:T(8,128)(2,1)} %get-tuple-element.408), channel_id=1, source_target_pairs={{0,8},{8,0},{1,9},{9,1},{2,10},{10,2},{3,11},{11,3},{4,12},{12,4},... | collective-permute-start | bytes 1572872 | tf_op jit(solution)/shard_map/ppermute | solution.py:235
  446.9 28.2 %collective-permute-start.81 = (bf16[2,1024,256]{2,1,0:T(8,128)(2,1)}, bf16[2,1024,256]{2,1,0:T(8,128)(2,1)}, u32[]{:S(2)}, u32[]{:S(2)}) collective-permute-start(bf16[2,1024,256]{2,1,0:T(8,128)(2,1)} %get-tuple-element.425), channel_id=1, source_target_pairs={{0,16},{16,0},{1,17},{17,1},{2,18},{18,2},{3,19},{19,3},{4,20},{20... | collective-permute-start | bytes 3145736 | tf_op jit(solution)/shard_map/ppermute | solution.py:106
  447.7 27.5 %collective-permute-start.77 = (bf16[2,2,2,128,256]{4,3,2,1,0:T(8,128)(2,1)}, bf16[2,2,2,128,256]{4,3,2,1,0:T(8,128)(2,1)}, u32[]{:S(2)}, u32[]{:S(2)}) collective-permute-start(bf16[2,2,2,128,256]{4,3,2,1,0:T(8,128)(2,1)} %get-tuple-element.488), channel_id=1, source_target_pairs={{0,2},{2,4},{4,6},{6,7},{7,5},{5,3},{3,1},{1,0},{8,10},{10,12},{12... | collective-permute-start | bytes 1572872 | tf_op jit(solution)/shard_map/ppermute | solution.py:106
  448.4 30.6 %collective-permute-start.78 = (bf16[2,2,2,128,256]{4,3,2,1,0:T(8,128)(2,1)}, bf16[2,2,2,128,256]{4,3,2,1,0:T(8,128)(2,1)}, u32[]{:S(2)}, u32[]{:S(2)}) collective-permute-start(bf16[2,2,2,128,256]{4,3,2,1,0:T(8,128)(2,1)} %get-tuple-element.487), channel_id=1, source_target_pairs={{2,0},{4,2},{6,4},{7,6},{5,7},{3,5},{1,3},{0,1},{10,8},{12,10},{14... | collective-permute-start | bytes 1572872 | tf_op jit(solution)/shard_map/ppermute | solution.py:106
  456.3 20.2 %collective-permute-start.76 = (f32[34,1024]{1,0:T(8,128)}, f32[34,1024]{1,0:T(8,128)S(1)}, u32[]{:S(2)}, u32[]{:S(2)}) collective-permute-start(f32[34,1024]{1,0:T(8,128)} %get-tuple-element.423), channel_id=1, source_target_pairs={{0,8},{8,0},{1,9},{9,1},{2,10},{10,2},{3,11},{11,3},{4,12},{12,4},... | collective-permute-start | bytes 417800 | tf_op jit(solution)/shard_map/ppermute | solution.py:106
  480.4 33.7 %collective-permute-start.87 = (bf16[2,1024,256]{2,1,0:T(8,128)(2,1)S(1)}, bf16[2,1024,256]{2,1,0:T(8,128)(2,1)S(1)}, u32[]{:S(2)}, u32[]{:S(2)}) collective-permute-start(bf16[2,1024,256]{2,1,0:T(8,128)(2,1)S(1)} %copy-done.66), channel_id=1, source_target_pairs={{0,16},{16,0},{1,17},{17,1},{2,18},{18,2},{3,19},{19,3},{4,20},{20... | collective-permute-start | bytes 3145736 | tf_op jit(solution)/shard_map/ppermute | solution.py:106
  514.5 22.3 %collective-permute-start.90 = (bf16[2,2,2,128,256]{4,3,2,1,0:T(8,128)(2,1)S(1)}, bf16[2,2,2,128,256]{4,3,2,1,0:T(8,128)(2,1)S(1)}, u32[]{:S(2)}, u32[]{:S(2)}) collective-permute-start(bf16[2,2,2,128,256]{4,3,2,1,0:T(8,128)(2,1)S(1)} %get-tuple-element.435), channel_id=1, source_target_pairs={{2,0},{4,2},{6,4},{7,6},{5,7},{3,5},{1,3},{0,1},{10,8},{12,10},{14... | collective-permute-start | bytes 1572872 | tf_op jit(solution)/shard_map/ppermute | solution.py:106
  515.9 21.9 %collective-permute-start.94 = (bf16[2,2,2,128,256]{4,3,2,1,0:T(8,128)(2,1)S(1)}, bf16[2,2,2,128,256]{4,3,2,1,0:T(8,128)(2,1)S(1)}, u32[]{:S(2)}, u32[]{:S(2)}) collective-permute-start(bf16[2,2,2,128,256]{4,3,2,1,0:T(8,128)(2,1)S(1)} %get-tuple-element.439), channel_id=1, source_target_pairs={{0,2},{2,4},{4,6},{6,7},{7,5},{5,3},{3,1},{1,0},{8,10},{10,12},{12... | collective-permute-start | bytes 1572872 | tf_op jit(solution)/shard_map/ppermute | solution.py:106
  516.0 20.6 %collective-permute-start.95 = (bf16[4,128,256]{2,1,0:T(8,128)(2,1)S(1)}, bf16[4,128,256]{2,1,0:T(8,128)(2,1)S(1)}, u32[]{:S(2)}, u32[]{:S(2)}) collective-permute-start(bf16[4,128,256]{2,1,0:T(8,128)(2,1)S(1)} %get-tuple-element.440), channel_id=1, source_target_pairs={{0,2},{2,4},{4,6},{6,7},{7,5},{5,3},{3,1},{1,0},{8,10},{10,12},{12... | collective-permute-start | bytes 786440 | tf_op jit(solution)/shard_map/ppermute | solution.py:106
  597.9 41.2 %all-to-all-start = ((bf16[8,3,128,256]{3,2,1,0:T(8,128)(2,1)}), bf16[8,3,128,256]{3,2,1,0:T(8,128)(2,1)}, u32[]{:S(2)}, u32[]{:S(2)}) async-start(bf16[8,3,128,256]{3,2,1,0:T(8,128)(2,1)} %bitcast.303), calls=%async_computation | async-start | bytes 3145728 | tf_op jit(solution)/shard_map/all_to_all | solution.py:1249
  681.8 22.6 %collective-permute-start.122 = (bf16[256,1024]{1,0:T(8,128)(2,1)S(1)}, bf16[256,1024]{1,0:T(8,128)(2,1)S(1)}, u32[]{:S(2)}, u32[]{:S(2)}) collective-permute-start(bf16[256,1024]{1,0:T(8,128)(2,1)S(1)} %fusion.50), channel_id=1, source_target_pairs={{0,16},{16,0},{1,17},{17,1},{2,18},{18,2},{3,19},{19,3},{4,20},{20... | collective-permute-start | bytes 1572872 | tf_op jit(solution)/shard_map/ppermute | solution.py:249
  683.8 31.9 %collective-permute-start.120 = (bf16[256,1024]{1,0:T(8,128)(2,1)S(1)}, bf16[256,1024]{1,0:T(8,128)(2,1)S(1)}, u32[]{:S(2)}, u32[]{:S(2)}) collective-permute-start(bf16[256,1024]{1,0:T(8,128)(2,1)S(1)} %fusion.44), channel_id=1, source_target_pairs={{0,16},{16,0},{1,17},{17,1},{2,18},{18,2},{3,19},{19,3},{4,20},{20... | collective-permute-start | bytes 1572872 | tf_op jit(solution)/shard_map/ppermute | solution.py:249
  693.4 25.2 %collective-permute-start.125 = (bf16[2,256,1024]{2,1,0:T(8,128)(2,1)S(1)}, bf16[2,256,1024]{2,1,0:T(8,128)(2,1)S(1)}, u32[]{:S(2)}, u32[]{:S(2)}) collective-permute-start(bf16[2,256,1024]{2,1,0:T(8,128)(2,1)S(1)} %pad_maximum_fusion.9), channel_id=1, source_target_pairs={{0,8},{8,0},{1,9},{9,1},{2,10},{10,2},{3,11},{11,3},{4,12},{12,4},... | collective-permute-start | bytes 3145736 | tf_op jit(solution)/shard_map/ppermute | solution.py:249
  (167 other events, 2440.8 us)

commit v2 on v1

--- a/solution.py
+++ b/solution.py
@@ -26,7 +26,7 @@
 VMEM = pltpu.VMEM
 SMEM = pltpu.SMEM
 SWAP = [(0, 1), (1, 0)]
-TILE = 256
+TILE = 1024
 tie = lax.optimization_barrier
 VMEM_LIMIT = 56 * 1024 * 1024
 
@@ -96,8 +96,12 @@
         self.place = jnp.where(index % 2 == 0, index // 2, owners_count - 1 - index // 2)
         self.past = []
 
-    def start(self, *groups, after=()):
+    def start(self, *groups, after=(), beside=()):
         sends = [send for group in groups for send in group]
+        if sends and not after:
+            cells = [Cell(value) for value, route, take in sends]
+            bind(*cells, *beside)
+            sends = [(cell.value, *send[1:]) for cell, send in zip(cells, sends)]
         came = []
         for value, route, take in sends:
             if after:
@@ -151,31 +155,109 @@
 
 
 class Reduce:
-    def __init__(self, wires, part_of, turn):
-        self.wires, self.part_of = wires, part_of
+    def __init__(self, wires, matrices, depth, turn):
+        self.wires, self.depth = wires, depth
+        self.lead = matrices.shape[:-2]
+        self.flat = matrices.reshape((-1,) + matrices.shape[-2:])
         self.left = list(wires.reach(turn))
         self.moving = [None, None]
 
     def hop(self):
-        sends = []
-        for way, (route, sign) in enumerate((("onward", 1), ("back", -1))):
-            if self.left[way]:
-                value = self.part_of(self.wires.index_at(sign * self.left[way]))
-                if self.moving[way] is not None:
-                    value = value.astype(f32) + self.moving[way].value.astype(f32)
-
-                def take(cell, way=way):
-                    self.moving[way] = cell
-
-                sends.append((value.astype(bf16), route, take))
-                self.left[way] -= 1
-        return sends
+        return hop_together(self)
+
+    def arrived(self, way):
+        cell, first = self.moving[way]
+        return cell.value[first : first + self.flat.shape[0]]
 
     def total(self):
         while any(self.left):
             self.wires.slot(self.hop())
-        own = self.part_of(self.wires.index_at(0)).astype(f32)
-        return own + self.moving[0].value.astype(f32) + self.moving[1].value.astype(f32)
+        start = self.wires.index_at(0) * self.depth
+        own = lax.dynamic_slice_in_dim(self.flat, start, self.depth, 1).astype(f32)
+        total = own + self.arrived(0).astype(f32) + self.arrived(1).astype(f32)
+        return total.reshape(self.lead + total.shape[1:])
+
+
+def hop_kernel(plan, counts, starts, *refs):
+    n_in = counts[0]
+    outs = refs[n_in : n_in + counts[1]]
+    came, sems = refs[n_in + counts[1] : -1], refs[-1]
+    depth = outs[0].shape[1]
+    copies = []
+    for i, (way, place, panels, matrix, had, spot) in enumerate(plan):
+        row = pl.multiple_of(starts[i] * depth, depth)
+        out = outs[way].at[pl.ds(place, panels)]
+        copies.append(
+            pltpu.make_async_copy(refs[matrix].at[:, pl.ds(row, depth)], out, sems.at[2 * i])
+        )
+        if had is not None:
+            copies.append(
+                pltpu.make_async_copy(
+                    refs[had].at[pl.ds(spot, panels)],
+                    came[way].at[pl.ds(place, panels)],
+                    sems.at[2 * i + 1],
+                )
+            )
+    start_all(copies)
+    wait_all(copies)
+    for way, place, panels, matrix, had, spot in plan:
+        if had is not None:
+            for p in range(place, place + panels):
+                total = outs[way][p].astype(f32) + came[way][p].astype(f32)
+                outs[way][p] = total.astype(bf16)
+
+
+def hop_together(*sums):
+    wires, depth = sums[0].wires, sums[0].depth
+    columns = sums[0].flat.shape[-1]
+    arrays = [part.flat for part in sums]
+    cells, plan, starts, sends, sizes = [], [], [], [], []
+    for way, (route, sign) in enumerate((("onward", 1), ("back", -1))):
+        going = [i for i, part in enumerate(sums) if part.left[way]]
+        if not going:
+            continue
+        place = 0
+        places = []
+        for i in going:
+            part = sums[i]
+            had, spot = None, 0
+            if part.moving[way] is not None:
+                cell, spot = part.moving[way]
+                if all(cell is not c for c in cells):
+                    cells.append(cell)
+                had = len(arrays) + [cell is c for c in cells].index(True)
+            panels = part.flat.shape[0]
+            plan.append((len(sends), place, panels, i, had, spot))
+            starts.append(wires.index_at(sign * part.left[way]))
+            part.left[way] -= 1
+            places.append((part, place))
+            place += panels
+
+        def take(cell, way=way, places=places):
+            for part, first in places:
+                part.moving[way] = (cell, first)
+
+        sends.append((route, take))
+        sizes.append(place)
+    if not sends:
+        return []
+    inputs = arrays + [cell.value for cell in cells]
+    messages = pl.pallas_call(
+        functools.partial(hop_kernel, tuple(plan), (len(inputs), len(sizes))),
+        out_shape=[jax.ShapeDtypeStruct((n, depth, columns), bf16) for n in sizes],
+        in_specs=[pl.BlockSpec(memory_space=SMEM)] + [pl.BlockSpec(memory_space=ANY)] * len(inputs),
+        out_specs=[pl.BlockSpec(memory_space=VMEM)] * len(sizes),
+        scratch_shapes=[VMEM((n, depth, columns), bf16) for n in sizes]
+        + [pltpu.SemaphoreType.DMA((2 * len(plan),))],
+        compiler_params=pltpu.CompilerParams(vmem_limit_bytes=VMEM_LIMIT),
+        cost_estimate=pl.CostEstimate(
+            flops=sum(sizes) * depth * columns,
+            bytes_accessed=6 * sum(sizes) * depth * columns,
+            transcendentals=0,
+        ),
+        name="hop",
+    )(jnp.stack(starts).astype(jnp.int32), *inputs)
+    return [(message, *send) for message, send in zip(messages, sends)]
 
 
 class AllSum:
@@ -206,12 +288,13 @@
 
 
 class ChipSum:
-    def __init__(self, wires, blocks=None, here=None, there=None):
-        self.wires, self.blocks = wires, blocks
+    def __init__(self, wires, blocks=None, here=None, there=None, cuts=None):
+        self.wires, self.blocks, self.cuts = wires, blocks, cuts
         if blocks is not None and wires.outer == 2:
             index = lax.axis_index("o")
             here = lax.dynamic_index_in_dim(blocks, index, 0, keepdims=False)
-            there = [lax.dynamic_index_in_dim(blocks, 1 - index, 0, keepdims=False)]
+            there = lax.dynamic_index_in_dim(blocks, 1 - index, 0, keepdims=False)
+            there = [there] if cuts is None else [there[a:b] for a, b in cuts]
         self.here, self.there, self.came = here, list(there or []), []
 
     def send(self):
@@ -227,20 +310,15 @@
         while self.there:
             self.wires.slot(self.send())
         came = [cell.value for cell in self.came]
-        came = came[0] if len(came) == 1 else jnp.stack(came)
+        if len(came) > 1:
+            came = jnp.stack(came) if self.cuts is None else jnp.concatenate(came)
+        else:
+            came = came[0]
         return self.here.astype(f32) + came.astype(f32)
 
 
 def swap_cores(values):
     return lax.ppermute(values, "c", SWAP)
-
-
-def row_parts(depth, *matrices):
-    def part_of(index):
-        parts = [lax.dynamic_slice_in_dim(m, index * depth, depth, m.ndim - 2) for m in matrices]
-        return jnp.concatenate(parts, axis=-3) if len(parts) > 1 else parts[0]
-
-    return part_of
 
 
 def gather_blocks(values, name, count):
@@ -285,31 +363,35 @@
     )(source, grads)
 
 
-def load_share(mine, other, spots, depth, first, weights, sems):
+def load_share(sides, spots, first, weights, sems):
+    depth = sides[0][0].shape[1]
     copies = []
-    for i in range(len(mine)):
-        row = pl.multiple_of(spots[i] * depth, depth)
-        for side, pieces in enumerate((mine, other)):
+    for side, pieces in enumerate(sides):
+        for i, piece in enumerate(pieces):
+            row = pl.multiple_of(spots[i] * depth, depth)
             copies.append(
                 pltpu.make_async_copy(
-                    pieces[i].at[first],
-                    weights.at[2 * first + side, pl.ds(row, depth)],
+                    piece.at[first],
+                    weights.at[len(sides) * first + side, pl.ds(row, depth)],
                     sems.at[first, side, i],
                 )
             )
     return copies
 
 
-def ffn_forward_kernel(count, meta, normed, bias, *refs):
-    mine, other = refs[:count], refs[count : 2 * count]
-    hidden, active, branch, away, weights, sems = refs[2 * count :]
-    depth, width = mine[0].shape[1:]
-    tokens = branch.shape[0]
-    ins = load_share(mine, other, meta, depth, 0, weights, sems)
-    outs = load_share(mine, other, meta, depth, 1, weights, sems)
+def cut_sides(refs, count, halves):
+    return [refs[i * count : (i + 1) * count] for i in range(halves)], refs[halves * count :]
+
+
+def ffn_forward_kernel(count, halves, meta, normed, bias, *refs):
+    sides, refs = cut_sides(refs, count, halves)
+    hidden, active, branch, away, weights, sems = refs
+    tokens, width = branch.shape
+    ins = load_share(sides, meta, 0, weights, sems)
+    outs = load_share(sides, meta, 1, weights, sems)
     start_all(ins + outs)
     wait_all(ins)
-    for p in range(2):
+    for p in range(halves):
 
         @column_loop(width)
         def columns(cols):
@@ -321,19 +403,21 @@
 
     @column_loop(width)
     def out_columns(cols):
-        total = dot(active[0], weights[2, :, cols]) + dot(active[1], weights[3, :, cols])
+        total = dot(active[0], weights[halves, :, cols])
+        for p in range(1, halves):
+            total = total + dot(active[p], weights[halves + p, :, cols])
         branch[:, cols] = total[:tokens]
         away[:, cols] = total[tokens:].astype(bf16)
 
 
-def ffn_forward_call(normed, bias, mine, other, meta):
+def ffn_forward_call(normed, bias, sides, meta):
     tokens, width = normed.shape
-    count = len(mine)
+    count, halves = len(sides[0]), len(sides)
     return pl.pallas_call(
-        functools.partial(ffn_forward_kernel, count),
+        functools.partial(ffn_forward_kernel, count, halves),
         out_shape=[
-            jax.ShapeDtypeStruct((2, tokens, width), f32),
-            jax.ShapeDtypeStruct((2, tokens, width), bf16),
+            jax.ShapeDtypeStruct((halves, tokens, width), f32),
+            jax.ShapeDtypeStruct((halves, tokens, width), bf16),
             jax.ShapeDtypeStruct((tokens // 2, width), f32),
             jax.ShapeDtypeStruct((tokens // 2, width), bf16),
         ],
@@ -342,36 +426,36 @@
             pl.BlockSpec(memory_space=VMEM),
             pl.BlockSpec(memory_space=VMEM),
         ]
-        + [pl.BlockSpec(memory_space=ANY)] * (2 * count),
+        + [pl.BlockSpec(memory_space=ANY)] * (halves * count),
         out_specs=[pl.BlockSpec(memory_space=VMEM)] * 4,
         scratch_shapes=[
-            VMEM((4, width, width), bf16),
-            pltpu.SemaphoreType.DMA((2, 2, count)),
+            VMEM((2 * halves, width, width), bf16),
+            pltpu.SemaphoreType.DMA((2, halves, count)),
         ],
         compiler_params=pltpu.CompilerParams(vmem_limit_bytes=VMEM_LIMIT),
         cost_estimate=pl.CostEstimate(
-            flops=8 * tokens * width * width,
+            flops=4 * halves * tokens * width * width,
             bytes_accessed=8 * width * width + tokens * width * 18,
-            transcendentals=2 * tokens * width,
+            transcendentals=halves * tokens * width,
         ),
         name="ffn_forward",
-    )(meta, normed, bias, *mine, *other)
-
-
-def ffn_out_backward_kernel(count, bias, blocks, meta, hidden, active, grad, had, *refs):
-    mine, other = refs[:count], refs[count : 2 * count]
-    low, sums, *matrices, weights, sems = refs[2 * count :]
-    depth, width = mine[0].shape[1:]
+    )(meta, normed, bias, *[piece for pieces in sides for piece in pieces])
+
+
+def ffn_out_backward_kernel(count, halves, bias, blocks, meta, hidden, active, grad, had, *refs):
+    sides, refs = cut_sides(refs, count, halves)
+    low, sums, *matrices, weights, sems = refs
     outer, ways = blocks
+    width = low.shape[-1]
     parity, core = meta[count], meta[count + 1]
     store = share_store(ways, meta[count + 2], matrices)
     sums[...] = had[...]
-    copies = load_share(mine, other, meta, depth, 1, weights, sems)
+    copies = load_share(sides, meta, 1, weights, sems)
     start_all(copies)
-    for p in range(2):
-        put_blocks(store, p ^ parity, active.at[p], grad, outer)
+    for p in range(halves):
+        put_blocks(store, p ^ parity if halves == 2 else p, active.at[p], grad, outer)
     wait_all(copies)
-    for p in range(2):
+    for p in range(halves):
         row = bias + 2 * core + (p ^ parity)
 
         @column_loop(width)
@@ -379,28 +463,29 @@
             value = hidden[p, :, cols]
             share = jax.nn.sigmoid(value)
             slope = share * (1.0 + value * (1.0 - share))
-            part = (dot_nt(grad[...], weights[2 + p, cols, :]) * slope).astype(bf16)
+            part = (dot_nt(grad[...], weights[halves + p, cols, :]) * slope).astype(bf16)
             low[p, :, cols] = part
             sums[pl.ds(row, 1), cols] = jnp.sum(part.astype(f32), axis=0, keepdims=True)
 
 
-def ffn_in_backward_kernel(count, bias, blocks, meta, normed, low, *refs):
-    mine, other = refs[:count], refs[count : 2 * count]
-    normed_grad, away, *matrices, weights, sems = refs[2 * count :]
-    tokens = away.shape[0]
-    depth, width = mine[0].shape[1:]
+def ffn_in_backward_kernel(count, halves, bias, blocks, meta, normed, low, *refs):
+    sides, refs = cut_sides(refs, count, halves)
+    normed_grad, away, *matrices, weights, sems = refs
+    tokens, width = away.shape
     outer, ways = blocks
     parity = meta[count]
     store = share_store(ways, meta[count + 2], matrices)
-    copies = load_share(mine, other, meta, depth, 0, weights, sems)
+    copies = load_share(sides, meta, 0, weights, sems)
     start_all(copies)
-    for p in range(2):
-        put_blocks(store, p ^ parity, normed, low.at[p], outer)
+    for p in range(halves):
+        put_blocks(store, p ^ parity if halves == 2 else p, normed, low.at[p], outer)
     wait_all(copies)
 
     @column_loop(width)
     def back(cols):
-        total = dot_nt(low[0], weights[0, cols, :]) + dot_nt(low[1], weights[1, cols, :])
+        total = dot_nt(low[0], weights[0, cols, :])
+        for p in range(1, halves):
+            total = total + dot_nt(low[p], weights[p, cols, :])
         normed_grad[:, cols] = total[:tokens]
         away[:, cols] = total[tokens:].astype(bf16)
 
@@ -411,35 +496,35 @@
     return store_all(matrices[0])
 
 
-def ffn_backward_call(kernel, name, bias, outer, ways, meta, arrays, mine, other, outs):
-    width = mine[0].shape[-1]
+def ffn_backward_call(kernel, name, bias, outer, ways, meta, arrays, sides, outs):
+    width = sides[0][0].shape[-1]
     tokens = arrays[0].shape[-2]
-    count = len(mine)
+    count, halves = len(sides[0]), len(sides)
     quarter = width // (2 * outer)
     if ways:
         part = jax.ShapeDtypeStruct((2, width, quarter), bf16)
         blocks = [jax.ShapeDtypeStruct((2, 2, width, quarter), bf16), part, part]
     else:
-        blocks = [jax.ShapeDtypeStruct((outer, 2, 2, width, quarter), bf16)]
+        blocks = [jax.ShapeDtypeStruct((outer, 2, halves, width, quarter), bf16)]
     return pl.pallas_call(
-        functools.partial(kernel, count, bias, (outer, ways)),
+        functools.partial(kernel, count, halves, bias, (outer, ways)),
         out_shape=[*outs, *blocks],
         in_specs=[pl.BlockSpec(memory_space=SMEM)]
         + [pl.BlockSpec(memory_space=VMEM)] * len(arrays)
-        + [pl.BlockSpec(memory_space=ANY)] * (2 * count),
+        + [pl.BlockSpec(memory_space=ANY)] * (halves * count),
         out_specs=[pl.BlockSpec(memory_space=VMEM)] * (len(outs) + len(blocks)),
         scratch_shapes=[
-            VMEM((4, width, width), bf16),
-            pltpu.SemaphoreType.DMA((2, 2, count)),
+            VMEM((2 * halves, width, width), bf16),
+            pltpu.SemaphoreType.DMA((2, halves, count)),
         ],
         compiler_params=pltpu.CompilerParams(vmem_limit_bytes=VMEM_LIMIT),
         cost_estimate=pl.CostEstimate(
-            flops=8 * tokens * width * width,
+            flops=4 * halves * tokens * width * width,
             bytes_accessed=8 * width * width + tokens * width * 16,
             transcendentals=tokens * width,
         ),
         name=name,
-    )(meta, *arrays, *mine, *other)
+    )(meta, *arrays, *[piece for pieces in sides for piece in pieces])
 
 
 def norm_parts(values):
@@ -487,9 +572,8 @@
 
 def column_loop(width):
     def run(body):
-        @pl.loop(0, width // TILE)
-        def step(j):
-            body(pl.ds(pl.multiple_of(j * TILE, TILE), TILE))
+        for start in range(0, width, TILE):
+            body(slice(start, start + TILE))
 
     return run
 
@@ -868,15 +952,14 @@
     shape = jax.ShapeDtypeStruct
 
     def chip_share(first, side):
-        panel = 2 * core + side
-        ins = lax.dynamic_slice_in_dim(panels, first + panel, 1, 0)
-        outs = lax.dynamic_slice_in_dim(panels, first + 4 + panel, 1, 0)
+        panel = first + 2 * core + side
+        ins = lax.dynamic_slice_in_dim(panels, panel, 1, 0)
+        outs = lax.dynamic_slice_in_dim(panels, panel + 4, 1, 0)
         return jnp.concatenate([ins, outs], axis=0)
 
     first = Gather(wires, chip_share(0, parity), 0)
-    middle = Gather(wires, lax.dynamic_slice_in_dim(panels[8:15], core * half, half, 2), 1)
+    middle = Gather(wires, lax.dynamic_slice(panels, (8, 0, core * half), (7, depth, half)), 1)
     second = Gather(wires, chip_share(15, parity), 0)
-    first_other = [Cell(chip_share(0, 1 - parity))]
     second_other = [Cell(chip_share(15, 1 - parity))]
     middle_other = []
 
@@ -892,8 +975,7 @@
                 most -= 1
             return sends
 
-    to_chip = Passing(first, "chip", first_other, 1)
-    to_chip_too = Passing(second, "chip", second_other, 1)
+    to_chip = Passing(second, "chip", second_other, 1)
     to_core = Passing(middle, "core", middle_other, 0)
     slot = wires.slot
 
@@ -913,46 +995,63 @@
 
     left = Cell(basis_left.astype(bf16))
     right = Cell(basis_right.astype(bf16))
+    def exchange(values):
+        return lax.ppermute(values, "o", wires.routes["chip"][1])
+
+    def all_four(own, came):
+        mine = jnp.concatenate([own, came])
+        return jnp.concatenate([mine, swap_cores(mine)])
+
+    def sum_four(mine, away):
+        total = mine + swap_cores(away).astype(f32)
+        return total[:tokens], total[tokens:].astype(bf16)
+
     start = Cell(frames.reshape(tokens, width).astype(f32))
-    normed = Cell(
-        both_cores(layer_norm(start.value, vectors[0], vectors[1]).astype(bf16))
-    )
-    bias_first, bias_second = Cell(core_rows(12)), Cell(core_rows(17))
-    ready = [start, normed, bias_first, bias_second, *first_other, *second_other]
-    came = slot(first.hop(), to_core.more())
+    own_first = layer_norm(start.value, vectors[0], vectors[1]).astype(bf16)
+    bias_first, bias_second = Cell(core_rows(12)[:1]), Cell(core_rows(17))
+    ready = [start, bias_first, bias_second, *second_other]
+    far_first = []
+    came = slot(first.hop(), [(own_first, "chip", far_first.append)])
     bind(*ready, *came)
+    slot(middle.hop(), to_core.more())
+    normed = Cell(all_four(own_first, far_first[0].value))
+    slot(first.hop())
+    bind(normed, *wires.past[-2])
+    slot(second.hop(), to_core.more(2))
     slot(first.hop(), to_chip.more())
-    slot(middle.hop(), to_chip.more(2))
-    slot(first.hop(), to_chip.more(), to_core.more(2))
-    slot(second.hop(), to_chip.more())
-    slot(first.hop(), to_chip.more())
-    came = slot(middle.hop(), to_chip.more(), to_chip_too.more())
+    came = slot(middle.hop(), to_chip.more())
     bind(left, right, *wires.past[-2])
+    came = slot(first.hop())
     while any(first.left):
         came = slot(first.hop())
-    while to_chip.next < len(first.pieces):
-        came = slot(to_chip.more(2))
-    came = slot(second.hop(), to_chip_too.more(), to_core.more(2))
-    bind(normed, *wires.past[-2])
-    slot(middle.hop(), to_chip_too.more(2))
+    slot(second.hop(), to_core.more(2))
+    bind(normed, *came)
+    slot(middle.hop(), to_chip.more())
     hidden, active, mine, away = ffn_forward_call(
-        normed.value, bias_first.value, values(first.pieces), values(first_other),
-        meta_of(first, parity),
-    )
+        normed.value, bias_first.value, [values(first.pieces)], meta_of(first, parity)
+    )
+    own, far = sum_four(mine, away)
+    own, far = Cell(own), Cell(far)
+    kept_first = (normed.value, hidden, active)
+    bind(own, far, *wires.past[-1], *wires.past[-2])
+    far_came = []
+    slot(second.hop(), to_chip.more(), [(far.value, "chip", far_came.append)])
+    slot(middle.hop(), to_chip.more(), to_core.more(2))
+    slot(second.hop(), to_chip.more())
+    while any(middle.left) or any(second.left):
+        slot(middle.hop(), second.hop(), to_chip.more(2), to_core.more(2))
     after_first = Cell(
-        start.value + 0.5 * (mine + swap_cores(away).astype(f32) + vectors[16])
-    )
-    kept_first = (normed.value, hidden, active)
-    bind(after_first, *wires.past[-1], *wires.past[-2])
-    slot(second.hop(), to_core.more(2))
-    slot(middle.hop(), second.hop(), to_chip_too.more(2))
-    while any(middle.left) or any(second.left):
-        slot(middle.hop(), second.hop(), to_chip_too.more(2), to_core.more(2))
-    came = wires.start(to_core.more(2), to_chip_too.more(), after=wires.past[-1])
+        start.value + 0.5 * (own.value + far_came[0].value.astype(f32) + vectors[16])
+    )
+    came = wires.start(to_core.more(2), to_chip.more(), after=wires.past[-1])
     while to_core.next < len(middle.pieces):
         came += slot(to_core.more(2))
     middle_meta = meta_of(middle, core, lengths[0])
-    bind(after_first, *wires.past[-1])
+
+    def sides_of(gather, other):
+        return [values(gather.pieces)] + ([values(other)] if other else [])
+
+    bind(after_first, *[cell for past in wires.past[-4:] for cell in past])
     after_attn, attn_normed, queries, keys, values_, mixed = panel_call(
         attention_forward_kernel,
         "attention_forward",
@@ -968,8 +1067,8 @@
     after_attn = Cell(after_attn)
     bind(after_attn, *came)
     came = []
-    while to_chip_too.next < len(second.pieces):
-        came += wires.start(to_chip_too.more(2), after=[after_attn])
+    while to_chip.next < len(second.pieces):
+        came += wires.start(to_chip.more(2), after=[after_attn])
     after_conv, conv_normed, wide, conv_active = panel_call(
         conv_forward_kernel,
         "conv_forward",
@@ -984,16 +1083,15 @@
     )
     normed = both_cores(layer_norm(after_conv, vectors[8], vectors[9]).astype(bf16))
     hidden, active, mine, away = ffn_forward_call(
-        normed, bias_second.value, values(second.pieces), values(second_other),
-        meta_of(second, parity),
+        normed, bias_second.value, sides_of(second, second_other), meta_of(second, parity)
     )
     kept_second = (normed, hidden, active)
     layer_out, grad_flow, half_low, sums = turn_call(
         lengths, after_conv, mine, swap_cores(away), cotangent.reshape(tokens, width), vectors
     )
 
-    def ring_of(turn, *matrices):
-        return Reduce(wires, row_parts(depth, *matrices), turn)
+    def ring_of(turn, matrices):
+        return Reduce(wires, matrices, depth, turn)
 
     class Share:
         def __init__(self, here, there):
@@ -1019,7 +1117,7 @@
     chip = lax.axis_index("o")
     pairs = outer == 2
 
-    def ffn_backward_out(half_low, gather, other, kept, bias, sums, ways):
+    def ffn_backward_out(both_low, gather, other, kept, bias, sums, ways):
         normed, hidden, active = kept
         return ffn_backward_call(
             ffn_out_backward_kernel,
@@ -1028,10 +1126,9 @@
             outer,
             ways,
             meta_of(gather, parity, core, chip),
-            [hidden, active, both_cores(half_low), sums],
-            values(gather.pieces),
-            values(other),
-            [shape((2, 2 * tokens, width), bf16), shape(vectors.shape, f32)],
+            [hidden, active, both_low, sums],
+            sides_of(gather, other),
+            [shape(active.shape, bf16), shape(vectors.shape, f32)],
         )
 
     def ffn_backward_in(low, gather, other, kept, ways):
@@ -1043,9 +1140,11 @@
             ways,
             meta_of(gather, parity, core, chip),
             [kept[0], low],
-            values(gather.pieces),
-            values(other),
-            [shape((tokens, width), f32), shape((tokens, width), bf16)],
+            sides_of(gather, other),
+            [
+                shape((kept[0].shape[0] // 2, width), f32),
+                shape((kept[0].shape[0] // 2, width), bf16),
+            ],
         )
 
     def middle_call(kernel, name, used, arrays, outs, scratch, flops):
@@ -1071,14 +1170,17 @@
                 self.chips = ChipSum(wires, here=matrices[0], there=matrices[1:])
             else:
                 self.chips = None
-                self.ring = ring_of(turn, *matrices)
+                self.ring = ring_of(turn, matrices[0])
 
         def send(self):
-            return self.chips.send()
-
-        def hop(self):
+            return self.chips.send() if self.chips is not None and not hasattr(self, "late") else []
+
+        def ready(self):
             if self.ring is None:
                 self.ring = ring_of(self.turn, self.chips.total().astype(bf16))
+
+        def hop(self):
+            self.ready()
             return self.ring.hop()
 
         def finish(self):
@@ -1095,20 +1197,18 @@
 
     begin = wires.start
     low, sums, *matrices = ffn_backward_out(
-        half_low, second, second_other, kept_second, 17, sums, False
+        both_cores(half_low), second, second_other, kept_second, 17, sums, False
     )
     second_out = Part(matrices, 0)
     low = Cell(low)
-    came = begin(second_out.hop(), after=[low])
-    mine, away, *matrices = ffn_backward_in(
-        low.value, second, second_other, kept_second, pairs
-    )
-    mine = Cell(mine)
-    bind(mine, *came)
+    came = begin(second_out.hop(), beside=[low])
+    mine, away, *matrices = ffn_backward_in(low.value, second, second_other, kept_second, pairs)
+    mine, away = Cell(mine), Cell(away)
+    bind(mine, away, *came)
     second_in = Part(matrices, 1)
-    came = begin(second_out.hop(), second_in.send() if pairs else [], after=[mine])
+    came = begin(second_out.hop(), second_in.send(), beside=[mine, away])
     grad_flow, sums = pull_call(
-        8, grad_flow, after_conv, mine.value, swap_cores(away), vectors, sums, f32
+        8, grad_flow, after_conv, mine.value, swap_cores(away.value), vectors, sums, f32
     )
     lows, here, there, sums = middle_call(
         conv_out_backward_kernel,
@@ -1120,11 +1220,9 @@
         4,
     )
     lows = Cell(lows)
+    conv_out = Share(here, there)
     bind(lows, *came)
-    conv_out = Share(here, there)
-    came = begin(
-        second_out.hop(), second_in.send() if pairs else [], conv_out.hop(), after=[lows]
-    )
+    came = begin(second_out.hop(), second_in.send(), conv_out.hop(), beside=[lows])
     flow, here, there, sums = middle_call(
         conv_in_backward_kernel,
         "conv_in_backward",
@@ -1146,10 +1244,14 @@
         6,
     )
     lows = Cell(lows)
+    attn_out = Share(here, there)
     bind(lows, *came)
-    attn_out = Share(here, there)
+    second_in.ready()
     came = begin(
-        second_out.hop(), second_in.hop(), conv_in.hop(), attn_out.hop(), after=[lows]
+        hop_together(second_out.ring, second_in.ring),
+        conv_in.hop(),
+        attn_out.hop(),
+        beside=[lows],
     )
     flow.value, here, there, sums, half_low = middle_call(
         attention_in_backward_kernel,
@@ -1160,63 +1262,88 @@
         [VMEM((tokens, width), f32)],
         12,
     )
+    attn_in = Share(here, there)
     half_low = Cell(half_low)
     bind(half_low, *came)
-    attn_in = Share(here, there)
-    conv_part = ring_of(0, conv_in.total(), conv_out.total())
+    conv_total = jnp.concatenate([conv_in.total(), conv_out.total()], axis=1)
+    if pairs:
+        conv_chips = ChipSum(wires, blocks=conv_total, cuts=[(0, 2), (2, 3)])
+    else:
+        conv_part = ring_of(0, conv_total)
+    far_low = []
     came = begin(
-        conv_part.hop(), second_in.hop(), attn_in.hop(), second_out.finish(), after=[half_low]
-    )
+        second_in.hop(),
+        attn_in.hop(),
+        [(half_low.value, "chip", far_low.append)],
+        beside=[half_low],
+    )
+    both_low = Cell(all_four(half_low.value, far_low[0].value))
     low, sums, *matrices = ffn_backward_out(
-        half_low.value, first, first_other, kept_first, 12, sums, pairs
-    )
-    first_out = Part(matrices, 1)
+        both_low.value, first, [], kept_first, 12, sums, False
+    )
+    first_out = ring_of(0, matrices[0])
     low = Cell(low)
     bind(low, *came)
-    attn_in_total, attn_out_total = attn_in.total(), attn_out.total()
+    attn_part = ring_of(1, jnp.concatenate([attn_in.total(), attn_out.total()], axis=1))
+    conv_sends = conv_chips.send() if pairs else []
+    came = begin(hop_together(second_in.ring, attn_part, first_out), conv_sends, beside=[low])
+    mine, away, *matrices = ffn_backward_in(low.value, first, [], kept_first, False)
+    first_in = ring_of(0, matrices[0])
+    own, far = sum_four(mine, away)
+    own, far = Cell(own), Cell(far)
+    bind(own, far, *came)
+    conv_sends = conv_chips.send() if pairs else []
+    far_came = []
+    came = begin(
+        hop_together(second_in.ring, attn_part, first_out, first_in),
+        conv_sends,
+        [(far.value, "chip", far_came.append)],
+        beside=[own],
+    )
+    bind(*came)
     if pairs:
-        attn_chips = ChipSum(
-            wires, blocks=jnp.concatenate([attn_in_total, attn_out_total], axis=1)
-        )
-        attn_sends = attn_chips.send()
-    else:
-        attn_part, attn_sends = ring_of(1, attn_in_total, attn_out_total), []
-    came = begin(conv_part.hop(), second_in.hop(), attn_sends, after=[low])
-    mine, away, *matrices = ffn_backward_in(low.value, first, first_other, kept_first, False)
-    first_in = Part(matrices, 0)
-    mine = Cell(mine)
-    bind(mine, *came)
-    wires.past = [came]
-    slot(first_in.hop(), conv_part.hop(), first_out.send() if pairs else [])
+        conv_part = ring_of(1, conv_chips.total().astype(bf16))
+    came = begin(hop_together(attn_part, first_out, first_in, conv_part), second_out.finish())
     frames_grad, sums = pull_call(
-        0, flow.value, start.value, mine.value, swap_cores(away), vectors, sums, bf16
+        0, flow.value, start.value, own.value, far_came[0].value, vectors, sums, bf16
     )
     frames_grad, sums = Cell(frames_grad), Cell(sums)
-    bind(sums, frames_grad, *came)
     vector_sum = AllSum(wires, sums.value)
-    if pairs:
-        attn_part = ring_of(1, attn_chips.total().astype(bf16))
-    slot(first_in.hop(), attn_part.hop(), first_out.send() if pairs else [], vector_sum.hop())
-    slot(first_in.hop(), conv_part.hop(), second_in.hop(), vector_sum.hop())
-    slot(first_in.hop(), attn_part.hop(), vector_sum.hop())
-    conv_chips = ChipSum(wires, blocks=conv_part.total())
-    slot(attn_part.hop(), first_out.hop(), conv_chips.send(), vector_sum.hop())
-    slot(attn_part.hop(), first_out.hop(), first_in.finish(), vector_sum.hop())
-    early = [trade_cores(second_in.total()), trade_cores(second_out.total()), conv_chips.total()]
+    bind(vector_sum.value, frames_grad, *came)
+    came = begin(hop_together(attn_part, first_out, first_in, conv_part))
+    bind(*came)
+    attn_chips = ChipSum(wires, blocks=attn_part.total())
+    came = begin(hop_together(first_out, first_in, conv_part), attn_chips.send())
+    bind(*came)
+    came = begin(hop_together(first_in, conv_part))
+    bind(*came)
+    conv_total = conv_part.total()
+    if not pairs:
+        conv_total = ChipSum(wires, blocks=conv_total).total()
+
+    def spread(mine):
+        if not pairs:
+            big = jnp.zeros((outer, 2, 2, 2) + mine.shape[2:], f32)
+            at = (lax.broadcasted_iota(jnp.int32, (1, 1, 2, 2, 1, 1, 1), 2) == core) & (
+                lax.broadcasted_iota(jnp.int32, (1, 1, 2, 2, 1, 1, 1), 3) == parity
+            )
+            big = jnp.where(at, mine[:, :, None, None], big).astype(bf16)
+            big = big.reshape((outer * 2,) + big.shape[2:])
+            return lax.psum_scatter(big, ("o", "c"), scatter_dimension=0, tiled=True)[0].astype(f32)
+        low = trade_blocks(mine.astype(bf16), "o", outer)
+        low = trade_blocks(low.transpose(1, 0, 2, 3, 4), "c", 2)
+        return low.astype(f32)
+
+    first_sum = spread(jnp.concatenate([first_in.total(), first_out.total()], axis=2))
+    first_sum = [first_sum[:, :, kind].reshape(4, depth, quarter) for kind in range(2)]
+    early = [trade_cores(second_in.total()), trade_cores(second_out.total()), conv_total]
     early = [Cell(part) for part in early]
-    slot(first_out.hop())
-    slot(first_out.hop())
-    late = [trade_cores(first_in.total()), attn_part.total()]
-    if not pairs:
-        late[1] = ChipSum(wires, blocks=late[1]).total()
-    late = [Cell(part) for part in late]
-    vector_grads = Cell(vector_sum.total())
-    bind(vector_grads, *early, *late, *wires.past[-2])
-    vector_grads = vector_grads.value
+    late = [Cell(first_sum[0]), Cell(attn_chips.total()), Cell(first_sum[1])]
+    bind(*early, *late)
     panel_grads = jnp.concatenate(
         [
             late[0].value,
-            trade_cores(first_out.total()),
+            late[2].value,
             late[1].value,
             early[2].value,
             early[0].value,
@@ -1224,12 +1351,8 @@
         ],
         axis=0,
     )
-    vector_first_new = beta_one * vector_first + (1.0 - beta_one) * vector_grads
-    vector_second_new = beta_two * vector_second + (1.0 - beta_two) * vector_grads * vector_grads
-    vectors_new = vectors - vector_rate * adam_step(vector_first_new, vector_second_new)
     panel_grads = Cell(panel_grads)
-    updated = [Cell(vector_first_new), Cell(vector_second_new), Cell(vectors_new)]
-    bind(panel_grads, frames_grad, *updated)
+    bind(panel_grads, vector_sum.value, frames_grad)
     panel_grads = panel_grads.value
 
     slot_count = panel_first.shape[1]
@@ -1249,29 +1372,46 @@
     incoming = lax.all_to_all(outgoing, "f", split_axis=0, concat_axis=0, tiled=True)
     block = lax.axis_index("o") * 2 + core
     left_rows = lax.dynamic_slice_in_dim(left.value, block * quarter, quarter, 1)
-    results = []
+    incoming = Cell(incoming)
+    last = None
+    while vector_sum.todo:
+        last = begin(vector_sum.hop())
+        if len(vector_sum.todo) == 2:
+            bind(incoming, *last)
+    vector_grads = vector_sum.total()
+    vector_first_new = beta_one * vector_first + (1.0 - beta_one) * vector_grads
+    vector_second_new = beta_two * vector_second + (1.0 - beta_two) * vector_grads * vector_grads
+    vectors_new = vectors - vector_rate * adam_step(vector_first_new, vector_second_new)
+    updated = [Cell(vector_first_new), Cell(vector_second_new), Cell(vectors_new)]
+
+    traded = []
     for s in range(slot_count):
-        turned = dot_tn(left.value[s], incoming[:, s].reshape(width, quarter)).astype(bf16)
-        turned = trade_blocks(turned.reshape(outer, 2 * quarter, quarter), "o", outer)
-        turned = turned.reshape(outer, 2, quarter, quarter).transpose(1, 0, 2, 3)
+        turned = dot_tn(left.value[s], incoming.value[:, s].reshape(width, quarter)).astype(bf16)
+        turned = turned.reshape(outer, 2 * quarter, quarter)
+        traded.append(Cell(trade_blocks(turned, "o", outer)))
+    backs, firsts, seconds = [], [], []
+    for s in range(slot_count):
+        if s:
+            bind(traded[s], backs[-1])
+        turned = traded[s].value.reshape(outer, 2, quarter, quarter).transpose(1, 0, 2, 3)
         turned = trade_blocks(turned, "c", 2)
         turned = turned.transpose(2, 1, 0, 3).reshape(quarter, width)
         rotated = dot(turned, right.value[s])
         first_new = beta_one * panel_first[:, s] + (1.0 - beta_one) * rotated
         second_new = beta_two * panel_second[:, s] + (1.0 - beta_two) * rotated * rotated
         step_values = adam_step(first_new, second_new).astype(bf16)
-        back_turn = dot_nt(step_values, right.value[s]).astype(bf16)
-        back_turn = gather_blocks(back_turn, "o", outer)
+        back_turn = Cell(dot_nt(step_values, right.value[s]).astype(bf16))
+        firsts.append(jnp.where(mine[s], first_new, 0.0))
+        seconds.append(jnp.where(mine[s], second_new, 0.0))
+        backs.append(back_turn)
+    masters = []
+    for s in range(slot_count):
+        back_turn = gather_blocks(backs[s].value, "o", outer)
         back_turn = gather_blocks(back_turn, "c", 2)
         back_turn = back_turn.transpose(1, 0, 2, 3).reshape(width, width)
         update = dot(left_rows[s], back_turn)
-        results.append(
-            (
-                jnp.where(mine[s], first_new, 0.0),
-                jnp.where(mine[s], second_new, 0.0),
-                jnp.where(mine[s], panel_master[:, s] - learn_rate * update, 0.0),
-            )
-        )
+        masters.append(jnp.where(mine[s], panel_master[:, s] - learn_rate * update, 0.0))
+    results = list(zip(firsts, seconds, masters))
     first_new, second_new, master_new = [jnp.stack(part, axis=1) for part in zip(*results)]
     return (
         layer_out.reshape(frames.shape),

time: 741 us -> 716 us (0.966)
  starting transfers between devices: 162 us -> 129 us
  Pallas kernels: 159 us -> 167 us
    ppermute x102 -> x76, waiting for transfers between devices: 188 us -> 219 us  [start(): came.append(Cell(lax.ppermute(value, axis, pairs)))]
    pallas_call x6 -> x17, Pallas kernels: 77.5 us -> 99.8 us  [the longest x4 42.9 us: ffn_backward_call(): pl.pallas_call(functools.partial(kernel, count, halves, bias, (outer, way...]
    all_to_all x1, waiting for transfers between devices: 35.7 us -> 17.6 us  [on_device(): lax.all_to_all(outgoing, 'f', split_axis=0, concat_axis=0, tiled=True)]
    convert_element_type x25 -> x4, other arithmetic: 23.9 us -> 6.08 us  [the longest x1 2.89 us: on_device(): conv_part = ring_of(1, conv_chips.total().astype(bf16))]
    ppermute x102 -> x76, starting transfers between devices: 102 us -> 84.5 us  [start(): came.append(Cell(lax.ppermute(value, axis, pairs)))]
    ppermute x6, waiting for transfers between devices: 22.6 us -> 7.24 us  [gather_blocks(): other = lax.ppermute(values, name, SWAP)]
    ppermute x12 -> x10, starting transfers between devices: 36.7 us -> 21.5 us  [swap_cores(): return lax.ppermute(values, 'c', SWAP)]
    pallas_call x6, Pallas kernels: 66 us -> 52.2 us  [panel_call(): pl.pallas_call(functools.partial(kernel, count), out_shape=outs, in_specs...]
  transfers between devices with their start and end apart: 127 -> 101, of which waited for: 46 -> 49; matrix products, arithmetic and copies ran while one was open for 14% -> 14% of each run, Pallas kernels for 16% -> 12%
where the time goes in v2:
time: 716 us; the launch traced here: 706 us
  waiting for transfers between devices  256 us (36%)
  Pallas kernels  167 us (23%)
  starting transfers between devices  129 us (18%)
  other arithmetic  86.2 us (12%)
  local copies, waits for them, and re-layouts  34.5 us (5%)
  matrix products  30.3 us (4%)
    ppermute x76, waiting for transfers between devices, start(): came.append(Cell(lax.ppermute(value, axis, pairs)))  219 us
    ppermute x76, starting transfers between devices, start(): came.append(Cell(lax.ppermute(value, axis, pairs)))  84.5 us
    pallas_call x6, Pallas kernels, panel_call(): pl.pallas_call(functools.partial(kernel, count), out_shape=outs, in_specs...  52.2 us
    pallas_call x4, Pallas kernels, ffn_backward_call(): pl.pallas_call(functools.partial(kernel, count, halves, bias, (outer, way...  42.9 us
    pallas_call x11, Pallas kernels, hop_together(): pl.pallas_call(functools.partial(hop_kernel, tuple(plan), (len(inputs), l...  37.9 us
    ppermute x10, starting transfers between devices, swap_cores(): return lax.ppermute(values, 'c', SWAP)  21.5 us
    pallas_call x2, Pallas kernels, ffn_forward_call(): pl.pallas_call(functools.partial(ffn_forward_kernel, count, halves), out_...  19 us
    all_to_all x1, waiting for transfers between devices, on_device(): lax.all_to_all(outgoing, 'f', split_axis=0, concat_axis=0, tiled=True)  17.6 us
  transfers between devices with their start and end apart: 101, of which 49 were waited for; matrix products, arithmetic and copies ran while one was open for 14% of the time, Pallas kernels for 12%

profile of v2, /device:TPU:1, one launch (start us, length us, event | category | flops | bytes accessed | tf_op | source)
XLA Modules:
  0.0 706.3 jit_solution(3173840778029110835)
XLA Ops:
  15.8 7.5 %collective-permute-done.refs_1_ = bf16[2,128,1024]{2,1,0:T(8,128)(2,1)S(1)} collective-permute-done((bf16[2,128,1024]{2,1,0:T(8,128)(2,1)S(1)}, bf16[2,128,1024]{2,1,0:T(8,128)(2,1)S(1)}, u32[]{:S(2)}, u32[]{:S(2)}) %collective-permute-start) | collective-permute-done | bytes 524320 | tf_op jit(solution)/shard_map/ppermute | solution.py:110
  34.7 15.8 %collective-permute-done.4.refs_1_ = bf16[7,128,512]{2,1,0:T(8,128)(2,1)S(1)} collective-permute-done((bf16[7,128,512]{2,1,0:T(8,128)(2,1)S(1)}, bf16[7,128,512]{2,1,0:T(8,128)(2,1)S(1)}, u32[]{:S(2)}, u32[]{:S(2)}) %collective-permute-start.4) | collective-permute-done | bytes 917536 | tf_op jit(solution)/shard_map/ppermute | solution.py:110
  52.9 8.8 %collective-permute-done.7.refs_3_ = bf16[2,128,1024]{2,1,0:T(8,128)(2,1)S(1)} collective-permute-done((bf16[2,128,1024]{2,1,0:T(8,128)(2,1)}, bf16[2,128,1024]{2,1,0:T(8,128)(2,1)S(1)}, u32[]{:S(2)}, u32[]{:S(2)}) %collective-permute-start.7) | collective-permute-done | bytes 524320 | tf_op jit(solution)/shard_map/ppermute | solution.py:110
  65.6 7.3 %collective-permute-done.11.refs_1_ = bf16[2,128,1024]{2,1,0:T(8,128)(2,1)S(1)} collective-permute-done((bf16[2,128,1024]{2,1,0:T(8,128)(2,1)S(1)}, bf16[2,128,1024]{2,1,0:T(8,128)(2,1)S(1)}, u32[]{:S(2)}, u32[]{:S(2)}) %collective-permute-start.11) | collective-permute-done | bytes 524320 | tf_op jit(solution)/shard_map/ppermute | solution.py:110
  75.4 8.3 %convert_element_type.217 = bf16[3,1024,1024]{2,1,0:T(8,128)(2,1)} convert(f32[3,1024,1024]{2,1,0:T(8,128)} %param.21) | non-fusion elementwise | flops 3145728 | bytes 18874368 | tf_op jit(solution)/shard_map/convert_element_type | solution.py:996
  83.7 8.2 %convert_element_type.218 = bf16[3,1024,1024]{2,1,0:T(8,128)(2,1)} convert(f32[3,1024,1024]{2,1,0:T(8,128)} %param.22) | non-fusion elementwise | flops 3145728 | bytes 18874368 | tf_op jit(solution)/shard_map/convert_element_type | solution.py:997
  97.4 6.2 collective-permute-done.13.refs_7_
  103.5 9.5 %ffn_forward.2 = (f32[1,1024,1024]{2,1,0:T(8,128)}, bf16[1,1024,1024]{2,1,0:T(8,128)(2,1)}, f32[512,1024]{1,0:T(8,128)}, bf16[512,1024]{1,0:T(8,128)(2,1)}) custom-call(s32[9]{0:T(128)} %concatenate.74.meta, bf16[1024,1024]{1,0:T(8,128)(2,1)} %pad_maximum_fusion.4.normed, f32[1,1,1024]{2,1,0:T(1,128)} %get-tuple-element.284.bias, ...), custom_call_target="tpu_custom_call" | custom-call | flops 4294967296 | bytes 27262976 | tf_op jit(solution)/shard_map/ffn_forward/pallas_call | solution.py:416
  113.0 5.9 collective-permute-start.14
  128.3 5.4 collective-permute-done.25.refs_4_
  139.3 13.3 %collective-permute-done.21.refs_6_ = bf16[7,128,512]{2,1,0:T(8,128)(2,1)S(1)} collective-permute-done((bf16[7,128,512]{2,1,0:T(8,128)(2,1)}, bf16[7,128,512]{2,1,0:T(8,128)(2,1)S(1)}, u32[]{:S(2)}, u32[]{:S(2)}) %collective-permute-start.21) | collective-permute-done | bytes 917536 | tf_op jit(solution)/shard_map/ppermute | solution.py:110
  157.4 6.0 collective-permute-done.30.refs_6_
  163.9 9.7 %collective-permute-done.28 = bf16[256,1024]{1,0:T(8,128)(2,1)S(1)} collective-permute-done((bf16[256,1024]{1,0:T(8,128)(2,1)S(1)}, bf16[256,1024]{1,0:T(8,128)(2,1)S(1)}, u32[]{:S(2)}, u32[]{:S(2)}) %collective-permute-start.28) | collective-permute-done | bytes 524320 | tf_op jit(solution)/shard_map/ppermute | solution.py:110
  174.3 11.6 %collective-permute-start.35 = (bf16[7,128,512]{2,1,0:T(8,128)(2,1)S(1)}, bf16[7,128,512]{2,1,0:T(8,128)(2,1)}, u32[]{:S(2)}, u32[]{:S(2)}) collective-permute-start(bf16[7,128,512]{2,1,0:T(8,128)(2,1)S(1)} %collective-permute-done.21.refs_6_), channel_id=1, source_target_pairs={{0,8},{8,0},{1,9},{9,1},{2,10},{10,2},{3,11},{11,3},{4,12},{12,4},... | collective-permute-start | bytes 2752520 | tf_op jit(solution)/shard_map/ppermute | solution.py:110
  186.7 8.2 %collective-permute-start.38 = (bf16[7,128,512]{2,1,0:T(8,128)(2,1)}, bf16[7,128,512]{2,1,0:T(8,128)(2,1)}, u32[]{:S(2)}, u32[]{:S(2)}) collective-permute-start(bf16[7,128,512]{2,1,0:T(8,128)(2,1)} %collective-permute-done.32.refs_7_), channel_id=1, source_target_pairs={{0,8},{8,0},{1,9},{9,1},{2,10},{10,2},{3,11},{11,3},{4,12},{12,4},... | collective-permute-start | bytes 2752520 | tf_op jit(solution)/shard_map/ppermute | solution.py:110
  200.6 8.2 %collective-permute-done.33.refs_13_ = bf16[2,128,1024]{2,1,0:T(8,128)(2,1)} collective-permute-done((bf16[2,128,1024]{2,1,0:T(8,128)(2,1)}, bf16[2,128,1024]{2,1,0:T(8,128)(2,1)}, u32[]{:S(2)}, u32[]{:S(2)}) %collective-permute-start.33) | collective-permute-done | bytes 524320 | tf_op jit(solution)/shard_map/ppermute | solution.py:110
  208.8 9.5 %attention_forward.1 = (f32[256,1024]{1,0:T(8,128)}, bf16[256,1024]{1,0:T(8,128)(2,1)}, bf16[256,1024]{1,0:T(8,128)(2,1)}, bf16[256,1024]{1,0:T(8,128)(2,1)}, bf...) custom-call(s32[10]{0:T(128)} %concatenate.71.meta, f32[256,1024]{1,0:T(8,128)} %multiply_add_fusion.3.stream, ...), custom_call_target="tpu_custom_call" | custom-call | flops 2147483648 | bytes 16777216 | tf_op jit(solution)/shard_map/attention_forward/pallas_call | solution.py:903
  220.1 8.0 %conv_forward.1 = (f32[256,1024]{1,0:T(8,128)}, bf16[256,1024]{1,0:T(8,128)(2,1)}, f32[2,256,1024]{2,1,0:T(8,128)}, bf16[256,1024]{1,0:T(8,128)(2,1)}) custom-call(s32[10]{0:T(128)} %concatenate.71.meta, f32[256,1024]{1,0:T(8,128)} %get-tuple-element.326.stream, f32[34,1024]{1,0:T(8,128)} %rows.15, bf16[7,128,512]{2,1,0:T(8,128)(2,1)} %copy-done, ...), custom_call_target="tpu_custom_call" | custom-call | flops 1610612736 | bytes 14680064 | tf_op jit(solution)/shard_map/conv_forward/pallas_call | solution.py:903
  234.8 9.5 %ffn_forward.3 = (f32[2,512,1024]{2,1,0:T(8,128)}, bf16[2,512,1024]{2,1,0:T(8,128)(2,1)}, f32[256,1024]{1,0:T(8,128)}, bf16[256,1024]{1,0:T(8,128)(2,1)}) custom-call(s32[9]{0:T(128)} %concatenate.74.meta, bf16[512,1024]{1,0:T(8,128)(2,1)} %pad_maximum_fusion.7.normed, f32[2,1,1024]{2,1,0:T(1,128)} %broadcast_in_dim.13.bias, ...), custom_call_target="tpu_custom_call" | custom-call | flops 4294967296 | bytes 17825792 | tf_op jit(solution)/shard_map/ffn_forward/pallas_call | solution.py:416
  247.2 4.4 turn.1
  255.8 12.7 %ffn_out_backward.2 = (bf16[2,512,1024]{2,1,0:T(8,128)(2,1)}, f32[34,1024]{1,0:T(8,128)}, bf16[2,2,2,1024,256]{4,3,2,1,0:T(8,128)(2,1)}) custom-call(s32[11]{0:T(128)} %concatenate.79.meta, f32[2,512,1024]{2,1,0:T(8,128)} %get-tuple-element.342.hidden, bf16[2,512,1024]{2,1,0:T(8,128)(2,1)} %get-tuple-element.343.active, ...), custom_call_target="tpu_custom_call" | custom-call | flops 4294967296 | bytes 16777216 | tf_op jit(solution)/shard_map/ffn_out_backward/pallas_call | solution.py:509
  273.0 9.5 %ffn_in_backward.2 = (f32[256,1024]{1,0:T(8,128)}, bf16[256,1024]{1,0:T(8,128)(2,1)}, bf16[2,2,1024,256]{3,2,1,0:T(8,128)(2,1)}, bf16[2,1024,256]{2,1,0:T(8,128)(2,1)}, bf16[2,1024,256]{2,1,0:T(8,128)(2,1)}) custom-call(s32[11]{0:T(128)} %concatenate.79.meta, bf16[512,1024]{1,0:T(8,128)(2,1)} %pad_maximum_fusion.7.normed, ...), custom_call_target="tpu_custom_call" | custom-call | flops 4294967296 | bytes 16777216 | tf_op jit(solution)/shard_map/ffn_in_backward/pallas_call | solution.py:509
  298.2 8.8 %conv_out_backward.1 = (bf16[2,256,1024]{2,1,0:T(8,128)(2,1)}, bf16[2,1,1024,256]{3,2,1,0:T(8,128)(2,1)}, bf16[2,1,1024,256]{3,2,1,0:T(8,128)(2,1)}, f32[34,1024]{1,0:T(8,128)}) custom-call(s32[10]{0:T(128)} %concatenate.71.meta, f32[256,1024]{1,0:T(8,128)} %get-tuple-element.367.grad, f32[2,256,1024]{2,1,0:T(8,128)} %get-tuple-element.368.wide, ...), custom_call_target="tpu_custom_call" | custom-call | flops 1073741824 | bytes 10485760 | tf_op jit(solution)/shard_map/conv_out_backward/pallas_call | solution.py:903
  307.1 5.8 collective-permute-done.48
  321.4 7.1 %conv_in_backward.1 = (f32[256,1024]{1,0:T(8,128)}, bf16[2,2,1024,256]{3,2,1,0:T(8,128)(2,1)}, bf16[2,2,1024,256]{3,2,1,0:T(8,128)(2,1)}, f32[34,1024]{1,0:T(8,128)}) custom-call(s32[10]{0:T(128)} %concatenate.71.meta, f32[256,1024]{1,0:T(8,128)} %get-tuple-element.367.grad, f32[256,1024]{1,0:T(8,128)} %get-tuple-element.326.stream, ...), custom_call_target="tpu_custom_call" | custom-call | flops 2147483648 | bytes 12582912 | tf_op jit(solution)/shard_map/conv_in_backward/pallas_call | solution.py:903
  328.6 9.7 %attention_heads_backward.1 = (bf16[3,256,1024]{2,1,0:T(8,128)(2,1)}, bf16[2,1,1024,256]{3,2,1,0:T(8,128)(2,1)}, bf16[2,1,1024,256]{3,2,1,0:T(8,128)(2,1)}, f32[34,1024]{1,0:T(8,128)}) custom-call(s32[10]{0:T(128)} %concatenate.71.meta, f32[256,1024]{1,0:T(8,128)} %get-tuple-element.386.grad, bf16[256,1024]{1,0:T(8,128)(2,1)} %get-tuple-element.387.queries, ...), custom_call_target="tpu_custom_call" | custom-call | flops 1610612736 | bytes 10485760 | tf_op jit(solution)/shard_map/attention_heads_backward/pallas_call | solution.py:903
  349.3 9.0 %attention_in_backward.1 = (f32[256,1024]{1,0:T(8,128)}, bf16[2,3,1024,256]{3,2,1,0:T(8,128)(2,1)}, bf16[2,3,1024,256]{3,2,1,0:T(8,128)(2,1)}, f32[34,1024]{1,0:T(8,128)}, bf16[256,1024]{1,0:T(8,128)(2,1)}) custom-call(s32[10]{0:T(128)} %concatenate.71.meta, f32[256,1024]{1,0:T(8,128)} %get-tuple-element.386.grad, f32[256,1024]{1,0:T(8,128)} %multiply_add_fusion.3.stream, ...), custom_call_target="tpu_custom_call" | custom-call | flops 3221225472 | bytes 14680064 | tf_op jit(solution)/shard_map/attention_in_backward/pallas_call | solution.py:903
  358.4 8.7 %collective-permute-done.53.refs_1_ = bf16[12,128,256]{2,1,0:T(8,128)(2,1)S(1)} collective-permute-done((bf16[12,128,256]{2,1,0:T(8,128)(2,1)}, bf16[12,128,256]{2,1,0:T(8,128)(2,1)S(1)}, u32[]{:S(2)}, u32[]{:S(2)}) %collective-permute-start.53) | collective-permute-done | bytes 786464 | tf_op jit(solution)/shard_map/ppermute | solution.py:110
  376.6 9.3 %collective-permute-done.57 = bf16[256,1024]{1,0:T(8,128)(2,1)S(1)} collective-permute-done((bf16[256,1024]{1,0:T(8,128)(2,1)S(1)}, bf16[256,1024]{1,0:T(8,128)(2,1)S(1)}, u32[]{:S(2)}, u32[]{:S(2)}) %collective-permute-start.57) | collective-permute-done | bytes 524320 | tf_op jit(solution)/shard_map/ppermute | solution.py:110
  391.9 11.4 %ffn_out_backward.3 = (bf16[1,1024,1024]{2,1,0:T(8,128)(2,1)}, f32[34,1024]{1,0:T(8,128)}, bf16[2,2,1,1024,256]{4,3,2,1,0:T(8,128)(2,1)}) custom-call(s32[11]{0:T(128)} %concatenate.79.meta, f32[1,1024,1024]{2,1,0:T(8,128)} %get-tuple-element.408.hidden, bf16[1,1024,1024]{2,1,0:T(8,128)(2,1)} %get-tuple-element.409.active, ...), custom_call_target="tpu_custom_call" | custom-call | flops 4294967296 | bytes 25165824 | tf_op jit(solution)/shard_map/ffn_out_backward/pallas_call | solution.py:509
  412.5 9.3 %ffn_in_backward.3 = (f32[512,1024]{1,0:T(8,128)}, bf16[512,1024]{1,0:T(8,128)(2,1)}, bf16[2,2,1,1024,256]{4,3,2,1,0:T(8,128)(2,1)}) custom-call(s32[11]{0:T(128)} %concatenate.79.meta, bf16[1024,1024]{1,0:T(8,128)(2,1)} %pad_maximum_fusion.4.normed, bf16[1,1024,1024]{2,1,0:T(8,128)(2,1)} %get-tuple-element.441.low, bf16[2,128,1024]{2,1,0:T(8,128)(2,1)} %copy-done.41, ...), custom_call_target="tpu_custom_call" | custom-call | flops 4294967296 | bytes 25165824 | tf_op jit(solution)/shard_map/ffn_in_backward/pallas_call | solution.py:509
  431.1 16.5 %collective-permute-done.63.refs_4_ = bf16[16,128,256]{2,1,0:T(8,128)(2,1)} collective-permute-done((bf16[16,128,256]{2,1,0:T(8,128)(2,1)}, bf16[16,128,256]{2,1,0:T(8,128)(2,1)}, u32[]{:S(2)}, u32[]{:S(2)}) %collective-permute-start.63) | collective-permute-done | bytes 1048608 | tf_op jit(solution)/shard_map/ppermute | solution.py:110
  448.9 4.5 hop.17
  460.2 6.4 collective-permute-done.68
  466.6 11.2 %collective-permute-done.69.came = bf16[256,1024]{1,0:T(8,128)(2,1)} collective-permute-done((bf16[256,1024]{1,0:T(8,128)(2,1)}, bf16[256,1024]{1,0:T(8,128)(2,1)}, u32[]{:S(2)}, u32[]{:S(2)}) %collective-permute-start.69) | collective-permute-done | bytes 524320 | tf_op jit(solution)/shard_map/ppermute | solution.py:110
  478.1 4.5 collective-permute-done.67.refs_5_
  485.4 4.7 hop.18
  497.4 19.4 %collective-permute-done.71.refs_4_ = bf16[19,128,256]{2,1,0:T(8,128)(2,1)S(1)} collective-permute-done((bf16[19,128,256]{2,1,0:T(8,128)(2,1)}, bf16[19,128,256]{2,1,0:T(8,128)(2,1)S(1)}, u32[]{:S(2)}, u32[]{:S(2)}) %collective-permute-start.71) | collective-permute-done | bytes 1245216 | tf_op jit(solution)/shard_map/ppermute | solution.py:110
  530.5 8.0 %collective-permute-done.75.refs_3_ = bf16[11,128,256]{2,1,0:T(8,128)(2,1)S(1)} collective-permute-done((bf16[11,128,256]{2,1,0:T(8,128)(2,1)}, bf16[11,128,256]{2,1,0:T(8,128)(2,1)S(1)}, u32[]{:S(2)}, u32[]{:S(2)}) %collective-permute-start.75) | collective-permute-done | bytes 720928 | tf_op jit(solution)/shard_map/ppermute | solution.py:110
  548.8 5.0 collective-permute-start.74
  555.3 5.1 collective-permute-done.78.refs_2_
  578.7 4.6 all-to-all-start
  586.5 5.4 collective-permute-done.84
  594.5 6.1 collective-permute-done.85
  600.6 17.6 %all-to-all-done = bf16[8,3,128,256]{3,2,1,0:T(8,128)(2,1)} async-done(((bf16[8,3,128,256]{3,2,1,0:T(8,128)(2,1)}), bf16[8,3,128,256]{3,2,1,0:T(8,128)(2,1)}, u32[]{:S(2)}, u32[]{:S(2)}) %all-to-all-start) | async-done | bytes 1572896 | tf_op jit(solution)/shard_map/all_to_all | solution.py:1372
  635.2 5.1 collective-permute-done.92
  643.0 4.3 fusion.43
  660.6 4.7 collective-permute-done.94
  (493 shorter events, 297.5 us)
Async XLA Ops:
  28.4 22.0 %collective-permute-start.4 = (bf16[7,128,512]{2,1,0:T(8,128)(2,1)S(1)}, bf16[7,128,512]{2,1,0:T(8,128)(2,1)S(1)}, u32[]{:S(2)}, u32[]{:S(2)}) collective-permute-start(bf16[7,128,512]{2,1,0:T(8,128)(2,1)S(1)} %constant_dynamic-slice_fusion.3.refs_0_), channel_id=1, source_target_pairs={{0,2},{2,4},{4,6},{6,7},{7,5},{5,3},{3,1},{1,0},{8,10},{10,12},{12... | collective-permute-start | bytes 2752520 | tf_op jit(solution)/shard_map/ppermute | solution.py:110
  29.8 21.7 %collective-permute-start.5 = (bf16[7,128,512]{2,1,0:T(8,128)(2,1)S(1)}, bf16[7,128,512]{2,1,0:T(8,128)(2,1)S(1)}, u32[]{:S(2)}, u32[]{:S(2)}) collective-permute-start(bf16[7,128,512]{2,1,0:T(8,128)(2,1)S(1)} %constant_dynamic-slice_fusion.3.refs_0_), channel_id=1, source_target_pairs={{2,0},{4,2},{6,4},{7,6},{5,7},{3,5},{1,3},{0,1},{10,8},{12,10},{14... | collective-permute-start | bytes 2752520 | tf_op jit(solution)/shard_map/ppermute | solution.py:110
  29.9 21.6 %collective-permute-start.6 = (bf16[7,128,512]{2,1,0:T(8,128)(2,1)S(1)}, bf16[7,128,512]{2,1,0:T(8,128)(2,1)S(1)}, u32[]{:S(2)}, u32[]{:S(2)}) collective-permute-start(bf16[7,128,512]{2,1,0:T(8,128)(2,1)S(1)} %constant_dynamic-slice_fusion.3.refs_0_), channel_id=1, source_target_pairs={{0,8},{8,0},{1,9},{9,1},{2,10},{10,2},{3,11},{11,3},{4,12},{12,4},... | collective-permute-start | bytes 2752520 | tf_op jit(solution)/shard_map/ppermute | solution.py:110
  30.5 31.2 %collective-permute-start.7 = (bf16[2,128,1024]{2,1,0:T(8,128)(2,1)}, bf16[2,128,1024]{2,1,0:T(8,128)(2,1)S(1)}, u32[]{:S(2)}, u32[]{:S(2)}) collective-permute-start(bf16[2,128,1024]{2,1,0:T(8,128)(2,1)} %copy-done.62), channel_id=1, source_target_pairs={{0,2},{2,4},{4,6},{6,7},{7,5},{5,3},{3,1},{1,0},{8,10},{10,12},{12... | collective-permute-start | bytes 1572872 | tf_op jit(solution)/shard_map/ppermute | solution.py:110
  31.9 30.9 %collective-permute-start.8 = (bf16[2,128,1024]{2,1,0:T(8,128)(2,1)}, bf16[2,128,1024]{2,1,0:T(8,128)(2,1)S(1)}, u32[]{:S(2)}, u32[]{:S(2)}) collective-permute-start(bf16[2,128,1024]{2,1,0:T(8,128)(2,1)} %collective-permute-done.1.refs_2_), channel_id=1, source_target_pairs={{2,0},{4,2},{6,4},{7,6},{5,7},{3,5},{1,3},{0,1},{10,8},{12,10},{14... | collective-permute-start | bytes 1572872 | tf_op jit(solution)/shard_map/ppermute | solution.py:110
  51.5 21.4 %collective-permute-start.11 = (bf16[2,128,1024]{2,1,0:T(8,128)(2,1)S(1)}, bf16[2,128,1024]{2,1,0:T(8,128)(2,1)S(1)}, u32[]{:S(2)}, u32[]{:S(2)}) collective-permute-start(bf16[2,128,1024]{2,1,0:T(8,128)(2,1)S(1)} %copy-done.42), channel_id=1, source_target_pairs={{0,2},{2,4},{4,6},{6,7},{7,5},{5,3},{3,1},{1,0},{8,10},{10,12},{12... | collective-permute-start | bytes 1572872 | tf_op jit(solution)/shard_map/ppermute | solution.py:110
  63.0 30.2 %collective-permute-start.16 = (bf16[7,128,512]{2,1,0:T(8,128)(2,1)S(1)}, bf16[7,128,512]{2,1,0:T(8,128)(2,1)S(1)}, u32[]{:S(2)}, u32[]{:S(2)}) collective-permute-start(bf16[7,128,512]{2,1,0:T(8,128)(2,1)S(1)} %collective-permute-done.4.refs_1_), channel_id=1, source_target_pairs={{0,8},{8,0},{1,9},{9,1},{2,10},{10,2},{3,11},{11,3},{4,12},{12,4},... | collective-permute-start | bytes 2752520 | tf_op jit(solution)/shard_map/ppermute | solution.py:110
  64.5 28.7 %collective-permute-start.17 = (bf16[7,128,512]{2,1,0:T(8,128)(2,1)S(1)}, bf16[7,128,512]{2,1,0:T(8,128)(2,1)S(1)}, u32[]{:S(2)}, u32[]{:S(2)}) collective-permute-start(bf16[7,128,512]{2,1,0:T(8,128)(2,1)S(1)} %collective-permute-done.5.refs_2_), channel_id=1, source_target_pairs={{0,8},{8,0},{1,9},{9,1},{2,10},{10,2},{3,11},{11,3},{4,12},{12,4},... | collective-permute-start | bytes 2752520 | tf_op jit(solution)/shard_map/ppermute | solution.py:110
  64.5 27.5 %collective-permute-start.9 = (bf16[2,128,1024]{2,1,0:T(8,128)(2,1)S(1)}, bf16[2,128,1024]{2,1,0:T(8,128)(2,1)}, u32[]{:S(2)}, u32[]{:S(2)}) collective-permute-start(bf16[2,128,1024]{2,1,0:T(8,128)(2,1)S(1)} %collective-permute-done.7.refs_3_), channel_id=1, source_target_pairs={{0,2},{2,4},{4,6},{6,7},{7,5},{5,3},{3,1},{1,0},{8,10},{10,12},{12... | collective-permute-start | bytes 1572872 | tf_op jit(solution)/shard_map/ppermute | solution.py:110
  72.9 19.0 %collective-permute-start.12 = (bf16[2,128,1024]{2,1,0:T(8,128)(2,1)S(1)}, bf16[2,128,1024]{2,1,0:T(8,128)(2,1)}, u32[]{:S(2)}, u32[]{:S(2)}) collective-permute-start(bf16[2,128,1024]{2,1,0:T(8,128)(2,1)S(1)} %collective-permute-done.11.refs_1_), channel_id=1, source_target_pairs={{0,16},{16,0},{1,17},{17,1},{2,18},{18,2},{3,19},{19,3},{4,20},{20... | collective-permute-start | bytes 1572872 | tf_op jit(solution)/shard_map/ppermute | solution.py:110
  75.2 18.0 %collective-permute-start.15 = (bf16[2,128,1024]{2,1,0:T(8,128)(2,1)S(1)}, bf16[2,128,1024]{2,1,0:T(8,128)(2,1)}, u32[]{:S(2)}, u32[]{:S(2)}) collective-permute-start(bf16[2,128,1024]{2,1,0:T(8,128)(2,1)S(1)} %copy-done.42), channel_id=1, source_target_pairs={{2,0},{4,2},{6,4},{7,6},{5,7},{3,5},{1,3},{0,1},{10,8},{12,10},{14... | collective-permute-start | bytes 1572872 | tf_op jit(solution)/shard_map/ppermute | solution.py:110
  93.2 25.7 %collective-permute-start.20 = (bf16[7,128,512]{2,1,0:T(8,128)(2,1)S(1)}, bf16[7,128,512]{2,1,0:T(8,128)(2,1)}, u32[]{:S(2)}, u32[]{:S(2)}) collective-permute-start(bf16[7,128,512]{2,1,0:T(8,128)(2,1)S(1)} %collective-permute-done.5.refs_2_), channel_id=1, source_target_pairs={{2,0},{4,2},{6,4},{7,6},{5,7},{3,5},{1,3},{0,1},{10,8},{12,10},{14... | collective-permute-start | bytes 2752520 | tf_op jit(solution)/shard_map/ppermute | solution.py:110
  94.2 29.0 %collective-permute-start.18 = (bf16[7,128,512]{2,1,0:T(8,128)(2,1)S(1)}, bf16[7,128,512]{2,1,0:T(8,128)(2,1)}, u32[]{:S(2)}, u32[]{:S(2)}) collective-permute-start(bf16[7,128,512]{2,1,0:T(8,128)(2,1)S(1)} %collective-permute-done.4.refs_1_), channel_id=1, source_target_pairs={{0,2},{2,4},{4,6},{6,7},{7,5},{5,3},{3,1},{1,0},{8,10},{10,12},{12... | collective-permute-start | bytes 2752520 | tf_op jit(solution)/shard_map/ppermute | solution.py:110
  96.1 22.8 %collective-permute-start.22 = (bf16[2,128,1024]{2,1,0:T(8,128)(2,1)}, bf16[2,128,1024]{2,1,0:T(8,128)(2,1)S(1)}, u32[]{:S(2)}, u32[]{:S(2)}) collective-permute-start(bf16[2,128,1024]{2,1,0:T(8,128)(2,1)} %collective-permute-done.15.refs_2_), channel_id=1, source_target_pairs={{0,16},{16,0},{1,17},{17,1},{2,18},{18,2},{3,19},{19,3},{4,20},{20... | collective-permute-start | bytes 1572872 | tf_op jit(solution)/shard_map/ppermute | solution.py:110
  113.0 22.1 %collective-permute-start.14 = (bf16[512,1024]{1,0:T(8,128)(2,1)}, bf16[512,1024]{1,0:T(8,128)(2,1)S(1)}, u32[]{:S(2)}, u32[]{:S(2)}) collective-permute-start(bf16[512,1024]{1,0:T(8,128)(2,1)} %get-tuple-element.287), channel_id=1, source_target_pairs={{0,8},{8,0},{1,9},{9,1},{2,10},{10,2},{3,11},{11,3},{4,12},{12,4},... | collective-permute-start | bytes 3145736 | tf_op jit(solution)/shard_map/ppermute | solution.py:321
  133.7 18.9 %collective-permute-start.21 = (bf16[7,128,512]{2,1,0:T(8,128)(2,1)}, bf16[7,128,512]{2,1,0:T(8,128)(2,1)S(1)}, u32[]{:S(2)}, u32[]{:S(2)}) collective-permute-start(bf16[7,128,512]{2,1,0:T(8,128)(2,1)} %collective-permute-done.20.refs_4_), channel_id=1, source_target_pairs={{2,0},{4,2},{6,4},{7,6},{5,7},{3,5},{1,3},{0,1},{10,8},{12,10},{14... | collective-permute-start | bytes 2752520 | tf_op jit(solution)/shard_map/ppermute | solution.py:110
  135.0 18.2 %collective-permute-start.19 = (bf16[7,128,512]{2,1,0:T(8,128)(2,1)}, bf16[7,128,512]{2,1,0:T(8,128)(2,1)}, u32[]{:S(2)}, u32[]{:S(2)}) collective-permute-start(bf16[7,128,512]{2,1,0:T(8,128)(2,1)} %collective-permute-done.18.refs_3_), channel_id=1, source_target_pairs={{0,2},{2,4},{4,6},{6,7},{7,5},{5,3},{3,1},{1,0},{8,10},{10,12},{12... | collective-permute-start | bytes 2752520 | tf_op jit(solution)/shard_map/ppermute | solution.py:110
  135.2 18.0 %collective-permute-start.24 = (bf16[2,128,1024]{2,1,0:T(8,128)(2,1)S(1)}, bf16[2,128,1024]{2,1,0:T(8,128)(2,1)S(1)}, u32[]{:S(2)}, u32[]{:S(2)}) collective-permute-start(bf16[2,128,1024]{2,1,0:T(8,128)(2,1)S(1)} %collective-permute-done.23.refs_3_), channel_id=1, source_target_pairs={{0,16},{16,0},{1,17},{17,1},{2,18},{18,2},{3,19},{19,3},{4,20},{20... | collective-permute-start | bytes 1572872 | tf_op jit(solution)/shard_map/ppermute | solution.py:110
  155.7 17.9 %collective-permute-start.28 = (bf16[256,1024]{1,0:T(8,128)(2,1)S(1)}, bf16[256,1024]{1,0:T(8,128)(2,1)S(1)}, u32[]{:S(2)}, u32[]{:S(2)}) collective-permute-start(bf16[256,1024]{1,0:T(8,128)(2,1)S(1)} %slice.327), channel_id=1, source_target_pairs={{0,16},{16,0},{1,17},{17,1},{2,18},{18,2},{3,19},{19,3},{4,20},{20... | collective-permute-start | bytes 1572872 | tf_op jit(solution)/shard_map/ppermute | solution.py:110
  156.1 29.8 %collective-permute-start.32 = (bf16[7,128,512]{2,1,0:T(8,128)(2,1)S(1)}, bf16[7,128,512]{2,1,0:T(8,128)(2,1)}, u32[]{:S(2)}, u32[]{:S(2)}) collective-permute-start(bf16[7,128,512]{2,1,0:T(8,128)(2,1)S(1)} %collective-permute-done.21.refs_6_), channel_id=1, source_target_pairs={{2,0},{4,2},{6,4},{7,6},{5,7},{3,5},{1,3},{0,1},{10,8},{12,10},{14... | collective-permute-start | bytes 2752520 | tf_op jit(solution)/shard_map/ppermute | solution.py:110
  174.3 26.2 %collective-permute-start.35 = (bf16[7,128,512]{2,1,0:T(8,128)(2,1)S(1)}, bf16[7,128,512]{2,1,0:T(8,128)(2,1)}, u32[]{:S(2)}, u32[]{:S(2)}) collective-permute-start(bf16[7,128,512]{2,1,0:T(8,128)(2,1)S(1)} %collective-permute-done.21.refs_6_), channel_id=1, source_target_pairs={{0,8},{8,0},{1,9},{9,1},{2,10},{10,2},{3,11},{11,3},{4,12},{12,4},... | collective-permute-start | bytes 2752520 | tf_op jit(solution)/shard_map/ppermute | solution.py:110
  186.7 22.1 %collective-permute-start.38 = (bf16[7,128,512]{2,1,0:T(8,128)(2,1)}, bf16[7,128,512]{2,1,0:T(8,128)(2,1)}, u32[]{:S(2)}, u32[]{:S(2)}) collective-permute-start(bf16[7,128,512]{2,1,0:T(8,128)(2,1)} %collective-permute-done.32.refs_7_), channel_id=1, source_target_pairs={{0,8},{8,0},{1,9},{9,1},{2,10},{10,2},{3,11},{11,3},{4,12},{12,4},... | collective-permute-start | bytes 2752520 | tf_op jit(solution)/shard_map/ppermute | solution.py:110
  195.0 25.1 %collective-permute-start.39 = (bf16[2,128,1024]{2,1,0:T(8,128)(2,1)}, bf16[2,128,1024]{2,1,0:T(8,128)(2,1)}, u32[]{:S(2)}, u32[]{:S(2)}) collective-permute-start(bf16[2,128,1024]{2,1,0:T(8,128)(2,1)} %collective-permute-done.36.refs_7_), channel_id=1, source_target_pairs={{0,16},{16,0},{1,17},{17,1},{2,18},{18,2},{3,19},{19,3},{4,20},{20... | collective-permute-start | bytes 1572872 | tf_op jit(solution)/shard_map/ppermute | solution.py:110
  289.3 23.6 %collective-permute-start.48 = (bf16[2,1024,256]{2,1,0:T(8,128)(2,1)S(1)}, bf16[2,1024,256]{2,1,0:T(8,128)(2,1)S(1)}, u32[]{:S(2)}, u32[]{:S(2)}) collective-permute-start(bf16[2,1024,256]{2,1,0:T(8,128)(2,1)S(1)} %copy-done.61), channel_id=1, source_target_pairs={{0,16},{16,0},{1,17},{17,1},{2,18},{18,2},{3,19},{19,3},{4,20},{20... | collective-permute-start | bytes 3145736 | tf_op jit(solution)/shard_map/ppermute | solution.py:110
  290.9 16.2 %collective-permute-start.46 = (bf16[8,128,256]{2,1,0:T(8,128)(2,1)}, bf16[8,128,256]{2,1,0:T(8,128)(2,1)S(1)}, u32[]{:S(2)}, u32[]{:S(2)}) collective-permute-start(bf16[8,128,256]{2,1,0:T(8,128)(2,1)} %get-tuple-element.372), channel_id=1, source_target_pairs={{0,2},{2,4},{4,6},{6,7},{7,5},{5,3},{3,1},{1,0},{8,10},{10,12},{12... | collective-permute-start | bytes 1572872 | tf_op jit(solution)/shard_map/ppermute | solution.py:110
  316.4 22.7 %collective-permute-start.51 = (bf16[2,1024,256]{2,1,0:T(8,128)(2,1)S(1)}, bf16[2,1024,256]{2,1,0:T(8,128)(2,1)S(1)}, u32[]{:S(2)}, u32[]{:S(2)}) collective-permute-start(bf16[2,1024,256]{2,1,0:T(8,128)(2,1)S(1)} %copy-done.59), channel_id=1, source_target_pairs={{0,16},{16,0},{1,17},{17,1},{2,18},{18,2},{3,19},{19,3},{4,20},{20... | collective-permute-start | bytes 3145736 | tf_op jit(solution)/shard_map/ppermute | solution.py:110
  316.5 22.6 %collective-permute-start.52 = (bf16[2,1,1024,256]{3,2,1,0:T(8,128)(2,1)}, bf16[2,1,1024,256]{3,2,1,0:T(8,128)(2,1)S(1)}, u32[]{:S(2)}, u32[]{:S(2)}) collective-permute-start(bf16[2,1,1024,256]{3,2,1,0:T(8,128)(2,1)} %get-tuple-element.396), channel_id=1, source_target_pairs={{0,8},{8,0},{1,9},{9,1},{2,10},{10,2},{3,11},{11,3},{4,12},{12,4},... | collective-permute-start | bytes 3145736 | tf_op jit(solution)/shard_map/ppermute | solution.py:110
  318.9 19.4 %collective-permute-start.49 = (bf16[8,128,256]{2,1,0:T(8,128)(2,1)}, bf16[8,128,256]{2,1,0:T(8,128)(2,1)S(1)}, u32[]{:S(2)}, u32[]{:S(2)}) collective-permute-start(bf16[8,128,256]{2,1,0:T(8,128)(2,1)} %get-tuple-element.393), channel_id=1, source_target_pairs={{0,2},{2,4},{4,6},{6,7},{7,5},{5,3},{3,1},{1,0},{8,10},{10,12},{12... | collective-permute-start | bytes 1572872 | tf_op jit(solution)/shard_map/ppermute | solution.py:110
  319.9 18.4 %collective-permute-start.50 = (bf16[8,128,256]{2,1,0:T(8,128)(2,1)}, bf16[8,128,256]{2,1,0:T(8,128)(2,1)S(1)}, u32[]{:S(2)}, u32[]{:S(2)}) collective-permute-start(bf16[8,128,256]{2,1,0:T(8,128)(2,1)} %get-tuple-element.394), channel_id=1, source_target_pairs={{2,0},{4,2},{6,4},{7,6},{5,7},{3,5},{1,3},{0,1},{10,8},{12,10},{14... | collective-permute-start | bytes 1572872 | tf_op jit(solution)/shard_map/ppermute | solution.py:110
  344.1 23.0 %collective-permute-start.55 = (bf16[2,2,1024,256]{3,2,1,0:T(8,128)(2,1)}, bf16[2,2,1024,256]{3,2,1,0:T(8,128)(2,1)S(1)}, u32[]{:S(2)}, u32[]{:S(2)}) collective-permute-start(bf16[2,2,1024,256]{3,2,1,0:T(8,128)(2,1)} %get-tuple-element.413), channel_id=1, source_target_pairs={{0,8},{8,0},{1,9},{9,1},{2,10},{10,2},{3,11},{11,3},{4,12},{12,4},... | collective-permute-start | bytes 6291464 | tf_op jit(solution)/shard_map/ppermute | solution.py:110
  347.2 19.9 %collective-permute-start.56 = (bf16[2,1,1024,256]{3,2,1,0:T(8,128)(2,1)S(1)}, bf16[2,1,1024,256]{3,2,1,0:T(8,128)(2,1)S(1)}, u32[]{:S(2)}, u32[]{:S(2)}) collective-permute-start(bf16[2,1,1024,256]{3,2,1,0:T(8,128)(2,1)S(1)} %copy-done.60), channel_id=1, source_target_pairs={{0,8},{8,0},{1,9},{9,1},{2,10},{10,2},{3,11},{11,3},{4,12},{12,4},... | collective-permute-start | bytes 3145736 | tf_op jit(solution)/shard_map/ppermute | solution.py:110
  347.2 19.8 %collective-permute-start.53 = (bf16[12,128,256]{2,1,0:T(8,128)(2,1)}, bf16[12,128,256]{2,1,0:T(8,128)(2,1)S(1)}, u32[]{:S(2)}, u32[]{:S(2)}) collective-permute-start(bf16[12,128,256]{2,1,0:T(8,128)(2,1)} %get-tuple-element.411), channel_id=1, source_target_pairs={{0,2},{2,4},{4,6},{6,7},{7,5},{5,3},{3,1},{1,0},{8,10},{10,12},{12... | collective-permute-start | bytes 2359304 | tf_op jit(solution)/shard_map/ppermute | solution.py:110
  371.5 32.0 %collective-permute-start.61 = (bf16[2,3,1024,256]{3,2,1,0:T(8,128)(2,1)}, bf16[2,3,1024,256]{3,2,1,0:T(8,128)(2,1)}, u32[]{:S(2)}, u32[]{:S(2)}) collective-permute-start(bf16[2,3,1024,256]{3,2,1,0:T(8,128)(2,1)} %get-tuple-element.427), channel_id=1, source_target_pairs={{0,8},{8,0},{1,9},{9,1},{2,10},{10,2},{3,11},{11,3},{4,12},{12,4},... | collective-permute-start | bytes 9437192 | tf_op jit(solution)/shard_map/ppermute | solution.py:110
  374.8 28.6 %collective-permute-start.59 = (bf16[4,128,256]{2,1,0:T(8,128)(2,1)}, bf16[4,128,256]{2,1,0:T(8,128)(2,1)S(1)}, u32[]{:S(2)}, u32[]{:S(2)}) collective-permute-start(bf16[4,128,256]{2,1,0:T(8,128)(2,1)} %get-tuple-element.425), channel_id=1, source_target_pairs={{0,2},{2,4},{4,6},{6,7},{7,5},{5,3},{3,1},{1,0},{8,10},{10,12},{12... | collective-permute-start | bytes 786440 | tf_op jit(solution)/shard_map/ppermute | solution.py:110
  374.9 28.5 %collective-permute-start.60 = (bf16[4,128,256]{2,1,0:T(8,128)(2,1)S(1)}, bf16[4,128,256]{2,1,0:T(8,128)(2,1)S(1)}, u32[]{:S(2)}, u32[]{:S(2)}) collective-permute-start(bf16[4,128,256]{2,1,0:T(8,128)(2,1)S(1)} %copy-done.76), channel_id=1, source_target_pairs={{2,0},{4,2},{6,4},{7,6},{5,7},{3,5},{1,3},{0,1},{10,8},{12,10},{14... | collective-permute-start | bytes 786440 | tf_op jit(solution)/shard_map/ppermute | solution.py:110
  422.6 25.1 %collective-permute-start.63 = (bf16[16,128,256]{2,1,0:T(8,128)(2,1)}, bf16[16,128,256]{2,1,0:T(8,128)(2,1)}, u32[]{:S(2)}, u32[]{:S(2)}) collective-permute-start(bf16[16,128,256]{2,1,0:T(8,128)(2,1)} %get-tuple-element.444), channel_id=1, source_target_pairs={{0,2},{2,4},{4,6},{6,7},{7,5},{5,3},{3,1},{1,0},{8,10},{10,12},{12... | collective-permute-start | bytes 3145736 | tf_op jit(solution)/shard_map/ppermute | solution.py:110
  422.6 25.2 %collective-permute-start.64 = (bf16[16,128,256]{2,1,0:T(8,128)(2,1)}, bf16[16,128,256]{2,1,0:T(8,128)(2,1)}, u32[]{:S(2)}, u32[]{:S(2)}) collective-permute-start(bf16[16,128,256]{2,1,0:T(8,128)(2,1)} %get-tuple-element.445), channel_id=1, source_target_pairs={{2,0},{4,2},{6,4},{7,6},{5,7},{3,5},{1,3},{0,1},{10,8},{12,10},{14... | collective-permute-start | bytes 3145736 | tf_op jit(solution)/shard_map/ppermute | solution.py:110
  424.5 24.4 %collective-permute-start.65 = (bf16[2,1024,256]{2,1,0:T(8,128)(2,1)}, bf16[2,1024,256]{2,1,0:T(8,128)(2,1)}, u32[]{:S(2)}, u32[]{:S(2)}) collective-permute-start(bf16[2,1024,256]{2,1,0:T(8,128)(2,1)} %slice_bitcast_fusion), channel_id=1, source_target_pairs={{0,16},{16,0},{1,17},{17,1},{2,18},{18,2},{3,19},{19,3},{4,20},{20... | collective-permute-start | bytes 3145736 | tf_op jit(solution)/shard_map/ppermute | solution.py:110
  453.4 29.2 %collective-permute-start.67 = (bf16[20,128,256]{2,1,0:T(8,128)(2,1)}, bf16[20,128,256]{2,1,0:T(8,128)(2,1)}, u32[]{:S(2)}, u32[]{:S(2)}) collective-permute-start(bf16[20,128,256]{2,1,0:T(8,128)(2,1)} %get-tuple-element.455), channel_id=1, source_target_pairs={{2,0},{4,2},{6,4},{7,6},{5,7},{3,5},{1,3},{0,1},{10,8},{12,10},{14... | collective-permute-start | bytes 3932168 | tf_op jit(solution)/shard_map/ppermute | solution.py:110
  454.9 23.2 %collective-permute-start.66 = (bf16[16,128,256]{2,1,0:T(8,128)(2,1)}, bf16[16,128,256]{2,1,0:T(8,128)(2,1)}, u32[]{:S(2)}, u32[]{:S(2)}) collective-permute-start(bf16[16,128,256]{2,1,0:T(8,128)(2,1)} %get-tuple-element.454), channel_id=1, source_target_pairs={{0,2},{2,4},{4,6},{6,7},{7,5},{5,3},{3,1},{1,0},{8,10},{10,12},{12... | collective-permute-start | bytes 3145736 | tf_op jit(solution)/shard_map/ppermute | solution.py:110
  454.9 22.9 %collective-permute-start.69 = (bf16[256,1024]{1,0:T(8,128)(2,1)}, bf16[256,1024]{1,0:T(8,128)(2,1)}, u32[]{:S(2)}, u32[]{:S(2)}) collective-permute-start(bf16[256,1024]{1,0:T(8,128)(2,1)} %slice.326), channel_id=1, source_target_pairs={{0,16},{16,0},{1,17},{17,1},{2,18},{18,2},{3,19},{19,3},{4,20},{20... | collective-permute-start | bytes 1572872 | tf_op jit(solution)/shard_map/ppermute | solution.py:110
  490.2 26.7 %collective-permute-start.71 = (bf16[19,128,256]{2,1,0:T(8,128)(2,1)}, bf16[19,128,256]{2,1,0:T(8,128)(2,1)S(1)}, u32[]{:S(2)}, u32[]{:S(2)}) collective-permute-start(bf16[19,128,256]{2,1,0:T(8,128)(2,1)} %get-tuple-element.471), channel_id=1, source_target_pairs={{0,2},{2,4},{4,6},{6,7},{7,5},{5,3},{3,1},{1,0},{8,10},{10,12},{12... | collective-permute-start | bytes 3735560 | tf_op jit(solution)/shard_map/ppermute | solution.py:110
  490.3 26.5 %collective-permute-start.72 = (bf16[19,128,256]{2,1,0:T(8,128)(2,1)}, bf16[19,128,256]{2,1,0:T(8,128)(2,1)S(1)}, u32[]{:S(2)}, u32[]{:S(2)}) collective-permute-start(bf16[19,128,256]{2,1,0:T(8,128)(2,1)} %get-tuple-element.472), channel_id=1, source_target_pairs={{2,0},{4,2},{6,4},{7,6},{5,7},{3,5},{1,3},{0,1},{10,8},{12,10},{14... | collective-permute-start | bytes 3735560 | tf_op jit(solution)/shard_map/ppermute | solution.py:110
  522.5 20.2 %collective-permute-start.76 = (bf16[15,128,256]{2,1,0:T(8,128)(2,1)}, bf16[15,128,256]{2,1,0:T(8,128)(2,1)S(1)}, u32[]{:S(2)}, u32[]{:S(2)}) collective-permute-start(bf16[15,128,256]{2,1,0:T(8,128)(2,1)} %get-tuple-element.478), channel_id=1, source_target_pairs={{2,0},{4,2},{6,4},{7,6},{5,7},{3,5},{1,3},{0,1},{10,8},{12,10},{14... | collective-permute-start | bytes 2949128 | tf_op jit(solution)/shard_map/ppermute | solution.py:110
  578.7 39.5 %all-to-all-start = ((bf16[8,3,128,256]{3,2,1,0:T(8,128)(2,1)}), bf16[8,3,128,256]{3,2,1,0:T(8,128)(2,1)}, u32[]{:S(2)}, u32[]{:S(2)}) async-start(bf16[8,3,128,256]{3,2,1,0:T(8,128)(2,1)} %bitcast.372), calls=%async_computation | async-start | bytes 3145728 | tf_op jit(solution)/shard_map/all_to_all | solution.py:1372
  630.4 20.0 %collective-permute-start.87 = (f32[34,1024]{1,0:T(8,128)S(1)}, f32[34,1024]{1,0:T(8,128)S(1)}, u32[]{:S(2)}, u32[]{:S(2)}) collective-permute-start(f32[34,1024]{1,0:T(8,128)S(1)} %add.740), channel_id=1, source_target_pairs={{0,4},{1,5},{2,6},{3,7},{4,0},{5,1},{6,2},{7,3},{8,12},{9,13},{10,... | collective-permute-start | bytes 417800 | tf_op jit(solution)/shard_map/ppermute | solution.py:110
  659.8 27.1 %collective-permute-start.96 = (bf16[256,1024]{1,0:T(8,128)(2,1)}, bf16[256,1024]{1,0:T(8,128)(2,1)}, u32[]{:S(2)}, u32[]{:S(2)}) collective-permute-start(bf16[256,1024]{1,0:T(8,128)(2,1)} %fusion.49), channel_id=1, source_target_pairs={{0,16},{16,0},{1,17},{17,1},{2,18},{18,2},{3,19},{19,3},{4,20},{20... | collective-permute-start | bytes 1572872 | tf_op jit(solution)/shard_map/ppermute | solution.py:327
  667.6 24.7 %collective-permute-start.95 = (bf16[2,256,1024]{2,1,0:T(8,128)(2,1)}, bf16[2,256,1024]{2,1,0:T(8,128)(2,1)}, u32[]{:S(2)}, u32[]{:S(2)}) collective-permute-start(bf16[2,256,1024]{2,1,0:T(8,128)(2,1)} %pad_maximum_fusion.10), channel_id=1, source_target_pairs={{0,8},{8,0},{1,9},{9,1},{2,10},{10,2},{3,11},{11,3},{4,12},{12,4},... | collective-permute-start | bytes 3145736 | tf_op jit(solution)/shard_map/ppermute | solution.py:327
  (133 other events, 1409.9 us)

commit v3 on v2

--- a/solution.py
+++ b/solution.py
@@ -749,7 +749,7 @@
 
 def conv_forward_kernel(count, meta, stream, rows, *refs):
     own, other = refs[:count], refs[count : 2 * count]
-    out, normed, wide, active, weights, sems = refs[2 * count :]
+    out, normed, wide, active, next_low, weights, sems = refs[2 * count :]
     core, length = meta[count], meta[count + 1]
     width = stream.shape[1]
     copies = halves_to_panels(4, 7, own, other, meta, core, weights, sems)
@@ -773,6 +773,9 @@
         out[:, cols] = (
             stream[:, cols] + dot(active[...], weights[2, :, cols]) + rows[33:34, cols]
         )
+
+    inside, ignored = norm_parts(out[...])
+    next_low[...] = (inside * rows[8:9] + rows[9:10]).astype(bf16)
 
 
 def conv_out_backward_kernel(count, meta, grad, wide, active, rows, had, *refs):
@@ -1016,11 +1019,10 @@
     slot(middle.hop(), to_core.more())
     normed = Cell(all_four(own_first, far_first[0].value))
     slot(first.hop())
-    bind(normed, *wires.past[-2])
+    bind(normed, left, right, *wires.past[-2])
     slot(second.hop(), to_core.more(2))
     slot(first.hop(), to_chip.more())
-    came = slot(middle.hop(), to_chip.more())
-    bind(left, right, *wires.past[-2])
+    slot(middle.hop(), to_chip.more())
     came = slot(first.hop())
     while any(first.left):
         came = slot(first.hop())
@@ -1069,7 +1071,7 @@
     came = []
     while to_chip.next < len(second.pieces):
         came += wires.start(to_chip.more(2), after=[after_attn])
-    after_conv, conv_normed, wide, conv_active = panel_call(
+    after_conv, conv_normed, wide, conv_active, second_low = panel_call(
         conv_forward_kernel,
         "conv_forward",
         3,
@@ -1077,11 +1079,11 @@
         [after_attn.value, vectors],
         values(middle.pieces),
         values(middle_other),
-        [stream, low_stream, shape((2, tokens, width), f32), low_stream],
+        [stream, low_stream, shape((2, tokens, width), f32), low_stream, low_stream],
         [],
         6 * tokens * width * width,
     )
-    normed = both_cores(layer_norm(after_conv, vectors[8], vectors[9]).astype(bf16))
+    normed = both_cores(second_low)
     hidden, active, mine, away = ffn_forward_call(
         normed, bias_second.value, sides_of(second, second_other), meta_of(second, parity)
     )
@@ -1267,7 +1269,7 @@
     bind(half_low, *came)
     conv_total = jnp.concatenate([conv_in.total(), conv_out.total()], axis=1)
     if pairs:
-        conv_chips = ChipSum(wires, blocks=conv_total, cuts=[(0, 2), (2, 3)])
+        conv_chips = ChipSum(wires, blocks=conv_total, cuts=[(0, 1), (1, 3)])
     else:
         conv_part = ring_of(0, conv_total)
     far_low = []
@@ -1278,6 +1280,8 @@
         beside=[half_low],
     )
     both_low = Cell(all_four(half_low.value, far_low[0].value))
+    if pairs:
+        came += begin(conv_chips.send(), beside=[both_low])
     low, sums, *matrices = ffn_backward_out(
         both_low.value, first, [], kept_first, 12, sums, False
     )
@@ -1289,20 +1293,18 @@
     came = begin(hop_together(second_in.ring, attn_part, first_out), conv_sends, beside=[low])
     mine, away, *matrices = ffn_backward_in(low.value, first, [], kept_first, False)
     first_in = ring_of(0, matrices[0])
-    own, far = sum_four(mine, away)
-    own, far = Cell(own), Cell(far)
-    bind(own, far, *came)
-    conv_sends = conv_chips.send() if pairs else []
-    far_came = []
-    came = begin(
-        hop_together(second_in.ring, attn_part, first_out, first_in),
-        conv_sends,
-        [(far.value, "chip", far_came.append)],
-        beside=[own],
-    )
-    bind(*came)
+    mine, away = Cell(mine), Cell(away)
+    bind(mine, away, *came)
     if pairs:
         conv_part = ring_of(1, conv_chips.total().astype(bf16))
+    came = begin(
+        hop_together(second_in.ring, attn_part, first_out, first_in, conv_part),
+        beside=[mine, away],
+    )
+    own, far = sum_four(mine.value, away.value)
+    own, far_came = Cell(own), []
+    came += begin([(far, "chip", far_came.append)], beside=[own])
+    bind(*came)
     came = begin(hop_together(attn_part, first_out, first_in, conv_part), second_out.finish())
     frames_grad, sums = pull_call(
         0, flow.value, start.value, own.value, far_came[0].value, vectors, sums, bf16
@@ -1314,8 +1316,6 @@
     bind(*came)
     attn_chips = ChipSum(wires, blocks=attn_part.total())
     came = begin(hop_together(first_out, first_in, conv_part), attn_chips.send())
-    bind(*came)
-    came = begin(hop_together(first_in, conv_part))
     bind(*came)
     conv_total = conv_part.total()
     if not pairs:

time: 716 us -> 709 us (level)
  starting transfers between devices: 129 us -> 121 us
    ppermute x76 -> x75, waiting for transfers between devices: 219 us -> 216 us  [start(): came.append(Cell(lax.ppermute(value, axis, pairs)))]
    pallas_call x11 -> x10, Pallas kernels: 37.9 us -> 36.3 us  [hop_together(): pl.pallas_call(functools.partial(hop_kernel, tuple(plan), (len(inputs), l...]
    unnamed x165 -> x166, local copies, waits for them, and re-layouts: 13.3 us -> 14.6 us
    ppermute x76 -> x75, starting transfers between devices: 84.5 us -> 84 us  [start(): came.append(Cell(lax.ppermute(value, axis, pairs)))]
  transfers between devices with their start and end apart: 101 -> 100, of which waited for: 49 -> 51; matrix products, arithmetic and copies ran while one was open for 14% -> 14% of each run, Pallas kernels for 12% -> 13%
where the time goes in v3:
time: 709 us; the launch traced here: 699 us
  waiting for transfers between devices  262 us (37%)
  Pallas kernels  166 us (23%)
  starting transfers between devices  121 us (17%)
  other arithmetic  81.4 us (11%)
  local copies, waits for them, and re-layouts  34.8 us (5%)
  matrix products  30.3 us (4%)
    ppermute x75, waiting for transfers between devices, start(): came.append(Cell(lax.ppermute(value, axis, pairs)))  216 us
    ppermute x75, starting transfers between devices, start(): came.append(Cell(lax.ppermute(value, axis, pairs)))  84 us
    pallas_call x6, Pallas kernels, panel_call(): pl.pallas_call(functools.partial(kernel, count), out_shape=outs, in_specs...  52.8 us
    pallas_call x4, Pallas kernels, ffn_backward_call(): pl.pallas_call(functools.partial(kernel, count, halves, bias, (outer, way...  42.9 us
    pallas_call x10, Pallas kernels, hop_together(): pl.pallas_call(functools.partial(hop_kernel, tuple(plan), (len(inputs), l...  36.3 us
    ppermute x10, starting transfers between devices, swap_cores(): return lax.ppermute(values, 'c', SWAP)  19.6 us
    all_to_all x1, waiting for transfers between devices, on_device(): lax.all_to_all(outgoing, 'f', split_axis=0, concat_axis=0, tiled=True)  19.1 us
    pallas_call x2, Pallas kernels, ffn_forward_call(): pl.pallas_call(functools.partial(ffn_forward_kernel, count, halves), out_...  19 us
  transfers between devices with their start and end apart: 100, of which 51 were waited for; matrix products, arithmetic and copies ran while one was open for 14% of the time, Pallas kernels for 13%

profile of v3, /device:TPU:1, one launch (start us, length us, event | category | flops | bytes accessed | tf_op | source)
XLA Modules:
  0.0 699.5 jit_solution(1778203439452591511)
XLA Ops:
  15.8 7.5 %collective-permute-done.refs_1_ = bf16[2,128,1024]{2,1,0:T(8,128)(2,1)S(1)} collective-permute-done((bf16[2,128,1024]{2,1,0:T(8,128)(2,1)S(1)}, bf16[2,128,1024]{2,1,0:T(8,128)(2,1)S(1)}, u32[]{:S(2)}, u32[]{:S(2)}) %collective-permute-start) | collective-permute-done | bytes 524320 | tf_op jit(solution)/shard_map/ppermute | solution.py:110
  31.9 8.3 %convert_element_type.214 = bf16[3,1024,1024]{2,1,0:T(8,128)(2,1)} convert(f32[3,1024,1024]{2,1,0:T(8,128)} %param.21) | non-fusion elementwise | flops 3145728 | bytes 18874368 | tf_op jit(solution)/shard_map/convert_element_type | solution.py:999
  40.2 8.2 %convert_element_type.215 = bf16[3,1024,1024]{2,1,0:T(8,128)(2,1)} convert(f32[3,1024,1024]{2,1,0:T(8,128)} %param.22) | non-fusion elementwise | flops 3145728 | bytes 18874368 | tf_op jit(solution)/shard_map/convert_element_type | solution.py:1000
  52.8 8.8 %collective-permute-done.7.refs_3_ = bf16[2,128,1024]{2,1,0:T(8,128)(2,1)S(1)} collective-permute-done((bf16[2,128,1024]{2,1,0:T(8,128)(2,1)}, bf16[2,128,1024]{2,1,0:T(8,128)(2,1)S(1)}, u32[]{:S(2)}, u32[]{:S(2)}) %collective-permute-start.7) | collective-permute-done | bytes 524320 | tf_op jit(solution)/shard_map/ppermute | solution.py:110
  65.5 7.3 %collective-permute-done.11.refs_1_ = bf16[2,128,1024]{2,1,0:T(8,128)(2,1)S(1)} collective-permute-done((bf16[2,128,1024]{2,1,0:T(8,128)(2,1)S(1)}, bf16[2,128,1024]{2,1,0:T(8,128)(2,1)S(1)}, u32[]{:S(2)}, u32[]{:S(2)}) %collective-permute-start.11) | collective-permute-done | bytes 524320 | tf_op jit(solution)/shard_map/ppermute | solution.py:110
  75.4 8.8 %collective-permute-done.9.refs_5_ = bf16[2,128,1024]{2,1,0:T(8,128)(2,1)} collective-permute-done((bf16[2,128,1024]{2,1,0:T(8,128)(2,1)S(1)}, bf16[2,128,1024]{2,1,0:T(8,128)(2,1)}, u32[]{:S(2)}, u32[]{:S(2)}) %collective-permute-start.9) | collective-permute-done | bytes 524320 | tf_op jit(solution)/shard_map/ppermute | solution.py:110
  90.9 5.8 collective-permute-done.13.refs_7_
  96.8 9.5 %ffn_forward.2 = (f32[1,1024,1024]{2,1,0:T(8,128)}, bf16[1,1024,1024]{2,1,0:T(8,128)(2,1)}, f32[512,1024]{1,0:T(8,128)}, bf16[512,1024]{1,0:T(8,128)(2,1)}) custom-call(s32[9]{0:T(128)} %concatenate.74.meta, bf16[1024,1024]{1,0:T(8,128)(2,1)} %pad_maximum_fusion.4.normed, f32[1,1,1024]{2,1,0:T(1,128)} %get-tuple-element.282.bias, ...), custom_call_target="tpu_custom_call" | custom-call | flops 4294967296 | bytes 27262976 | tf_op jit(solution)/shard_map/ffn_forward/pallas_call | solution.py:416
  106.3 5.7 collective-permute-start.14
  112.0 4.4 collective-permute-done.18.refs_3_
  121.5 5.4 collective-permute-done.25.refs_4_
  132.7 13.0 %collective-permute-done.21.refs_6_ = bf16[7,128,512]{2,1,0:T(8,128)(2,1)S(1)} collective-permute-done((bf16[7,128,512]{2,1,0:T(8,128)(2,1)}, bf16[7,128,512]{2,1,0:T(8,128)(2,1)S(1)}, u32[]{:S(2)}, u32[]{:S(2)}) %collective-permute-start.21) | collective-permute-done | bytes 917536 | tf_op jit(solution)/shard_map/ppermute | solution.py:110
  151.0 5.3 collective-permute-done.30.refs_6_
  157.6 9.8 %collective-permute-done.28 = bf16[256,1024]{1,0:T(8,128)(2,1)S(1)} collective-permute-done((bf16[256,1024]{1,0:T(8,128)(2,1)S(1)}, bf16[256,1024]{1,0:T(8,128)(2,1)S(1)}, u32[]{:S(2)}, u32[]{:S(2)}) %collective-permute-start.28) | collective-permute-done | bytes 524320 | tf_op jit(solution)/shard_map/ppermute | solution.py:110
  168.7 10.5 %collective-permute-start.35 = (bf16[7,128,512]{2,1,0:T(8,128)(2,1)S(1)}, bf16[7,128,512]{2,1,0:T(8,128)(2,1)}, u32[]{:S(2)}, u32[]{:S(2)}) collective-permute-start(bf16[7,128,512]{2,1,0:T(8,128)(2,1)S(1)} %collective-permute-done.21.refs_6_), channel_id=1, source_target_pairs={{0,8},{8,0},{1,9},{9,1},{2,10},{10,2},{3,11},{11,3},{4,12},{12,4},... | collective-permute-start | bytes 2752520 | tf_op jit(solution)/shard_map/ppermute | solution.py:110
  180.0 8.1 %collective-permute-start.38 = (bf16[7,128,512]{2,1,0:T(8,128)(2,1)}, bf16[7,128,512]{2,1,0:T(8,128)(2,1)}, u32[]{:S(2)}, u32[]{:S(2)}) collective-permute-start(bf16[7,128,512]{2,1,0:T(8,128)(2,1)} %collective-permute-done.32.refs_7_), channel_id=1, source_target_pairs={{0,8},{8,0},{1,9},{9,1},{2,10},{10,2},{3,11},{11,3},{4,12},{12,4},... | collective-permute-start | bytes 2752520 | tf_op jit(solution)/shard_map/ppermute | solution.py:110
  193.7 8.3 %collective-permute-done.33.refs_13_ = bf16[2,128,1024]{2,1,0:T(8,128)(2,1)} collective-permute-done((bf16[2,128,1024]{2,1,0:T(8,128)(2,1)}, bf16[2,128,1024]{2,1,0:T(8,128)(2,1)}, u32[]{:S(2)}, u32[]{:S(2)}) %collective-permute-start.33) | collective-permute-done | bytes 524320 | tf_op jit(solution)/shard_map/ppermute | solution.py:110
  202.0 9.5 %attention_forward.1 = (f32[256,1024]{1,0:T(8,128)}, bf16[256,1024]{1,0:T(8,128)(2,1)}, bf16[256,1024]{1,0:T(8,128)(2,1)}, bf16[256,1024]{1,0:T(8,128)(2,1)}, bf...) custom-call(s32[10]{0:T(128)} %concatenate.71.meta, f32[256,1024]{1,0:T(8,128)} %multiply_add_fusion.3.stream, ...), custom_call_target="tpu_custom_call" | custom-call | flops 2147483648 | bytes 16777216 | tf_op jit(solution)/shard_map/attention_forward/pallas_call | solution.py:906
  213.2 8.1 %conv_forward.1 = (f32[256,1024]{1,0:T(8,128)}, bf16[256,1024]{1,0:T(8,128)(2,1)}, f32[2,256,1024]{2,1,0:T(8,128)}, bf16[256,1024]{1,0:T(8,128)(2,1)}, bf16[256,1024]{1,0:T(8,128)(2,1)}) custom-call(s32[10]{0:T(128)} %concatenate.71.meta, f32[256,1024]{1,0:T(8,128)} %get-tuple-element.324.stream, f32[34,1024]{1,0:T(8,128)} %rows.15, ...), custom_call_target="tpu_custom_call" | custom-call | flops 1610612736 | bytes 14680064 | tf_op jit(solution)/shard_map/conv_forward/pallas_call | solution.py:906
  225.0 9.5 %ffn_forward.3 = (f32[2,512,1024]{2,1,0:T(8,128)}, bf16[2,512,1024]{2,1,0:T(8,128)(2,1)}, f32[256,1024]{1,0:T(8,128)}, bf16[256,1024]{1,0:T(8,128)(2,1)}) custom-call(s32[9]{0:T(128)} %concatenate.74.meta, bf16[512,1024]{1,0:T(8,128)(2,1)} %copy-done.51, f32[2,1,1024]{2,1,0:T(1,128)} %broadcast_in_dim.25.bias, ...), custom_call_target="tpu_custom_call" | custom-call | flops 4294967296 | bytes 17825792 | tf_op jit(solution)/shard_map/ffn_forward/pallas_call | solution.py:416
  237.5 4.6 turn.1
  246.3 12.7 %ffn_out_backward.2 = (bf16[2,512,1024]{2,1,0:T(8,128)(2,1)}, f32[34,1024]{1,0:T(8,128)}, bf16[2,2,2,1024,256]{4,3,2,1,0:T(8,128)(2,1)}) custom-call(s32[11]{0:T(128)} %concatenate.79.meta, f32[2,512,1024]{2,1,0:T(8,128)} %get-tuple-element.341.hidden, bf16[2,512,1024]{2,1,0:T(8,128)(2,1)} %get-tuple-element.342.active, ...), custom_call_target="tpu_custom_call" | custom-call | flops 4294967296 | bytes 16777216 | tf_op jit(solution)/shard_map/ffn_out_backward/pallas_call | solution.py:509
  263.7 9.5 %ffn_in_backward.2 = (f32[256,1024]{1,0:T(8,128)}, bf16[256,1024]{1,0:T(8,128)(2,1)}, bf16[2,2,1024,256]{3,2,1,0:T(8,128)(2,1)}, bf16[2,1024,256]{2,1,0:T(8,128)(2,1)}, bf16[2,1024,256]{2,1,0:T(8,128)(2,1)}) custom-call(s32[11]{0:T(128)} %concatenate.79.meta, bf16[512,1024]{1,0:T(8,128)(2,1)} %copy-done.51, bf16[2,512,1024]{2,1,0:T(8,128)(2,1)} %get-tuple-element.349.low, ...), custom_call_target="tpu_custom_call" | custom-call | flops 4294967296 | bytes 16777216 | tf_op jit(solution)/shard_map/ffn_in_backward/pallas_call | solution.py:509
  288.8 8.9 %conv_out_backward.1 = (bf16[2,256,1024]{2,1,0:T(8,128)(2,1)}, bf16[2,1,1024,256]{3,2,1,0:T(8,128)(2,1)}, bf16[2,1,1024,256]{3,2,1,0:T(8,128)(2,1)}, f32[34,1024]{1,0:T(8,128)}) custom-call(s32[10]{0:T(128)} %concatenate.71.meta, f32[256,1024]{1,0:T(8,128)} %get-tuple-element.366.grad, f32[2,256,1024]{2,1,0:T(8,128)} %get-tuple-element.367.wide, ...), custom_call_target="tpu_custom_call" | custom-call | flops 1073741824 | bytes 10485760 | tf_op jit(solution)/shard_map/conv_out_backward/pallas_call | solution.py:906
  297.7 6.4 collective-permute-done.48
  312.1 7.1 %conv_in_backward.1 = (f32[256,1024]{1,0:T(8,128)}, bf16[2,2,1024,256]{3,2,1,0:T(8,128)(2,1)}, bf16[2,2,1024,256]{3,2,1,0:T(8,128)(2,1)}, f32[34,1024]{1,0:T(8,128)}) custom-call(s32[10]{0:T(128)} %concatenate.71.meta, f32[256,1024]{1,0:T(8,128)} %get-tuple-element.366.grad, f32[256,1024]{1,0:T(8,128)} %get-tuple-element.324.stream, ...), custom_call_target="tpu_custom_call" | custom-call | flops 2147483648 | bytes 12582912 | tf_op jit(solution)/shard_map/conv_in_backward/pallas_call | solution.py:906
  319.3 9.7 %attention_heads_backward.1 = (bf16[3,256,1024]{2,1,0:T(8,128)(2,1)}, bf16[2,1,1024,256]{3,2,1,0:T(8,128)(2,1)}, bf16[2,1,1024,256]{3,2,1,0:T(8,128)(2,1)}, f32[34,1024]{1,0:T(8,128)}) custom-call(s32[10]{0:T(128)} %concatenate.71.meta, f32[256,1024]{1,0:T(8,128)} %get-tuple-element.385.grad, bf16[256,1024]{1,0:T(8,128)(2,1)} %get-tuple-element.386.queries, ...), custom_call_target="tpu_custom_call" | custom-call | flops 1610612736 | bytes 10485760 | tf_op jit(solution)/shard_map/attention_heads_backward/pallas_call | solution.py:906
  340.8 9.4 %attention_in_backward.1 = (f32[256,1024]{1,0:T(8,128)}, bf16[2,3,1024,256]{3,2,1,0:T(8,128)(2,1)}, bf16[2,3,1024,256]{3,2,1,0:T(8,128)(2,1)}, f32[34,1024]{1,0:T(8,128)}, bf16[256,1024]{1,0:T(8,128)(2,1)}) custom-call(s32[10]{0:T(128)} %concatenate.71.meta, f32[256,1024]{1,0:T(8,128)} %get-tuple-element.385.grad, f32[256,1024]{1,0:T(8,128)} %multiply_add_fusion.3.stream, ...), custom_call_target="tpu_custom_call" | custom-call | flops 3221225472 | bytes 14680064 | tf_op jit(solution)/shard_map/attention_in_backward/pallas_call | solution.py:906
  350.3 7.6 %collective-permute-done.53.refs_1_ = bf16[12,128,256]{2,1,0:T(8,128)(2,1)S(1)} collective-permute-done((bf16[12,128,256]{2,1,0:T(8,128)(2,1)}, bf16[12,128,256]{2,1,0:T(8,128)(2,1)S(1)}, u32[]{:S(2)}, u32[]{:S(2)}) %collective-permute-start.53) | collective-permute-done | bytes 786464 | tf_op jit(solution)/shard_map/ppermute | solution.py:110
  365.6 11.1 %collective-permute-done.57 = bf16[256,1024]{1,0:T(8,128)(2,1)S(1)} collective-permute-done((bf16[256,1024]{1,0:T(8,128)(2,1)S(1)}, bf16[256,1024]{1,0:T(8,128)(2,1)S(1)}, u32[]{:S(2)}, u32[]{:S(2)}) %collective-permute-start.57) | collective-permute-done | bytes 524320 | tf_op jit(solution)/shard_map/ppermute | solution.py:110
  384.4 11.4 %ffn_out_backward.3 = (bf16[1,1024,1024]{2,1,0:T(8,128)(2,1)}, f32[34,1024]{1,0:T(8,128)}, bf16[2,2,1,1024,256]{4,3,2,1,0:T(8,128)(2,1)}) custom-call(s32[11]{0:T(128)} %concatenate.79.meta, f32[1,1024,1024]{2,1,0:T(8,128)} %get-tuple-element.407.hidden, bf16[1,1024,1024]{2,1,0:T(8,128)(2,1)} %get-tuple-element.408.active, ...), custom_call_target="tpu_custom_call" | custom-call | flops 4294967296 | bytes 25165824 | tf_op jit(solution)/shard_map/ffn_out_backward/pallas_call | solution.py:509
  408.7 9.4 %ffn_in_backward.3 = (f32[512,1024]{1,0:T(8,128)}, bf16[512,1024]{1,0:T(8,128)(2,1)}, bf16[2,2,1,1024,256]{4,3,2,1,0:T(8,128)(2,1)}) custom-call(s32[11]{0:T(128)} %concatenate.79.meta, bf16[1024,1024]{1,0:T(8,128)(2,1)} %pad_maximum_fusion.4.normed, bf16[1,1024,1024]{2,1,0:T(8,128)(2,1)} %get-tuple-element.442.low, bf16[2,128,1024]{2,1,0:T(8,128)(2,1)} %copy-done.41, ...), custom_call_target="tpu_custom_call" | custom-call | flops 4294967296 | bytes 25165824 | tf_op jit(solution)/shard_map/ffn_in_backward/pallas_call | solution.py:509
  418.1 10.4 %collective-permute-done.63.refs_5_ = bf16[16,128,256]{2,1,0:T(8,128)(2,1)} collective-permute-done((bf16[16,128,256]{2,1,0:T(8,128)(2,1)}, bf16[16,128,256]{2,1,0:T(8,128)(2,1)}, u32[]{:S(2)}, u32[]{:S(2)}) %collective-permute-start.63) | collective-permute-done | bytes 1048608 | tf_op jit(solution)/shard_map/ppermute | solution.py:110
  432.4 5.1 hop.16
  448.4 22.4 %collective-permute-done.66.refs_4_ = bf16[19,128,256]{2,1,0:T(8,128)(2,1)} collective-permute-done((bf16[19,128,256]{2,1,0:T(8,128)(2,1)}, bf16[19,128,256]{2,1,0:T(8,128)(2,1)}, u32[]{:S(2)}, u32[]{:S(2)}) %collective-permute-start.66) | collective-permute-done | bytes 1245216 | tf_op jit(solution)/shard_map/ppermute | solution.py:110
  470.8 4.5 collective-permute-done.67.refs_5_
  476.4 5.0 hop.17
  489.4 20.4 %collective-permute-done.71.refs_4_ = bf16[19,128,256]{2,1,0:T(8,128)(2,1)S(1)} collective-permute-done((bf16[19,128,256]{2,1,0:T(8,128)(2,1)}, bf16[19,128,256]{2,1,0:T(8,128)(2,1)S(1)}, u32[]{:S(2)}, u32[]{:S(2)}) %collective-permute-start.71) | collective-permute-done | bytes 1245216 | tf_op jit(solution)/shard_map/ppermute | solution.py:110
  522.7 9.4 %collective-permute-done.75.refs_3_ = bf16[11,128,256]{2,1,0:T(8,128)(2,1)S(1)} collective-permute-done((bf16[11,128,256]{2,1,0:T(8,128)(2,1)}, bf16[11,128,256]{2,1,0:T(8,128)(2,1)S(1)}, u32[]{:S(2)}, u32[]{:S(2)}) %collective-permute-start.75) | collective-permute-done | bytes 720928 | tf_op jit(solution)/shard_map/ppermute | solution.py:110
  532.2 4.5 collective-permute-done.76.refs_4_
  554.0 6.7 collective-permute-done.80
  570.7 5.1 all-to-all-start
  577.7 5.5 collective-permute-done.83
  585.8 7.3 %collective-permute-done.84 = f32[34,1024]{1,0:T(8,128)S(1)} collective-permute-done((f32[34,1024]{1,0:T(8,128)S(1)}, f32[34,1024]{1,0:T(8,128)S(1)}, u32[]{:S(2)}, u32[]{:S(2)}) %collective-permute-start.84) | collective-permute-done | bytes 139296 | tf_op jit(solution)/shard_map/ppermute | solution.py:110
  593.1 19.1 %all-to-all-done = bf16[8,3,128,256]{3,2,1,0:T(8,128)(2,1)} async-done(((bf16[8,3,128,256]{3,2,1,0:T(8,128)(2,1)}), bf16[8,3,128,256]{3,2,1,0:T(8,128)(2,1)}, u32[]{:S(2)}, u32[]{:S(2)}) %all-to-all-start) | async-done | bytes 1572896 | tf_op jit(solution)/shard_map/all_to_all | solution.py:1372
  628.4 5.5 collective-permute-done.91
  636.6 4.3 fusion.43
  653.5 4.8 collective-permute-done.93
  (487 shorter events, 286.5 us)
Async XLA Ops:
  28.4 22.8 %collective-permute-start.4 = (bf16[7,128,512]{2,1,0:T(8,128)(2,1)S(1)}, bf16[7,128,512]{2,1,0:T(8,128)(2,1)S(1)}, u32[]{:S(2)}, u32[]{:S(2)}) collective-permute-start(bf16[7,128,512]{2,1,0:T(8,128)(2,1)S(1)} %constant_dynamic-slice_fusion.3.refs_0_), channel_id=1, source_target_pairs={{0,2},{2,4},{4,6},{6,7},{7,5},{5,3},{3,1},{1,0},{8,10},{10,12},{12... | collective-permute-start | bytes 2752520 | tf_op jit(solution)/shard_map/ppermute | solution.py:110
  29.8 21.7 %collective-permute-start.5 = (bf16[7,128,512]{2,1,0:T(8,128)(2,1)S(1)}, bf16[7,128,512]{2,1,0:T(8,128)(2,1)S(1)}, u32[]{:S(2)}, u32[]{:S(2)}) collective-permute-start(bf16[7,128,512]{2,1,0:T(8,128)(2,1)S(1)} %constant_dynamic-slice_fusion.3.refs_0_), channel_id=1, source_target_pairs={{2,0},{4,2},{6,4},{7,6},{5,7},{3,5},{1,3},{0,1},{10,8},{12,10},{14... | collective-permute-start | bytes 2752520 | tf_op jit(solution)/shard_map/ppermute | solution.py:110
  29.9 21.6 %collective-permute-start.6 = (bf16[7,128,512]{2,1,0:T(8,128)(2,1)S(1)}, bf16[7,128,512]{2,1,0:T(8,128)(2,1)S(1)}, u32[]{:S(2)}, u32[]{:S(2)}) collective-permute-start(bf16[7,128,512]{2,1,0:T(8,128)(2,1)S(1)} %constant_dynamic-slice_fusion.3.refs_0_), channel_id=1, source_target_pairs={{0,8},{8,0},{1,9},{9,1},{2,10},{10,2},{3,11},{11,3},{4,12},{12,4},... | collective-permute-start | bytes 2752520 | tf_op jit(solution)/shard_map/ppermute | solution.py:110
  30.5 31.2 %collective-permute-start.7 = (bf16[2,128,1024]{2,1,0:T(8,128)(2,1)}, bf16[2,128,1024]{2,1,0:T(8,128)(2,1)S(1)}, u32[]{:S(2)}, u32[]{:S(2)}) collective-permute-start(bf16[2,128,1024]{2,1,0:T(8,128)(2,1)} %copy-done.60), channel_id=1, source_target_pairs={{0,2},{2,4},{4,6},{6,7},{7,5},{5,3},{3,1},{1,0},{8,10},{10,12},{12... | collective-permute-start | bytes 1572872 | tf_op jit(solution)/shard_map/ppermute | solution.py:110
  31.8 30.9 %collective-permute-start.8 = (bf16[2,128,1024]{2,1,0:T(8,128)(2,1)}, bf16[2,128,1024]{2,1,0:T(8,128)(2,1)S(1)}, u32[]{:S(2)}, u32[]{:S(2)}) collective-permute-start(bf16[2,128,1024]{2,1,0:T(8,128)(2,1)} %collective-permute-done.1.refs_2_), channel_id=1, source_target_pairs={{2,0},{4,2},{6,4},{7,6},{5,7},{3,5},{1,3},{0,1},{10,8},{12,10},{14... | collective-permute-start | bytes 1572872 | tf_op jit(solution)/shard_map/ppermute | solution.py:110
  51.5 21.4 %collective-permute-start.11 = (bf16[2,128,1024]{2,1,0:T(8,128)(2,1)S(1)}, bf16[2,128,1024]{2,1,0:T(8,128)(2,1)S(1)}, u32[]{:S(2)}, u32[]{:S(2)}) collective-permute-start(bf16[2,128,1024]{2,1,0:T(8,128)(2,1)S(1)} %copy-done.42), channel_id=1, source_target_pairs={{0,2},{2,4},{4,6},{6,7},{7,5},{5,3},{3,1},{1,0},{8,10},{10,12},{12... | collective-permute-start | bytes 1572872 | tf_op jit(solution)/shard_map/ppermute | solution.py:110
  63.0 23.6 %collective-permute-start.17 = (bf16[7,128,512]{2,1,0:T(8,128)(2,1)S(1)}, bf16[7,128,512]{2,1,0:T(8,128)(2,1)S(1)}, u32[]{:S(2)}, u32[]{:S(2)}) collective-permute-start(bf16[7,128,512]{2,1,0:T(8,128)(2,1)S(1)} %collective-permute-done.5.refs_2_), channel_id=1, source_target_pairs={{0,8},{8,0},{1,9},{9,1},{2,10},{10,2},{3,11},{11,3},{4,12},{12,4},... | collective-permute-start | bytes 2752520 | tf_op jit(solution)/shard_map/ppermute | solution.py:110
  64.4 22.2 %collective-permute-start.16 = (bf16[7,128,512]{2,1,0:T(8,128)(2,1)S(1)}, bf16[7,128,512]{2,1,0:T(8,128)(2,1)S(1)}, u32[]{:S(2)}, u32[]{:S(2)}) collective-permute-start(bf16[7,128,512]{2,1,0:T(8,128)(2,1)S(1)} %collective-permute-done.4.refs_1_), channel_id=1, source_target_pairs={{0,8},{8,0},{1,9},{9,1},{2,10},{10,2},{3,11},{11,3},{4,12},{12,4},... | collective-permute-start | bytes 2752520 | tf_op jit(solution)/shard_map/ppermute | solution.py:110
  64.4 19.8 %collective-permute-start.9 = (bf16[2,128,1024]{2,1,0:T(8,128)(2,1)S(1)}, bf16[2,128,1024]{2,1,0:T(8,128)(2,1)}, u32[]{:S(2)}, u32[]{:S(2)}) collective-permute-start(bf16[2,128,1024]{2,1,0:T(8,128)(2,1)S(1)} %collective-permute-done.7.refs_3_), channel_id=1, source_target_pairs={{0,2},{2,4},{4,6},{6,7},{7,5},{5,3},{3,1},{1,0},{8,10},{10,12},{12... | collective-permute-start | bytes 1572872 | tf_op jit(solution)/shard_map/ppermute | solution.py:110
  86.6 25.4 %collective-permute-start.20 = (bf16[7,128,512]{2,1,0:T(8,128)(2,1)S(1)}, bf16[7,128,512]{2,1,0:T(8,128)(2,1)}, u32[]{:S(2)}, u32[]{:S(2)}) collective-permute-start(bf16[7,128,512]{2,1,0:T(8,128)(2,1)S(1)} %collective-permute-done.5.refs_2_), channel_id=1, source_target_pairs={{2,0},{4,2},{6,4},{7,6},{5,7},{3,5},{1,3},{0,1},{10,8},{12,10},{14... | collective-permute-start | bytes 2752520 | tf_op jit(solution)/shard_map/ppermute | solution.py:110
  87.7 28.7 %collective-permute-start.18 = (bf16[7,128,512]{2,1,0:T(8,128)(2,1)S(1)}, bf16[7,128,512]{2,1,0:T(8,128)(2,1)}, u32[]{:S(2)}, u32[]{:S(2)}) collective-permute-start(bf16[7,128,512]{2,1,0:T(8,128)(2,1)S(1)} %collective-permute-done.4.refs_1_), channel_id=1, source_target_pairs={{0,2},{2,4},{4,6},{6,7},{7,5},{5,3},{3,1},{1,0},{8,10},{10,12},{12... | collective-permute-start | bytes 2752520 | tf_op jit(solution)/shard_map/ppermute | solution.py:110
  89.7 22.3 %collective-permute-start.22 = (bf16[2,128,1024]{2,1,0:T(8,128)(2,1)}, bf16[2,128,1024]{2,1,0:T(8,128)(2,1)S(1)}, u32[]{:S(2)}, u32[]{:S(2)}) collective-permute-start(bf16[2,128,1024]{2,1,0:T(8,128)(2,1)} %copy-done.67), channel_id=1, source_target_pairs={{0,16},{16,0},{1,17},{17,1},{2,18},{18,2},{3,19},{19,3},{4,20},{20... | collective-permute-start | bytes 1572872 | tf_op jit(solution)/shard_map/ppermute | solution.py:110
  106.3 22.0 %collective-permute-start.14 = (bf16[512,1024]{1,0:T(8,128)(2,1)}, bf16[512,1024]{1,0:T(8,128)(2,1)S(1)}, u32[]{:S(2)}, u32[]{:S(2)}) collective-permute-start(bf16[512,1024]{1,0:T(8,128)(2,1)} %get-tuple-element.285), channel_id=1, source_target_pairs={{0,8},{8,0},{1,9},{9,1},{2,10},{10,2},{3,11},{11,3},{4,12},{12,4},... | collective-permute-start | bytes 3145736 | tf_op jit(solution)/shard_map/ppermute | solution.py:321
  117.9 14.8 %collective-permute-start.27 = (bf16[7,128,512]{2,1,0:T(8,128)(2,1)}, bf16[7,128,512]{2,1,0:T(8,128)(2,1)S(1)}, u32[]{:S(2)}, u32[]{:S(2)}) collective-permute-start(bf16[7,128,512]{2,1,0:T(8,128)(2,1)} %collective-permute-done.20.refs_4_), channel_id=1, source_target_pairs={{0,8},{8,0},{1,9},{9,1},{2,10},{10,2},{3,11},{11,3},{4,12},{12,4},... | collective-permute-start | bytes 2752520 | tf_op jit(solution)/shard_map/ppermute | solution.py:110
  126.9 18.9 %collective-permute-start.21 = (bf16[7,128,512]{2,1,0:T(8,128)(2,1)}, bf16[7,128,512]{2,1,0:T(8,128)(2,1)S(1)}, u32[]{:S(2)}, u32[]{:S(2)}) collective-permute-start(bf16[7,128,512]{2,1,0:T(8,128)(2,1)} %collective-permute-done.20.refs_4_), channel_id=1, source_target_pairs={{2,0},{4,2},{6,4},{7,6},{5,7},{3,5},{1,3},{0,1},{10,8},{12,10},{14... | collective-permute-start | bytes 2752520 | tf_op jit(solution)/shard_map/ppermute | solution.py:110
  128.1 18.6 %collective-permute-start.19 = (bf16[7,128,512]{2,1,0:T(8,128)(2,1)}, bf16[7,128,512]{2,1,0:T(8,128)(2,1)}, u32[]{:S(2)}, u32[]{:S(2)}) collective-permute-start(bf16[7,128,512]{2,1,0:T(8,128)(2,1)} %collective-permute-done.18.refs_3_), channel_id=1, source_target_pairs={{0,2},{2,4},{4,6},{6,7},{7,5},{5,3},{3,1},{1,0},{8,10},{10,12},{12... | collective-permute-start | bytes 2752520 | tf_op jit(solution)/shard_map/ppermute | solution.py:110
  128.3 18.4 %collective-permute-start.24 = (bf16[2,128,1024]{2,1,0:T(8,128)(2,1)S(1)}, bf16[2,128,1024]{2,1,0:T(8,128)(2,1)S(1)}, u32[]{:S(2)}, u32[]{:S(2)}) collective-permute-start(bf16[2,128,1024]{2,1,0:T(8,128)(2,1)S(1)} %collective-permute-done.23.refs_3_), channel_id=1, source_target_pairs={{0,16},{16,0},{1,17},{17,1},{2,18},{18,2},{3,19},{19,3},{4,20},{20... | collective-permute-start | bytes 1572872 | tf_op jit(solution)/shard_map/ppermute | solution.py:110
  149.5 18.0 %collective-permute-start.28 = (bf16[256,1024]{1,0:T(8,128)(2,1)S(1)}, bf16[256,1024]{1,0:T(8,128)(2,1)S(1)}, u32[]{:S(2)}, u32[]{:S(2)}) collective-permute-start(bf16[256,1024]{1,0:T(8,128)(2,1)S(1)} %slice.314), channel_id=1, source_target_pairs={{0,16},{16,0},{1,17},{17,1},{2,18},{18,2},{3,19},{19,3},{4,20},{20... | collective-permute-start | bytes 1572872 | tf_op jit(solution)/shard_map/ppermute | solution.py:110
  149.7 29.5 %collective-permute-start.32 = (bf16[7,128,512]{2,1,0:T(8,128)(2,1)S(1)}, bf16[7,128,512]{2,1,0:T(8,128)(2,1)}, u32[]{:S(2)}, u32[]{:S(2)}) collective-permute-start(bf16[7,128,512]{2,1,0:T(8,128)(2,1)S(1)} %collective-permute-done.21.refs_6_), channel_id=1, source_target_pairs={{2,0},{4,2},{6,4},{7,6},{5,7},{3,5},{1,3},{0,1},{10,8},{12,10},{14... | collective-permute-start | bytes 2752520 | tf_op jit(solution)/shard_map/ppermute | solution.py:110
  168.7 25.0 %collective-permute-start.35 = (bf16[7,128,512]{2,1,0:T(8,128)(2,1)S(1)}, bf16[7,128,512]{2,1,0:T(8,128)(2,1)}, u32[]{:S(2)}, u32[]{:S(2)}) collective-permute-start(bf16[7,128,512]{2,1,0:T(8,128)(2,1)S(1)} %collective-permute-done.21.refs_6_), channel_id=1, source_target_pairs={{0,8},{8,0},{1,9},{9,1},{2,10},{10,2},{3,11},{11,3},{4,12},{12,4},... | collective-permute-start | bytes 2752520 | tf_op jit(solution)/shard_map/ppermute | solution.py:110
  179.2 14.5 %collective-permute-start.34 = (bf16[7,128,512]{2,1,0:T(8,128)(2,1)}, bf16[7,128,512]{2,1,0:T(8,128)(2,1)}, u32[]{:S(2)}, u32[]{:S(2)}) collective-permute-start(bf16[7,128,512]{2,1,0:T(8,128)(2,1)} %collective-permute-done.19.refs_5_), channel_id=1, source_target_pairs={{0,8},{8,0},{1,9},{9,1},{2,10},{10,2},{3,11},{11,3},{4,12},{12,4},... | collective-permute-start | bytes 2752520 | tf_op jit(solution)/shard_map/ppermute | solution.py:110
  180.0 22.0 %collective-permute-start.38 = (bf16[7,128,512]{2,1,0:T(8,128)(2,1)}, bf16[7,128,512]{2,1,0:T(8,128)(2,1)}, u32[]{:S(2)}, u32[]{:S(2)}) collective-permute-start(bf16[7,128,512]{2,1,0:T(8,128)(2,1)} %collective-permute-done.32.refs_7_), channel_id=1, source_target_pairs={{0,8},{8,0},{1,9},{9,1},{2,10},{10,2},{3,11},{11,3},{4,12},{12,4},... | collective-permute-start | bytes 2752520 | tf_op jit(solution)/shard_map/ppermute | solution.py:110
  188.1 25.1 %collective-permute-start.39 = (bf16[2,128,1024]{2,1,0:T(8,128)(2,1)}, bf16[2,128,1024]{2,1,0:T(8,128)(2,1)}, u32[]{:S(2)}, u32[]{:S(2)}) collective-permute-start(bf16[2,128,1024]{2,1,0:T(8,128)(2,1)} %collective-permute-done.36.refs_7_), channel_id=1, source_target_pairs={{0,16},{16,0},{1,17},{17,1},{2,18},{18,2},{3,19},{19,3},{4,20},{20... | collective-permute-start | bytes 1572872 | tf_op jit(solution)/shard_map/ppermute | solution.py:110
  280.3 23.8 %collective-permute-start.48 = (bf16[2,1024,256]{2,1,0:T(8,128)(2,1)S(1)}, bf16[2,1024,256]{2,1,0:T(8,128)(2,1)S(1)}, u32[]{:S(2)}, u32[]{:S(2)}) collective-permute-start(bf16[2,1024,256]{2,1,0:T(8,128)(2,1)S(1)} %copy-done.58), channel_id=1, source_target_pairs={{0,16},{16,0},{1,17},{17,1},{2,18},{18,2},{3,19},{19,3},{4,20},{20... | collective-permute-start | bytes 3145736 | tf_op jit(solution)/shard_map/ppermute | solution.py:110
  281.5 16.1 %collective-permute-start.46 = (bf16[8,128,256]{2,1,0:T(8,128)(2,1)}, bf16[8,128,256]{2,1,0:T(8,128)(2,1)S(1)}, u32[]{:S(2)}, u32[]{:S(2)}) collective-permute-start(bf16[8,128,256]{2,1,0:T(8,128)(2,1)} %get-tuple-element.371), channel_id=1, source_target_pairs={{0,2},{2,4},{4,6},{6,7},{7,5},{5,3},{3,1},{1,0},{8,10},{10,12},{12... | collective-permute-start | bytes 1572872 | tf_op jit(solution)/shard_map/ppermute | solution.py:110
  282.9 14.8 %collective-permute-start.47 = (bf16[8,128,256]{2,1,0:T(8,128)(2,1)}, bf16[8,128,256]{2,1,0:T(8,128)(2,1)S(1)}, u32[]{:S(2)}, u32[]{:S(2)}) collective-permute-start(bf16[8,128,256]{2,1,0:T(8,128)(2,1)} %get-tuple-element.372), channel_id=1, source_target_pairs={{2,0},{4,2},{6,4},{7,6},{5,7},{3,5},{1,3},{0,1},{10,8},{12,10},{14... | collective-permute-start | bytes 1572872 | tf_op jit(solution)/shard_map/ppermute | solution.py:110
  307.6 22.9 %collective-permute-start.51 = (bf16[2,1024,256]{2,1,0:T(8,128)(2,1)S(1)}, bf16[2,1024,256]{2,1,0:T(8,128)(2,1)S(1)}, u32[]{:S(2)}, u32[]{:S(2)}) collective-permute-start(bf16[2,1024,256]{2,1,0:T(8,128)(2,1)S(1)} %copy-done.56), channel_id=1, source_target_pairs={{0,16},{16,0},{1,17},{17,1},{2,18},{18,2},{3,19},{19,3},{4,20},{20... | collective-permute-start | bytes 3145736 | tf_op jit(solution)/shard_map/ppermute | solution.py:110
  307.7 22.8 %collective-permute-start.52 = (bf16[2,1,1024,256]{3,2,1,0:T(8,128)(2,1)}, bf16[2,1,1024,256]{3,2,1,0:T(8,128)(2,1)S(1)}, u32[]{:S(2)}, u32[]{:S(2)}) collective-permute-start(bf16[2,1,1024,256]{3,2,1,0:T(8,128)(2,1)} %get-tuple-element.395), channel_id=1, source_target_pairs={{0,8},{8,0},{1,9},{9,1},{2,10},{10,2},{3,11},{11,3},{4,12},{12,4},... | collective-permute-start | bytes 3145736 | tf_op jit(solution)/shard_map/ppermute | solution.py:110
  309.8 19.3 %collective-permute-start.49 = (bf16[8,128,256]{2,1,0:T(8,128)(2,1)}, bf16[8,128,256]{2,1,0:T(8,128)(2,1)S(1)}, u32[]{:S(2)}, u32[]{:S(2)}) collective-permute-start(bf16[8,128,256]{2,1,0:T(8,128)(2,1)} %get-tuple-element.392), channel_id=1, source_target_pairs={{0,2},{2,4},{4,6},{6,7},{7,5},{5,3},{3,1},{1,0},{8,10},{10,12},{12... | collective-permute-start | bytes 1572872 | tf_op jit(solution)/shard_map/ppermute | solution.py:110
  310.4 18.6 %collective-permute-start.50 = (bf16[8,128,256]{2,1,0:T(8,128)(2,1)}, bf16[8,128,256]{2,1,0:T(8,128)(2,1)S(1)}, u32[]{:S(2)}, u32[]{:S(2)}) collective-permute-start(bf16[8,128,256]{2,1,0:T(8,128)(2,1)} %get-tuple-element.393), channel_id=1, source_target_pairs={{2,0},{4,2},{6,4},{7,6},{5,7},{3,5},{1,3},{0,1},{10,8},{12,10},{14... | collective-permute-start | bytes 1572872 | tf_op jit(solution)/shard_map/ppermute | solution.py:110
  335.5 22.4 %collective-permute-start.55 = (bf16[2,2,1024,256]{3,2,1,0:T(8,128)(2,1)}, bf16[2,2,1024,256]{3,2,1,0:T(8,128)(2,1)S(1)}, u32[]{:S(2)}, u32[]{:S(2)}) collective-permute-start(bf16[2,2,1024,256]{3,2,1,0:T(8,128)(2,1)} %get-tuple-element.413), channel_id=1, source_target_pairs={{0,8},{8,0},{1,9},{9,1},{2,10},{10,2},{3,11},{11,3},{4,12},{12,4},... | collective-permute-start | bytes 6291464 | tf_op jit(solution)/shard_map/ppermute | solution.py:110
  338.4 19.6 %collective-permute-start.56 = (bf16[2,1,1024,256]{3,2,1,0:T(8,128)(2,1)S(1)}, bf16[2,1,1024,256]{3,2,1,0:T(8,128)(2,1)S(1)}, u32[]{:S(2)}, u32[]{:S(2)}) collective-permute-start(bf16[2,1,1024,256]{3,2,1,0:T(8,128)(2,1)S(1)} %copy-done.57), channel_id=1, source_target_pairs={{0,8},{8,0},{1,9},{9,1},{2,10},{10,2},{3,11},{11,3},{4,12},{12,4},... | collective-permute-start | bytes 3145736 | tf_op jit(solution)/shard_map/ppermute | solution.py:110
  338.4 19.5 %collective-permute-start.53 = (bf16[12,128,256]{2,1,0:T(8,128)(2,1)}, bf16[12,128,256]{2,1,0:T(8,128)(2,1)S(1)}, u32[]{:S(2)}, u32[]{:S(2)}) collective-permute-start(bf16[12,128,256]{2,1,0:T(8,128)(2,1)} %get-tuple-element.411), channel_id=1, source_target_pairs={{0,2},{2,4},{4,6},{6,7},{7,5},{5,3},{3,1},{1,0},{8,10},{10,12},{12... | collective-permute-start | bytes 2359304 | tf_op jit(solution)/shard_map/ppermute | solution.py:110
  362.2 33.7 %collective-permute-start.61 = (bf16[2,3,1024,256]{3,2,1,0:T(8,128)(2,1)}, bf16[2,3,1024,256]{3,2,1,0:T(8,128)(2,1)}, u32[]{:S(2)}, u32[]{:S(2)}) collective-permute-start(bf16[2,3,1024,256]{3,2,1,0:T(8,128)(2,1)} %get-tuple-element.431), channel_id=1, source_target_pairs={{0,8},{8,0},{1,9},{9,1},{2,10},{10,2},{3,11},{11,3},{4,12},{12,4},... | collective-permute-start | bytes 9437192 | tf_op jit(solution)/shard_map/ppermute | solution.py:110
  405.0 23.5 %collective-permute-start.63 = (bf16[16,128,256]{2,1,0:T(8,128)(2,1)}, bf16[16,128,256]{2,1,0:T(8,128)(2,1)}, u32[]{:S(2)}, u32[]{:S(2)}) collective-permute-start(bf16[16,128,256]{2,1,0:T(8,128)(2,1)} %get-tuple-element.445), channel_id=1, source_target_pairs={{0,2},{2,4},{4,6},{6,7},{7,5},{5,3},{3,1},{1,0},{8,10},{10,12},{12... | collective-permute-start | bytes 3145736 | tf_op jit(solution)/shard_map/ppermute | solution.py:110
  405.0 23.7 %collective-permute-start.64 = (bf16[16,128,256]{2,1,0:T(8,128)(2,1)}, bf16[16,128,256]{2,1,0:T(8,128)(2,1)}, u32[]{:S(2)}, u32[]{:S(2)}) collective-permute-start(bf16[16,128,256]{2,1,0:T(8,128)(2,1)} %get-tuple-element.446), channel_id=1, source_target_pairs={{2,0},{4,2},{6,4},{7,6},{5,7},{3,5},{1,3},{0,1},{10,8},{12,10},{14... | collective-permute-start | bytes 3145736 | tf_op jit(solution)/shard_map/ppermute | solution.py:110
  406.7 23.0 %collective-permute-start.65 = (bf16[2,1024,256]{2,1,0:T(8,128)(2,1)}, bf16[2,1024,256]{2,1,0:T(8,128)(2,1)}, u32[]{:S(2)}, u32[]{:S(2)}) collective-permute-start(bf16[2,1024,256]{2,1,0:T(8,128)(2,1)} %slice_bitcast_fusion), channel_id=1, source_target_pairs={{0,16},{16,0},{1,17},{17,1},{2,18},{18,2},{3,19},{19,3},{4,20},{20... | collective-permute-start | bytes 3145736 | tf_op jit(solution)/shard_map/ppermute | solution.py:110
  440.5 34.8 %collective-permute-start.67 = (bf16[23,128,256]{2,1,0:T(8,128)(2,1)}, bf16[23,128,256]{2,1,0:T(8,128)(2,1)S(1)}, u32[]{:S(2)}, u32[]{:S(2)}) collective-permute-start(bf16[23,128,256]{2,1,0:T(8,128)(2,1)} %get-tuple-element.458), channel_id=1, source_target_pairs={{2,0},{4,2},{6,4},{7,6},{5,7},{3,5},{1,3},{0,1},{10,8},{12,10},{14... | collective-permute-start | bytes 4521992 | tf_op jit(solution)/shard_map/ppermute | solution.py:110
  441.9 28.9 %collective-permute-start.66 = (bf16[19,128,256]{2,1,0:T(8,128)(2,1)}, bf16[19,128,256]{2,1,0:T(8,128)(2,1)}, u32[]{:S(2)}, u32[]{:S(2)}) collective-permute-start(bf16[19,128,256]{2,1,0:T(8,128)(2,1)} %get-tuple-element.457), channel_id=1, source_target_pairs={{0,2},{2,4},{4,6},{6,7},{7,5},{5,3},{3,1},{1,0},{8,10},{10,12},{12... | collective-permute-start | bytes 3735560 | tf_op jit(solution)/shard_map/ppermute | solution.py:110
  445.0 30.3 %collective-permute-start.69 = (bf16[256,1024]{1,0:T(8,128)(2,1)}, bf16[256,1024]{1,0:T(8,128)(2,1)}, u32[]{:S(2)}, u32[]{:S(2)}) collective-permute-start(bf16[256,1024]{1,0:T(8,128)(2,1)} %slice.313), channel_id=1, source_target_pairs={{0,16},{16,0},{1,17},{17,1},{2,18},{18,2},{3,19},{19,3},{4,20},{20... | collective-permute-start | bytes 1572872 | tf_op jit(solution)/shard_map/ppermute | solution.py:110
  481.3 28.4 %collective-permute-start.71 = (bf16[19,128,256]{2,1,0:T(8,128)(2,1)}, bf16[19,128,256]{2,1,0:T(8,128)(2,1)S(1)}, u32[]{:S(2)}, u32[]{:S(2)}) collective-permute-start(bf16[19,128,256]{2,1,0:T(8,128)(2,1)} %get-tuple-element.473), channel_id=1, source_target_pairs={{0,2},{2,4},{4,6},{6,7},{7,5},{5,3},{3,1},{1,0},{8,10},{10,12},{12... | collective-permute-start | bytes 3735560 | tf_op jit(solution)/shard_map/ppermute | solution.py:110
  481.4 28.4 %collective-permute-start.72 = (bf16[19,128,256]{2,1,0:T(8,128)(2,1)}, bf16[19,128,256]{2,1,0:T(8,128)(2,1)}, u32[]{:S(2)}, u32[]{:S(2)}) collective-permute-start(bf16[19,128,256]{2,1,0:T(8,128)(2,1)} %get-tuple-element.474), channel_id=1, source_target_pairs={{2,0},{4,2},{6,4},{7,6},{5,7},{3,5},{1,3},{0,1},{10,8},{12,10},{14... | collective-permute-start | bytes 3735560 | tf_op jit(solution)/shard_map/ppermute | solution.py:110
  514.8 21.9 %collective-permute-start.76 = (bf16[15,128,256]{2,1,0:T(8,128)(2,1)}, bf16[15,128,256]{2,1,0:T(8,128)(2,1)S(1)}, u32[]{:S(2)}, u32[]{:S(2)}) collective-permute-start(bf16[15,128,256]{2,1,0:T(8,128)(2,1)} %get-tuple-element.480), channel_id=1, source_target_pairs={{2,0},{4,2},{6,4},{7,6},{5,7},{3,5},{1,3},{0,1},{10,8},{12,10},{14... | collective-permute-start | bytes 2949128 | tf_op jit(solution)/shard_map/ppermute | solution.py:110
  516.3 15.9 %collective-permute-start.75 = (bf16[11,128,256]{2,1,0:T(8,128)(2,1)}, bf16[11,128,256]{2,1,0:T(8,128)(2,1)S(1)}, u32[]{:S(2)}, u32[]{:S(2)}) collective-permute-start(bf16[11,128,256]{2,1,0:T(8,128)(2,1)} %get-tuple-element.479), channel_id=1, source_target_pairs={{0,2},{2,4},{4,6},{6,7},{7,5},{5,3},{3,1},{1,0},{8,10},{10,12},{12... | collective-permute-start | bytes 2162696 | tf_op jit(solution)/shard_map/ppermute | solution.py:110
  570.7 41.5 %all-to-all-start = ((bf16[8,3,128,256]{3,2,1,0:T(8,128)(2,1)}), bf16[8,3,128,256]{3,2,1,0:T(8,128)(2,1)}, u32[]{:S(2)}, u32[]{:S(2)}) async-start(bf16[8,3,128,256]{3,2,1,0:T(8,128)(2,1)} %bitcast.369), calls=%async_computation | async-start | bytes 3145728 | tf_op jit(solution)/shard_map/all_to_all | solution.py:1372
  623.2 20.2 %collective-permute-start.86 = (f32[34,1024]{1,0:T(8,128)S(1)}, f32[34,1024]{1,0:T(8,128)S(1)}, u32[]{:S(2)}, u32[]{:S(2)}) collective-permute-start(f32[34,1024]{1,0:T(8,128)S(1)} %add.722), channel_id=1, source_target_pairs={{0,4},{1,5},{2,6},{3,7},{4,0},{5,1},{6,2},{7,3},{8,12},{9,13},{10,... | collective-permute-start | bytes 417800 | tf_op jit(solution)/shard_map/ppermute | solution.py:110
  651.4 26.9 %collective-permute-start.95 = (bf16[256,1024]{1,0:T(8,128)(2,1)}, bf16[256,1024]{1,0:T(8,128)(2,1)}, u32[]{:S(2)}, u32[]{:S(2)}) collective-permute-start(bf16[256,1024]{1,0:T(8,128)(2,1)} %fusion.49), channel_id=1, source_target_pairs={{0,16},{16,0},{1,17},{17,1},{2,18},{18,2},{3,19},{19,3},{4,20},{20... | collective-permute-start | bytes 1572872 | tf_op jit(solution)/shard_map/ppermute | solution.py:327
  660.6 24.7 %collective-permute-start.94 = (bf16[2,256,1024]{2,1,0:T(8,128)(2,1)}, bf16[2,256,1024]{2,1,0:T(8,128)(2,1)}, u32[]{:S(2)}, u32[]{:S(2)}) collective-permute-start(bf16[2,256,1024]{2,1,0:T(8,128)(2,1)} %pad_maximum_fusion.9), channel_id=1, source_target_pairs={{0,8},{8,0},{1,9},{9,1},{2,10},{10,2},{3,11},{11,3},{4,12},{12,4},... | collective-permute-start | bytes 3145736 | tf_op jit(solution)/shard_map/ppermute | solution.py:327
  (132 other events, 1471.7 us)

commit v4 on v3

--- a/solution.py
+++ b/solution.py
@@ -1053,7 +1053,7 @@
     def sides_of(gather, other):
         return [values(gather.pieces)] + ([values(other)] if other else [])
 
-    bind(after_first, *[cell for past in wires.past[-4:] for cell in past])
+    bind(after_first, *wires.past[-1])
     after_attn, attn_normed, queries, keys, values_, mixed = panel_call(
         attention_forward_kernel,
         "attention_forward",
@@ -1067,7 +1067,7 @@
         8 * tokens * width * width,
     )
     after_attn = Cell(after_attn)
-    bind(after_attn, *came)
+    bind(after_attn, *came, *[cell for past in wires.past[-4:-1] for cell in past])
     came = []
     while to_chip.next < len(second.pieces):
         came += wires.start(to_chip.more(2), after=[after_attn])

time: 709 us -> 709 us (level)
  transfers between devices with their start and end apart: 100 -> 100, of which waited for: 51 -> 48; matrix products, arithmetic and copies ran while one was open for 14% -> 14% of each run, Pallas kernels for 13% -> 13%
where the time goes in v4:
time: 709 us; the launch traced here: 699 us
  waiting for transfers between devices  262 us (37%)
  Pallas kernels  166 us (23%)
  starting transfers between devices  121 us (17%)
  other arithmetic  81.4 us (11%)
  local copies, waits for them, and re-layouts  34.8 us (5%)
  matrix products  30.3 us (4%)
    ppermute x75, waiting for transfers between devices, start(): came.append(Cell(lax.ppermute(value, axis, pairs)))  216 us
    ppermute x75, starting transfers between devices, start(): came.append(Cell(lax.ppermute(value, axis, pairs)))  84 us
    pallas_call x6, Pallas kernels, panel_call(): pl.pallas_call(functools.partial(kernel, count), out_shape=outs, in_specs...  52.8 us
    pallas_call x4, Pallas kernels, ffn_backward_call(): pl.pallas_call(functools.partial(kernel, count, halves, bias, (outer, way...  42.9 us
    pallas_call x10, Pallas kernels, hop_together(): pl.pallas_call(functools.partial(hop_kernel, tuple(plan), (len(inputs), l...  36.3 us
    ppermute x10, starting transfers between devices, swap_cores(): return lax.ppermute(values, 'c', SWAP)  19.6 us
    all_to_all x1, waiting for transfers between devices, on_device(): lax.all_to_all(outgoing, 'f', split_axis=0, concat_axis=0, tiled=True)  19.1 us
    pallas_call x2, Pallas kernels, ffn_forward_call(): pl.pallas_call(functools.partial(ffn_forward_kernel, count, halves), out_...  19 us
  transfers between devices with their start and end apart: 100, of which 48 were waited for; matrix products, arithmetic and copies ran while one was open for 14% of the time, Pallas kernels for 13%

profile of v4, /device:TPU:1, one launch (start us, length us, event | category | flops | bytes accessed | tf_op | source)
XLA Modules:
  0.0 699.5 jit_solution(4726225587930888943)
XLA Ops:
  15.8 7.5 %collective-permute-done.refs_1_ = bf16[2,128,1024]{2,1,0:T(8,128)(2,1)S(1)} collective-permute-done((bf16[2,128,1024]{2,1,0:T(8,128)(2,1)S(1)}, bf16[2,128,1024]{2,1,0:T(8,128)(2,1)S(1)}, u32[]{:S(2)}, u32[]{:S(2)}) %collective-permute-start) | collective-permute-done | bytes 524320 | tf_op jit(solution)/shard_map/ppermute | solution.py:110
  31.9 8.3 %convert_element_type.214 = bf16[3,1024,1024]{2,1,0:T(8,128)(2,1)} convert(f32[3,1024,1024]{2,1,0:T(8,128)} %param.21) | non-fusion elementwise | flops 3145728 | bytes 18874368 | tf_op jit(solution)/shard_map/convert_element_type | solution.py:999
  40.2 8.2 %convert_element_type.215 = bf16[3,1024,1024]{2,1,0:T(8,128)(2,1)} convert(f32[3,1024,1024]{2,1,0:T(8,128)} %param.22) | non-fusion elementwise | flops 3145728 | bytes 18874368 | tf_op jit(solution)/shard_map/convert_element_type | solution.py:1000
  52.8 8.8 %collective-permute-done.7.refs_3_ = bf16[2,128,1024]{2,1,0:T(8,128)(2,1)S(1)} collective-permute-done((bf16[2,128,1024]{2,1,0:T(8,128)(2,1)}, bf16[2,128,1024]{2,1,0:T(8,128)(2,1)S(1)}, u32[]{:S(2)}, u32[]{:S(2)}) %collective-permute-start.7) | collective-permute-done | bytes 524320 | tf_op jit(solution)/shard_map/ppermute | solution.py:110
  65.5 7.3 %collective-permute-done.11.refs_1_ = bf16[2,128,1024]{2,1,0:T(8,128)(2,1)S(1)} collective-permute-done((bf16[2,128,1024]{2,1,0:T(8,128)(2,1)S(1)}, bf16[2,128,1024]{2,1,0:T(8,128)(2,1)S(1)}, u32[]{:S(2)}, u32[]{:S(2)}) %collective-permute-start.11) | collective-permute-done | bytes 524320 | tf_op jit(solution)/shard_map/ppermute | solution.py:110
  75.4 8.8 %collective-permute-done.9.refs_5_ = bf16[2,128,1024]{2,1,0:T(8,128)(2,1)} collective-permute-done((bf16[2,128,1024]{2,1,0:T(8,128)(2,1)S(1)}, bf16[2,128,1024]{2,1,0:T(8,128)(2,1)}, u32[]{:S(2)}, u32[]{:S(2)}) %collective-permute-start.9) | collective-permute-done | bytes 524320 | tf_op jit(solution)/shard_map/ppermute | solution.py:110
  90.9 5.8 collective-permute-done.13.refs_7_
  96.8 9.5 %ffn_forward.2 = (f32[1,1024,1024]{2,1,0:T(8,128)}, bf16[1,1024,1024]{2,1,0:T(8,128)(2,1)}, f32[512,1024]{1,0:T(8,128)}, bf16[512,1024]{1,0:T(8,128)(2,1)}) custom-call(s32[9]{0:T(128)} %concatenate.74.meta, bf16[1024,1024]{1,0:T(8,128)(2,1)} %pad_maximum_fusion.4.normed, f32[1,1,1024]{2,1,0:T(1,128)} %get-tuple-element.282.bias, ...), custom_call_target="tpu_custom_call" | custom-call | flops 4294967296 | bytes 27262976 | tf_op jit(solution)/shard_map/ffn_forward/pallas_call | solution.py:416
  106.3 5.7 collective-permute-start.14
  112.0 4.4 collective-permute-done.18.refs_3_
  121.5 5.4 collective-permute-done.25.refs_4_
  132.7 13.0 %collective-permute-done.21.refs_6_ = bf16[7,128,512]{2,1,0:T(8,128)(2,1)S(1)} collective-permute-done((bf16[7,128,512]{2,1,0:T(8,128)(2,1)}, bf16[7,128,512]{2,1,0:T(8,128)(2,1)S(1)}, u32[]{:S(2)}, u32[]{:S(2)}) %collective-permute-start.21) | collective-permute-done | bytes 917536 | tf_op jit(solution)/shard_map/ppermute | solution.py:110
  151.0 6.6 collective-permute-done.29.refs_5_
  157.7 9.8 %collective-permute-done.28 = bf16[256,1024]{1,0:T(8,128)(2,1)S(1)} collective-permute-done((bf16[256,1024]{1,0:T(8,128)(2,1)S(1)}, bf16[256,1024]{1,0:T(8,128)(2,1)S(1)}, u32[]{:S(2)}, u32[]{:S(2)}) %collective-permute-start.28) | collective-permute-done | bytes 524320 | tf_op jit(solution)/shard_map/ppermute | solution.py:110
  168.7 10.5 %collective-permute-start.36 = (bf16[7,128,512]{2,1,0:T(8,128)(2,1)S(1)}, bf16[7,128,512]{2,1,0:T(8,128)(2,1)}, u32[]{:S(2)}, u32[]{:S(2)}) collective-permute-start(bf16[7,128,512]{2,1,0:T(8,128)(2,1)S(1)} %collective-permute-done.21.refs_6_), channel_id=1, source_target_pairs={{0,8},{8,0},{1,9},{9,1},{2,10},{10,2},{3,11},{11,3},{4,12},{12,4},... | collective-permute-start | bytes 2752520 | tf_op jit(solution)/shard_map/ppermute | solution.py:110
  180.0 8.1 %collective-permute-start.37 = (bf16[7,128,512]{2,1,0:T(8,128)(2,1)}, bf16[7,128,512]{2,1,0:T(8,128)(2,1)}, u32[]{:S(2)}, u32[]{:S(2)}) collective-permute-start(bf16[7,128,512]{2,1,0:T(8,128)(2,1)} %collective-permute-done.34.refs_7_), channel_id=1, source_target_pairs={{0,8},{8,0},{1,9},{9,1},{2,10},{10,2},{3,11},{11,3},{4,12},{12,4},... | collective-permute-start | bytes 2752520 | tf_op jit(solution)/shard_map/ppermute | solution.py:110
  193.7 9.5 %attention_forward.1 = (f32[256,1024]{1,0:T(8,128)}, bf16[256,1024]{1,0:T(8,128)(2,1)}, bf16[256,1024]{1,0:T(8,128)(2,1)}, bf16[256,1024]{1,0:T(8,128)(2,1)}, bf...) custom-call(s32[10]{0:T(128)} %concatenate.71.meta, f32[256,1024]{1,0:T(8,128)} %multiply_add_fusion.3.stream, ...), custom_call_target="tpu_custom_call" | custom-call | flops 2147483648 | bytes 16777216 | tf_op jit(solution)/shard_map/attention_forward/pallas_call | solution.py:906
  203.2 10.0 %collective-permute-done.38.refs_15_ = bf16[2,128,1024]{2,1,0:T(8,128)(2,1)} collective-permute-done((bf16[2,128,1024]{2,1,0:T(8,128)(2,1)}, bf16[2,128,1024]{2,1,0:T(8,128)(2,1)}, u32[]{:S(2)}, u32[]{:S(2)}) %collective-permute-start.38) | collective-permute-done | bytes 524320 | tf_op jit(solution)/shard_map/ppermute | solution.py:110
  213.2 8.1 %conv_forward.1 = (f32[256,1024]{1,0:T(8,128)}, bf16[256,1024]{1,0:T(8,128)(2,1)}, f32[2,256,1024]{2,1,0:T(8,128)}, bf16[256,1024]{1,0:T(8,128)(2,1)}, bf16[256,1024]{1,0:T(8,128)(2,1)}) custom-call(s32[10]{0:T(128)} %concatenate.71.meta, f32[256,1024]{1,0:T(8,128)} %get-tuple-element.319.stream, f32[34,1024]{1,0:T(8,128)} %rows.15, ...), custom_call_target="tpu_custom_call" | custom-call | flops 1610612736 | bytes 14680064 | tf_op jit(solution)/shard_map/conv_forward/pallas_call | solution.py:906
  225.0 9.5 %ffn_forward.3 = (f32[2,512,1024]{2,1,0:T(8,128)}, bf16[2,512,1024]{2,1,0:T(8,128)(2,1)}, f32[256,1024]{1,0:T(8,128)}, bf16[256,1024]{1,0:T(8,128)(2,1)}) custom-call(s32[9]{0:T(128)} %concatenate.74.meta, bf16[512,1024]{1,0:T(8,128)(2,1)} %copy-done.51, f32[2,1,1024]{2,1,0:T(1,128)} %broadcast_in_dim.25.bias, ...), custom_call_target="tpu_custom_call" | custom-call | flops 4294967296 | bytes 17825792 | tf_op jit(solution)/shard_map/ffn_forward/pallas_call | solution.py:416
  237.5 4.6 turn.1
  246.3 12.7 %ffn_out_backward.2 = (bf16[2,512,1024]{2,1,0:T(8,128)(2,1)}, f32[34,1024]{1,0:T(8,128)}, bf16[2,2,2,1024,256]{4,3,2,1,0:T(8,128)(2,1)}) custom-call(s32[11]{0:T(128)} %concatenate.79.meta, f32[2,512,1024]{2,1,0:T(8,128)} %get-tuple-element.341.hidden, bf16[2,512,1024]{2,1,0:T(8,128)(2,1)} %get-tuple-element.342.active, ...), custom_call_target="tpu_custom_call" | custom-call | flops 4294967296 | bytes 16777216 | tf_op jit(solution)/shard_map/ffn_out_backward/pallas_call | solution.py:509
  263.7 9.5 %ffn_in_backward.2 = (f32[256,1024]{1,0:T(8,128)}, bf16[256,1024]{1,0:T(8,128)(2,1)}, bf16[2,2,1024,256]{3,2,1,0:T(8,128)(2,1)}, bf16[2,1024,256]{2,1,0:T(8,128)(2,1)}, bf16[2,1024,256]{2,1,0:T(8,128)(2,1)}) custom-call(s32[11]{0:T(128)} %concatenate.79.meta, bf16[512,1024]{1,0:T(8,128)(2,1)} %copy-done.51, bf16[2,512,1024]{2,1,0:T(8,128)(2,1)} %get-tuple-element.349.low, ...), custom_call_target="tpu_custom_call" | custom-call | flops 4294967296 | bytes 16777216 | tf_op jit(solution)/shard_map/ffn_in_backward/pallas_call | solution.py:509
  288.8 8.9 %conv_out_backward.1 = (bf16[2,256,1024]{2,1,0:T(8,128)(2,1)}, bf16[2,1,1024,256]{3,2,1,0:T(8,128)(2,1)}, bf16[2,1,1024,256]{3,2,1,0:T(8,128)(2,1)}, f32[34,1024]{1,0:T(8,128)}) custom-call(s32[10]{0:T(128)} %concatenate.71.meta, f32[256,1024]{1,0:T(8,128)} %get-tuple-element.366.grad, f32[2,256,1024]{2,1,0:T(8,128)} %get-tuple-element.367.wide, ...), custom_call_target="tpu_custom_call" | custom-call | flops 1073741824 | bytes 10485760 | tf_op jit(solution)/shard_map/conv_out_backward/pallas_call | solution.py:906
  297.7 6.4 collective-permute-done.48
  312.1 7.1 %conv_in_backward.1 = (f32[256,1024]{1,0:T(8,128)}, bf16[2,2,1024,256]{3,2,1,0:T(8,128)(2,1)}, bf16[2,2,1024,256]{3,2,1,0:T(8,128)(2,1)}, f32[34,1024]{1,0:T(8,128)}) custom-call(s32[10]{0:T(128)} %concatenate.71.meta, f32[256,1024]{1,0:T(8,128)} %get-tuple-element.366.grad, f32[256,1024]{1,0:T(8,128)} %get-tuple-element.319.stream, ...), custom_call_target="tpu_custom_call" | custom-call | flops 2147483648 | bytes 12582912 | tf_op jit(solution)/shard_map/conv_in_backward/pallas_call | solution.py:906
  319.3 9.7 %attention_heads_backward.1 = (bf16[3,256,1024]{2,1,0:T(8,128)(2,1)}, bf16[2,1,1024,256]{3,2,1,0:T(8,128)(2,1)}, bf16[2,1,1024,256]{3,2,1,0:T(8,128)(2,1)}, f32[34,1024]{1,0:T(8,128)}) custom-call(s32[10]{0:T(128)} %concatenate.71.meta, f32[256,1024]{1,0:T(8,128)} %get-tuple-element.385.grad, bf16[256,1024]{1,0:T(8,128)(2,1)} %get-tuple-element.386.queries, ...), custom_call_target="tpu_custom_call" | custom-call | flops 1610612736 | bytes 10485760 | tf_op jit(solution)/shard_map/attention_heads_backward/pallas_call | solution.py:906
  340.8 9.4 %attention_in_backward.1 = (f32[256,1024]{1,0:T(8,128)}, bf16[2,3,1024,256]{3,2,1,0:T(8,128)(2,1)}, bf16[2,3,1024,256]{3,2,1,0:T(8,128)(2,1)}, f32[34,1024]{1,0:T(8,128)}, bf16[256,1024]{1,0:T(8,128)(2,1)}) custom-call(s32[10]{0:T(128)} %concatenate.71.meta, f32[256,1024]{1,0:T(8,128)} %get-tuple-element.385.grad, f32[256,1024]{1,0:T(8,128)} %multiply_add_fusion.3.stream, ...), custom_call_target="tpu_custom_call" | custom-call | flops 3221225472 | bytes 14680064 | tf_op jit(solution)/shard_map/attention_in_backward/pallas_call | solution.py:906
  350.3 7.6 %collective-permute-done.53.refs_1_ = bf16[12,128,256]{2,1,0:T(8,128)(2,1)S(1)} collective-permute-done((bf16[12,128,256]{2,1,0:T(8,128)(2,1)}, bf16[12,128,256]{2,1,0:T(8,128)(2,1)S(1)}, u32[]{:S(2)}, u32[]{:S(2)}) %collective-permute-start.53) | collective-permute-done | bytes 786464 | tf_op jit(solution)/shard_map/ppermute | solution.py:110
  365.6 11.1 %collective-permute-done.57 = bf16[256,1024]{1,0:T(8,128)(2,1)S(1)} collective-permute-done((bf16[256,1024]{1,0:T(8,128)(2,1)S(1)}, bf16[256,1024]{1,0:T(8,128)(2,1)S(1)}, u32[]{:S(2)}, u32[]{:S(2)}) %collective-permute-start.57) | collective-permute-done | bytes 524320 | tf_op jit(solution)/shard_map/ppermute | solution.py:110
  384.4 11.4 %ffn_out_backward.3 = (bf16[1,1024,1024]{2,1,0:T(8,128)(2,1)}, f32[34,1024]{1,0:T(8,128)}, bf16[2,2,1,1024,256]{4,3,2,1,0:T(8,128)(2,1)}) custom-call(s32[11]{0:T(128)} %concatenate.79.meta, f32[1,1024,1024]{2,1,0:T(8,128)} %get-tuple-element.407.hidden, bf16[1,1024,1024]{2,1,0:T(8,128)(2,1)} %get-tuple-element.408.active, ...), custom_call_target="tpu_custom_call" | custom-call | flops 4294967296 | bytes 25165824 | tf_op jit(solution)/shard_map/ffn_out_backward/pallas_call | solution.py:509
  408.7 9.4 %ffn_in_backward.3 = (f32[512,1024]{1,0:T(8,128)}, bf16[512,1024]{1,0:T(8,128)(2,1)}, bf16[2,2,1,1024,256]{4,3,2,1,0:T(8,128)(2,1)}) custom-call(s32[11]{0:T(128)} %concatenate.79.meta, bf16[1024,1024]{1,0:T(8,128)(2,1)} %pad_maximum_fusion.4.normed, bf16[1,1024,1024]{2,1,0:T(8,128)(2,1)} %get-tuple-element.442.low, bf16[2,128,1024]{2,1,0:T(8,128)(2,1)} %copy-done.41, ...), custom_call_target="tpu_custom_call" | custom-call | flops 4294967296 | bytes 25165824 | tf_op jit(solution)/shard_map/ffn_in_backward/pallas_call | solution.py:509
  418.1 10.4 %collective-permute-done.63.refs_5_ = bf16[16,128,256]{2,1,0:T(8,128)(2,1)} collective-permute-done((bf16[16,128,256]{2,1,0:T(8,128)(2,1)}, bf16[16,128,256]{2,1,0:T(8,128)(2,1)}, u32[]{:S(2)}, u32[]{:S(2)}) %collective-permute-start.63) | collective-permute-done | bytes 1048608 | tf_op jit(solution)/shard_map/ppermute | solution.py:110
  432.4 5.1 hop.16
  448.4 22.4 %collective-permute-done.66.refs_4_ = bf16[19,128,256]{2,1,0:T(8,128)(2,1)} collective-permute-done((bf16[19,128,256]{2,1,0:T(8,128)(2,1)}, bf16[19,128,256]{2,1,0:T(8,128)(2,1)}, u32[]{:S(2)}, u32[]{:S(2)}) %collective-permute-start.66) | collective-permute-done | bytes 1245216 | tf_op jit(solution)/shard_map/ppermute | solution.py:110
  470.8 4.5 collective-permute-done.67.refs_5_
  476.4 5.0 hop.17
  489.4 20.4 %collective-permute-done.71.refs_4_ = bf16[19,128,256]{2,1,0:T(8,128)(2,1)S(1)} collective-permute-done((bf16[19,128,256]{2,1,0:T(8,128)(2,1)}, bf16[19,128,256]{2,1,0:T(8,128)(2,1)S(1)}, u32[]{:S(2)}, u32[]{:S(2)}) %collective-permute-start.71) | collective-permute-done | bytes 1245216 | tf_op jit(solution)/shard_map/ppermute | solution.py:110
  522.7 9.4 %collective-permute-done.75.refs_3_ = bf16[11,128,256]{2,1,0:T(8,128)(2,1)S(1)} collective-permute-done((bf16[11,128,256]{2,1,0:T(8,128)(2,1)}, bf16[11,128,256]{2,1,0:T(8,128)(2,1)S(1)}, u32[]{:S(2)}, u32[]{:S(2)}) %collective-permute-start.75) | collective-permute-done | bytes 720928 | tf_op jit(solution)/shard_map/ppermute | solution.py:110
  532.2 4.5 collective-permute-done.76.refs_4_
  554.0 6.7 collective-permute-done.80
  570.7 5.1 all-to-all-start
  577.7 5.5 collective-permute-done.83
  585.8 7.3 %collective-permute-done.84 = f32[34,1024]{1,0:T(8,128)S(1)} collective-permute-done((f32[34,1024]{1,0:T(8,128)S(1)}, f32[34,1024]{1,0:T(8,128)S(1)}, u32[]{:S(2)}, u32[]{:S(2)}) %collective-permute-start.84) | collective-permute-done | bytes 139296 | tf_op jit(solution)/shard_map/ppermute | solution.py:110
  593.1 19.1 %all-to-all-done = bf16[8,3,128,256]{3,2,1,0:T(8,128)(2,1)} async-done(((bf16[8,3,128,256]{3,2,1,0:T(8,128)(2,1)}), bf16[8,3,128,256]{3,2,1,0:T(8,128)(2,1)}, u32[]{:S(2)}, u32[]{:S(2)}) %all-to-all-start) | async-done | bytes 1572896 | tf_op jit(solution)/shard_map/all_to_all | solution.py:1372
  628.4 5.5 collective-permute-done.91
  636.6 4.3 fusion.43
  653.5 4.8 collective-permute-done.93
  (487 shorter events, 283.5 us)
Async XLA Ops:
  28.4 22.8 %collective-permute-start.4 = (bf16[7,128,512]{2,1,0:T(8,128)(2,1)S(1)}, bf16[7,128,512]{2,1,0:T(8,128)(2,1)S(1)}, u32[]{:S(2)}, u32[]{:S(2)}) collective-permute-start(bf16[7,128,512]{2,1,0:T(8,128)(2,1)S(1)} %constant_dynamic-slice_fusion.3.refs_0_), channel_id=1, source_target_pairs={{0,2},{2,4},{4,6},{6,7},{7,5},{5,3},{3,1},{1,0},{8,10},{10,12},{12... | collective-permute-start | bytes 2752520 | tf_op jit(solution)/shard_map/ppermute | solution.py:110
  29.8 21.7 %collective-permute-start.5 = (bf16[7,128,512]{2,1,0:T(8,128)(2,1)S(1)}, bf16[7,128,512]{2,1,0:T(8,128)(2,1)S(1)}, u32[]{:S(2)}, u32[]{:S(2)}) collective-permute-start(bf16[7,128,512]{2,1,0:T(8,128)(2,1)S(1)} %constant_dynamic-slice_fusion.3.refs_0_), channel_id=1, source_target_pairs={{2,0},{4,2},{6,4},{7,6},{5,7},{3,5},{1,3},{0,1},{10,8},{12,10},{14... | collective-permute-start | bytes 2752520 | tf_op jit(solution)/shard_map/ppermute | solution.py:110
  29.9 21.6 %collective-permute-start.6 = (bf16[7,128,512]{2,1,0:T(8,128)(2,1)S(1)}, bf16[7,128,512]{2,1,0:T(8,128)(2,1)S(1)}, u32[]{:S(2)}, u32[]{:S(2)}) collective-permute-start(bf16[7,128,512]{2,1,0:T(8,128)(2,1)S(1)} %constant_dynamic-slice_fusion.3.refs_0_), channel_id=1, source_target_pairs={{0,8},{8,0},{1,9},{9,1},{2,10},{10,2},{3,11},{11,3},{4,12},{12,4},... | collective-permute-start | bytes 2752520 | tf_op jit(solution)/shard_map/ppermute | solution.py:110
  30.5 31.2 %collective-permute-start.7 = (bf16[2,128,1024]{2,1,0:T(8,128)(2,1)}, bf16[2,128,1024]{2,1,0:T(8,128)(2,1)S(1)}, u32[]{:S(2)}, u32[]{:S(2)}) collective-permute-start(bf16[2,128,1024]{2,1,0:T(8,128)(2,1)} %copy-done.60), channel_id=1, source_target_pairs={{0,2},{2,4},{4,6},{6,7},{7,5},{5,3},{3,1},{1,0},{8,10},{10,12},{12... | collective-permute-start | bytes 1572872 | tf_op jit(solution)/shard_map/ppermute | solution.py:110
  31.8 30.9 %collective-permute-start.8 = (bf16[2,128,1024]{2,1,0:T(8,128)(2,1)}, bf16[2,128,1024]{2,1,0:T(8,128)(2,1)S(1)}, u32[]{:S(2)}, u32[]{:S(2)}) collective-permute-start(bf16[2,128,1024]{2,1,0:T(8,128)(2,1)} %collective-permute-done.1.refs_2_), channel_id=1, source_target_pairs={{2,0},{4,2},{6,4},{7,6},{5,7},{3,5},{1,3},{0,1},{10,8},{12,10},{14... | collective-permute-start | bytes 1572872 | tf_op jit(solution)/shard_map/ppermute | solution.py:110
  51.5 21.4 %collective-permute-start.11 = (bf16[2,128,1024]{2,1,0:T(8,128)(2,1)S(1)}, bf16[2,128,1024]{2,1,0:T(8,128)(2,1)S(1)}, u32[]{:S(2)}, u32[]{:S(2)}) collective-permute-start(bf16[2,128,1024]{2,1,0:T(8,128)(2,1)S(1)} %copy-done.42), channel_id=1, source_target_pairs={{0,2},{2,4},{4,6},{6,7},{7,5},{5,3},{3,1},{1,0},{8,10},{10,12},{12... | collective-permute-start | bytes 1572872 | tf_op jit(solution)/shard_map/ppermute | solution.py:110
  63.0 23.6 %collective-permute-start.17 = (bf16[7,128,512]{2,1,0:T(8,128)(2,1)S(1)}, bf16[7,128,512]{2,1,0:T(8,128)(2,1)S(1)}, u32[]{:S(2)}, u32[]{:S(2)}) collective-permute-start(bf16[7,128,512]{2,1,0:T(8,128)(2,1)S(1)} %collective-permute-done.5.refs_2_), channel_id=1, source_target_pairs={{0,8},{8,0},{1,9},{9,1},{2,10},{10,2},{3,11},{11,3},{4,12},{12,4},... | collective-permute-start | bytes 2752520 | tf_op jit(solution)/shard_map/ppermute | solution.py:110
  64.4 22.2 %collective-permute-start.16 = (bf16[7,128,512]{2,1,0:T(8,128)(2,1)S(1)}, bf16[7,128,512]{2,1,0:T(8,128)(2,1)S(1)}, u32[]{:S(2)}, u32[]{:S(2)}) collective-permute-start(bf16[7,128,512]{2,1,0:T(8,128)(2,1)S(1)} %collective-permute-done.4.refs_1_), channel_id=1, source_target_pairs={{0,8},{8,0},{1,9},{9,1},{2,10},{10,2},{3,11},{11,3},{4,12},{12,4},... | collective-permute-start | bytes 2752520 | tf_op jit(solution)/shard_map/ppermute | solution.py:110
  64.4 19.8 %collective-permute-start.9 = (bf16[2,128,1024]{2,1,0:T(8,128)(2,1)S(1)}, bf16[2,128,1024]{2,1,0:T(8,128)(2,1)}, u32[]{:S(2)}, u32[]{:S(2)}) collective-permute-start(bf16[2,128,1024]{2,1,0:T(8,128)(2,1)S(1)} %collective-permute-done.7.refs_3_), channel_id=1, source_target_pairs={{0,2},{2,4},{4,6},{6,7},{7,5},{5,3},{3,1},{1,0},{8,10},{10,12},{12... | collective-permute-start | bytes 1572872 | tf_op jit(solution)/shard_map/ppermute | solution.py:110
  86.6 25.4 %collective-permute-start.20 = (bf16[7,128,512]{2,1,0:T(8,128)(2,1)S(1)}, bf16[7,128,512]{2,1,0:T(8,128)(2,1)}, u32[]{:S(2)}, u32[]{:S(2)}) collective-permute-start(bf16[7,128,512]{2,1,0:T(8,128)(2,1)S(1)} %collective-permute-done.5.refs_2_), channel_id=1, source_target_pairs={{2,0},{4,2},{6,4},{7,6},{5,7},{3,5},{1,3},{0,1},{10,8},{12,10},{14... | collective-permute-start | bytes 2752520 | tf_op jit(solution)/shard_map/ppermute | solution.py:110
  87.7 28.7 %collective-permute-start.18 = (bf16[7,128,512]{2,1,0:T(8,128)(2,1)S(1)}, bf16[7,128,512]{2,1,0:T(8,128)(2,1)}, u32[]{:S(2)}, u32[]{:S(2)}) collective-permute-start(bf16[7,128,512]{2,1,0:T(8,128)(2,1)S(1)} %collective-permute-done.4.refs_1_), channel_id=1, source_target_pairs={{0,2},{2,4},{4,6},{6,7},{7,5},{5,3},{3,1},{1,0},{8,10},{10,12},{12... | collective-permute-start | bytes 2752520 | tf_op jit(solution)/shard_map/ppermute | solution.py:110
  89.7 22.3 %collective-permute-start.22 = (bf16[2,128,1024]{2,1,0:T(8,128)(2,1)}, bf16[2,128,1024]{2,1,0:T(8,128)(2,1)S(1)}, u32[]{:S(2)}, u32[]{:S(2)}) collective-permute-start(bf16[2,128,1024]{2,1,0:T(8,128)(2,1)} %copy-done.67), channel_id=1, source_target_pairs={{0,16},{16,0},{1,17},{17,1},{2,18},{18,2},{3,19},{19,3},{4,20},{20... | collective-permute-start | bytes 1572872 | tf_op jit(solution)/shard_map/ppermute | solution.py:110
  106.3 22.0 %collective-permute-start.14 = (bf16[512,1024]{1,0:T(8,128)(2,1)}, bf16[512,1024]{1,0:T(8,128)(2,1)S(1)}, u32[]{:S(2)}, u32[]{:S(2)}) collective-permute-start(bf16[512,1024]{1,0:T(8,128)(2,1)} %get-tuple-element.285), channel_id=1, source_target_pairs={{0,8},{8,0},{1,9},{9,1},{2,10},{10,2},{3,11},{11,3},{4,12},{12,4},... | collective-permute-start | bytes 3145736 | tf_op jit(solution)/shard_map/ppermute | solution.py:321
  117.9 14.8 %collective-permute-start.27 = (bf16[7,128,512]{2,1,0:T(8,128)(2,1)}, bf16[7,128,512]{2,1,0:T(8,128)(2,1)S(1)}, u32[]{:S(2)}, u32[]{:S(2)}) collective-permute-start(bf16[7,128,512]{2,1,0:T(8,128)(2,1)} %collective-permute-done.20.refs_4_), channel_id=1, source_target_pairs={{0,8},{8,0},{1,9},{9,1},{2,10},{10,2},{3,11},{11,3},{4,12},{12,4},... | collective-permute-start | bytes 2752520 | tf_op jit(solution)/shard_map/ppermute | solution.py:110
  126.9 18.9 %collective-permute-start.21 = (bf16[7,128,512]{2,1,0:T(8,128)(2,1)}, bf16[7,128,512]{2,1,0:T(8,128)(2,1)S(1)}, u32[]{:S(2)}, u32[]{:S(2)}) collective-permute-start(bf16[7,128,512]{2,1,0:T(8,128)(2,1)} %collective-permute-done.20.refs_4_), channel_id=1, source_target_pairs={{2,0},{4,2},{6,4},{7,6},{5,7},{3,5},{1,3},{0,1},{10,8},{12,10},{14... | collective-permute-start | bytes 2752520 | tf_op jit(solution)/shard_map/ppermute | solution.py:110
  128.1 18.6 %collective-permute-start.19 = (bf16[7,128,512]{2,1,0:T(8,128)(2,1)}, bf16[7,128,512]{2,1,0:T(8,128)(2,1)}, u32[]{:S(2)}, u32[]{:S(2)}) collective-permute-start(bf16[7,128,512]{2,1,0:T(8,128)(2,1)} %collective-permute-done.18.refs_3_), channel_id=1, source_target_pairs={{0,2},{2,4},{4,6},{6,7},{7,5},{5,3},{3,1},{1,0},{8,10},{10,12},{12... | collective-permute-start | bytes 2752520 | tf_op jit(solution)/shard_map/ppermute | solution.py:110
  128.3 18.4 %collective-permute-start.24 = (bf16[2,128,1024]{2,1,0:T(8,128)(2,1)S(1)}, bf16[2,128,1024]{2,1,0:T(8,128)(2,1)S(1)}, u32[]{:S(2)}, u32[]{:S(2)}) collective-permute-start(bf16[2,128,1024]{2,1,0:T(8,128)(2,1)S(1)} %collective-permute-done.23.refs_3_), channel_id=1, source_target_pairs={{0,16},{16,0},{1,17},{17,1},{2,18},{18,2},{3,19},{19,3},{4,20},{20... | collective-permute-start | bytes 1572872 | tf_op jit(solution)/shard_map/ppermute | solution.py:110
  149.5 18.0 %collective-permute-start.28 = (bf16[256,1024]{1,0:T(8,128)(2,1)S(1)}, bf16[256,1024]{1,0:T(8,128)(2,1)S(1)}, u32[]{:S(2)}, u32[]{:S(2)}) collective-permute-start(bf16[256,1024]{1,0:T(8,128)(2,1)S(1)} %slice.314), channel_id=1, source_target_pairs={{0,16},{16,0},{1,17},{17,1},{2,18},{18,2},{3,19},{19,3},{4,20},{20... | collective-permute-start | bytes 1572872 | tf_op jit(solution)/shard_map/ppermute | solution.py:110
  149.7 29.5 %collective-permute-start.34 = (bf16[7,128,512]{2,1,0:T(8,128)(2,1)S(1)}, bf16[7,128,512]{2,1,0:T(8,128)(2,1)}, u32[]{:S(2)}, u32[]{:S(2)}) collective-permute-start(bf16[7,128,512]{2,1,0:T(8,128)(2,1)S(1)} %collective-permute-done.21.refs_6_), channel_id=1, source_target_pairs={{2,0},{4,2},{6,4},{7,6},{5,7},{3,5},{1,3},{0,1},{10,8},{12,10},{14... | collective-permute-start | bytes 2752520 | tf_op jit(solution)/shard_map/ppermute | solution.py:110
  168.7 25.0 %collective-permute-start.36 = (bf16[7,128,512]{2,1,0:T(8,128)(2,1)S(1)}, bf16[7,128,512]{2,1,0:T(8,128)(2,1)}, u32[]{:S(2)}, u32[]{:S(2)}) collective-permute-start(bf16[7,128,512]{2,1,0:T(8,128)(2,1)S(1)} %collective-permute-done.21.refs_6_), channel_id=1, source_target_pairs={{0,8},{8,0},{1,9},{9,1},{2,10},{10,2},{3,11},{11,3},{4,12},{12,4},... | collective-permute-start | bytes 2752520 | tf_op jit(solution)/shard_map/ppermute | solution.py:110
  179.2 14.5 %collective-permute-start.35 = (bf16[7,128,512]{2,1,0:T(8,128)(2,1)}, bf16[7,128,512]{2,1,0:T(8,128)(2,1)}, u32[]{:S(2)}, u32[]{:S(2)}) collective-permute-start(bf16[7,128,512]{2,1,0:T(8,128)(2,1)} %collective-permute-done.19.refs_5_), channel_id=1, source_target_pairs={{0,8},{8,0},{1,9},{9,1},{2,10},{10,2},{3,11},{11,3},{4,12},{12,4},... | collective-permute-start | bytes 2752520 | tf_op jit(solution)/shard_map/ppermute | solution.py:110
  188.1 15.1 %collective-permute-start.39 = (bf16[2,128,1024]{2,1,0:T(8,128)(2,1)}, bf16[2,128,1024]{2,1,0:T(8,128)(2,1)}, u32[]{:S(2)}, u32[]{:S(2)}) collective-permute-start(bf16[2,128,1024]{2,1,0:T(8,128)(2,1)} %collective-permute-done.29.refs_5_), channel_id=1, source_target_pairs={{0,16},{16,0},{1,17},{17,1},{2,18},{18,2},{3,19},{19,3},{4,20},{20... | collective-permute-start | bytes 1572872 | tf_op jit(solution)/shard_map/ppermute | solution.py:110
  188.1 25.1 %collective-permute-start.38 = (bf16[2,128,1024]{2,1,0:T(8,128)(2,1)}, bf16[2,128,1024]{2,1,0:T(8,128)(2,1)}, u32[]{:S(2)}, u32[]{:S(2)}) collective-permute-start(bf16[2,128,1024]{2,1,0:T(8,128)(2,1)} %collective-permute-done.32.refs_7_), channel_id=1, source_target_pairs={{0,16},{16,0},{1,17},{17,1},{2,18},{18,2},{3,19},{19,3},{4,20},{20... | collective-permute-start | bytes 1572872 | tf_op jit(solution)/shard_map/ppermute | solution.py:110
  280.3 23.8 %collective-permute-start.48 = (bf16[2,1024,256]{2,1,0:T(8,128)(2,1)S(1)}, bf16[2,1024,256]{2,1,0:T(8,128)(2,1)S(1)}, u32[]{:S(2)}, u32[]{:S(2)}) collective-permute-start(bf16[2,1024,256]{2,1,0:T(8,128)(2,1)S(1)} %copy-done.58), channel_id=1, source_target_pairs={{0,16},{16,0},{1,17},{17,1},{2,18},{18,2},{3,19},{19,3},{4,20},{20... | collective-permute-start | bytes 3145736 | tf_op jit(solution)/shard_map/ppermute | solution.py:110
  281.5 16.1 %collective-permute-start.46 = (bf16[8,128,256]{2,1,0:T(8,128)(2,1)}, bf16[8,128,256]{2,1,0:T(8,128)(2,1)S(1)}, u32[]{:S(2)}, u32[]{:S(2)}) collective-permute-start(bf16[8,128,256]{2,1,0:T(8,128)(2,1)} %get-tuple-element.371), channel_id=1, source_target_pairs={{0,2},{2,4},{4,6},{6,7},{7,5},{5,3},{3,1},{1,0},{8,10},{10,12},{12... | collective-permute-start | bytes 1572872 | tf_op jit(solution)/shard_map/ppermute | solution.py:110
  282.9 14.8 %collective-permute-start.47 = (bf16[8,128,256]{2,1,0:T(8,128)(2,1)}, bf16[8,128,256]{2,1,0:T(8,128)(2,1)S(1)}, u32[]{:S(2)}, u32[]{:S(2)}) collective-permute-start(bf16[8,128,256]{2,1,0:T(8,128)(2,1)} %get-tuple-element.372), channel_id=1, source_target_pairs={{2,0},{4,2},{6,4},{7,6},{5,7},{3,5},{1,3},{0,1},{10,8},{12,10},{14... | collective-permute-start | bytes 1572872 | tf_op jit(solution)/shard_map/ppermute | solution.py:110
  307.6 22.9 %collective-permute-start.51 = (bf16[2,1024,256]{2,1,0:T(8,128)(2,1)S(1)}, bf16[2,1024,256]{2,1,0:T(8,128)(2,1)S(1)}, u32[]{:S(2)}, u32[]{:S(2)}) collective-permute-start(bf16[2,1024,256]{2,1,0:T(8,128)(2,1)S(1)} %copy-done.56), channel_id=1, source_target_pairs={{0,16},{16,0},{1,17},{17,1},{2,18},{18,2},{3,19},{19,3},{4,20},{20... | collective-permute-start | bytes 3145736 | tf_op jit(solution)/shard_map/ppermute | solution.py:110
  307.7 22.8 %collective-permute-start.52 = (bf16[2,1,1024,256]{3,2,1,0:T(8,128)(2,1)}, bf16[2,1,1024,256]{3,2,1,0:T(8,128)(2,1)S(1)}, u32[]{:S(2)}, u32[]{:S(2)}) collective-permute-start(bf16[2,1,1024,256]{3,2,1,0:T(8,128)(2,1)} %get-tuple-element.395), channel_id=1, source_target_pairs={{0,8},{8,0},{1,9},{9,1},{2,10},{10,2},{3,11},{11,3},{4,12},{12,4},... | collective-permute-start | bytes 3145736 | tf_op jit(solution)/shard_map/ppermute | solution.py:110
  309.8 19.3 %collective-permute-start.49 = (bf16[8,128,256]{2,1,0:T(8,128)(2,1)}, bf16[8,128,256]{2,1,0:T(8,128)(2,1)S(1)}, u32[]{:S(2)}, u32[]{:S(2)}) collective-permute-start(bf16[8,128,256]{2,1,0:T(8,128)(2,1)} %get-tuple-element.392), channel_id=1, source_target_pairs={{0,2},{2,4},{4,6},{6,7},{7,5},{5,3},{3,1},{1,0},{8,10},{10,12},{12... | collective-permute-start | bytes 1572872 | tf_op jit(solution)/shard_map/ppermute | solution.py:110
  310.4 18.6 %collective-permute-start.50 = (bf16[8,128,256]{2,1,0:T(8,128)(2,1)}, bf16[8,128,256]{2,1,0:T(8,128)(2,1)S(1)}, u32[]{:S(2)}, u32[]{:S(2)}) collective-permute-start(bf16[8,128,256]{2,1,0:T(8,128)(2,1)} %get-tuple-element.393), channel_id=1, source_target_pairs={{2,0},{4,2},{6,4},{7,6},{5,7},{3,5},{1,3},{0,1},{10,8},{12,10},{14... | collective-permute-start | bytes 1572872 | tf_op jit(solution)/shard_map/ppermute | solution.py:110
  335.5 22.4 %collective-permute-start.55 = (bf16[2,2,1024,256]{3,2,1,0:T(8,128)(2,1)}, bf16[2,2,1024,256]{3,2,1,0:T(8,128)(2,1)S(1)}, u32[]{:S(2)}, u32[]{:S(2)}) collective-permute-start(bf16[2,2,1024,256]{3,2,1,0:T(8,128)(2,1)} %get-tuple-element.413), channel_id=1, source_target_pairs={{0,8},{8,0},{1,9},{9,1},{2,10},{10,2},{3,11},{11,3},{4,12},{12,4},... | collective-permute-start | bytes 6291464 | tf_op jit(solution)/shard_map/ppermute | solution.py:110
  338.4 19.6 %collective-permute-start.56 = (bf16[2,1,1024,256]{3,2,1,0:T(8,128)(2,1)S(1)}, bf16[2,1,1024,256]{3,2,1,0:T(8,128)(2,1)S(1)}, u32[]{:S(2)}, u32[]{:S(2)}) collective-permute-start(bf16[2,1,1024,256]{3,2,1,0:T(8,128)(2,1)S(1)} %copy-done.57), channel_id=1, source_target_pairs={{0,8},{8,0},{1,9},{9,1},{2,10},{10,2},{3,11},{11,3},{4,12},{12,4},... | collective-permute-start | bytes 3145736 | tf_op jit(solution)/shard_map/ppermute | solution.py:110
  338.4 19.5 %collective-permute-start.53 = (bf16[12,128,256]{2,1,0:T(8,128)(2,1)}, bf16[12,128,256]{2,1,0:T(8,128)(2,1)S(1)}, u32[]{:S(2)}, u32[]{:S(2)}) collective-permute-start(bf16[12,128,256]{2,1,0:T(8,128)(2,1)} %get-tuple-element.411), channel_id=1, source_target_pairs={{0,2},{2,4},{4,6},{6,7},{7,5},{5,3},{3,1},{1,0},{8,10},{10,12},{12... | collective-permute-start | bytes 2359304 | tf_op jit(solution)/shard_map/ppermute | solution.py:110
  362.2 33.7 %collective-permute-start.61 = (bf16[2,3,1024,256]{3,2,1,0:T(8,128)(2,1)}, bf16[2,3,1024,256]{3,2,1,0:T(8,128)(2,1)}, u32[]{:S(2)}, u32[]{:S(2)}) collective-permute-start(bf16[2,3,1024,256]{3,2,1,0:T(8,128)(2,1)} %get-tuple-element.431), channel_id=1, source_target_pairs={{0,8},{8,0},{1,9},{9,1},{2,10},{10,2},{3,11},{11,3},{4,12},{12,4},... | collective-permute-start | bytes 9437192 | tf_op jit(solution)/shard_map/ppermute | solution.py:110
  405.0 23.5 %collective-permute-start.63 = (bf16[16,128,256]{2,1,0:T(8,128)(2,1)}, bf16[16,128,256]{2,1,0:T(8,128)(2,1)}, u32[]{:S(2)}, u32[]{:S(2)}) collective-permute-start(bf16[16,128,256]{2,1,0:T(8,128)(2,1)} %get-tuple-element.445), channel_id=1, source_target_pairs={{0,2},{2,4},{4,6},{6,7},{7,5},{5,3},{3,1},{1,0},{8,10},{10,12},{12... | collective-permute-start | bytes 3145736 | tf_op jit(solution)/shard_map/ppermute | solution.py:110
  405.0 23.7 %collective-permute-start.64 = (bf16[16,128,256]{2,1,0:T(8,128)(2,1)}, bf16[16,128,256]{2,1,0:T(8,128)(2,1)}, u32[]{:S(2)}, u32[]{:S(2)}) collective-permute-start(bf16[16,128,256]{2,1,0:T(8,128)(2,1)} %get-tuple-element.446), channel_id=1, source_target_pairs={{2,0},{4,2},{6,4},{7,6},{5,7},{3,5},{1,3},{0,1},{10,8},{12,10},{14... | collective-permute-start | bytes 3145736 | tf_op jit(solution)/shard_map/ppermute | solution.py:110
  406.7 23.0 %collective-permute-start.65 = (bf16[2,1024,256]{2,1,0:T(8,128)(2,1)}, bf16[2,1024,256]{2,1,0:T(8,128)(2,1)}, u32[]{:S(2)}, u32[]{:S(2)}) collective-permute-start(bf16[2,1024,256]{2,1,0:T(8,128)(2,1)} %slice_bitcast_fusion), channel_id=1, source_target_pairs={{0,16},{16,0},{1,17},{17,1},{2,18},{18,2},{3,19},{19,3},{4,20},{20... | collective-permute-start | bytes 3145736 | tf_op jit(solution)/shard_map/ppermute | solution.py:110
  440.5 34.8 %collective-permute-start.67 = (bf16[23,128,256]{2,1,0:T(8,128)(2,1)}, bf16[23,128,256]{2,1,0:T(8,128)(2,1)S(1)}, u32[]{:S(2)}, u32[]{:S(2)}) collective-permute-start(bf16[23,128,256]{2,1,0:T(8,128)(2,1)} %get-tuple-element.458), channel_id=1, source_target_pairs={{2,0},{4,2},{6,4},{7,6},{5,7},{3,5},{1,3},{0,1},{10,8},{12,10},{14... | collective-permute-start | bytes 4521992 | tf_op jit(solution)/shard_map/ppermute | solution.py:110
  441.9 28.9 %collective-permute-start.66 = (bf16[19,128,256]{2,1,0:T(8,128)(2,1)}, bf16[19,128,256]{2,1,0:T(8,128)(2,1)}, u32[]{:S(2)}, u32[]{:S(2)}) collective-permute-start(bf16[19,128,256]{2,1,0:T(8,128)(2,1)} %get-tuple-element.457), channel_id=1, source_target_pairs={{0,2},{2,4},{4,6},{6,7},{7,5},{5,3},{3,1},{1,0},{8,10},{10,12},{12... | collective-permute-start | bytes 3735560 | tf_op jit(solution)/shard_map/ppermute | solution.py:110
  445.0 30.3 %collective-permute-start.69 = (bf16[256,1024]{1,0:T(8,128)(2,1)}, bf16[256,1024]{1,0:T(8,128)(2,1)}, u32[]{:S(2)}, u32[]{:S(2)}) collective-permute-start(bf16[256,1024]{1,0:T(8,128)(2,1)} %slice.313), channel_id=1, source_target_pairs={{0,16},{16,0},{1,17},{17,1},{2,18},{18,2},{3,19},{19,3},{4,20},{20... | collective-permute-start | bytes 1572872 | tf_op jit(solution)/shard_map/ppermute | solution.py:110
  481.3 28.4 %collective-permute-start.71 = (bf16[19,128,256]{2,1,0:T(8,128)(2,1)}, bf16[19,128,256]{2,1,0:T(8,128)(2,1)S(1)}, u32[]{:S(2)}, u32[]{:S(2)}) collective-permute-start(bf16[19,128,256]{2,1,0:T(8,128)(2,1)} %get-tuple-element.473), channel_id=1, source_target_pairs={{0,2},{2,4},{4,6},{6,7},{7,5},{5,3},{3,1},{1,0},{8,10},{10,12},{12... | collective-permute-start | bytes 3735560 | tf_op jit(solution)/shard_map/ppermute | solution.py:110
  481.4 28.4 %collective-permute-start.72 = (bf16[19,128,256]{2,1,0:T(8,128)(2,1)}, bf16[19,128,256]{2,1,0:T(8,128)(2,1)}, u32[]{:S(2)}, u32[]{:S(2)}) collective-permute-start(bf16[19,128,256]{2,1,0:T(8,128)(2,1)} %get-tuple-element.474), channel_id=1, source_target_pairs={{2,0},{4,2},{6,4},{7,6},{5,7},{3,5},{1,3},{0,1},{10,8},{12,10},{14... | collective-permute-start | bytes 3735560 | tf_op jit(solution)/shard_map/ppermute | solution.py:110
  514.8 21.9 %collective-permute-start.76 = (bf16[15,128,256]{2,1,0:T(8,128)(2,1)}, bf16[15,128,256]{2,1,0:T(8,128)(2,1)S(1)}, u32[]{:S(2)}, u32[]{:S(2)}) collective-permute-start(bf16[15,128,256]{2,1,0:T(8,128)(2,1)} %get-tuple-element.480), channel_id=1, source_target_pairs={{2,0},{4,2},{6,4},{7,6},{5,7},{3,5},{1,3},{0,1},{10,8},{12,10},{14... | collective-permute-start | bytes 2949128 | tf_op jit(solution)/shard_map/ppermute | solution.py:110
  516.3 15.9 %collective-permute-start.75 = (bf16[11,128,256]{2,1,0:T(8,128)(2,1)}, bf16[11,128,256]{2,1,0:T(8,128)(2,1)S(1)}, u32[]{:S(2)}, u32[]{:S(2)}) collective-permute-start(bf16[11,128,256]{2,1,0:T(8,128)(2,1)} %get-tuple-element.479), channel_id=1, source_target_pairs={{0,2},{2,4},{4,6},{6,7},{7,5},{5,3},{3,1},{1,0},{8,10},{10,12},{12... | collective-permute-start | bytes 2162696 | tf_op jit(solution)/shard_map/ppermute | solution.py:110
  570.7 41.5 %all-to-all-start = ((bf16[8,3,128,256]{3,2,1,0:T(8,128)(2,1)}), bf16[8,3,128,256]{3,2,1,0:T(8,128)(2,1)}, u32[]{:S(2)}, u32[]{:S(2)}) async-start(bf16[8,3,128,256]{3,2,1,0:T(8,128)(2,1)} %bitcast.369), calls=%async_computation | async-start | bytes 3145728 | tf_op jit(solution)/shard_map/all_to_all | solution.py:1372
  623.2 20.2 %collective-permute-start.86 = (f32[34,1024]{1,0:T(8,128)S(1)}, f32[34,1024]{1,0:T(8,128)S(1)}, u32[]{:S(2)}, u32[]{:S(2)}) collective-permute-start(f32[34,1024]{1,0:T(8,128)S(1)} %add.722), channel_id=1, source_target_pairs={{0,4},{1,5},{2,6},{3,7},{4,0},{5,1},{6,2},{7,3},{8,12},{9,13},{10,... | collective-permute-start | bytes 417800 | tf_op jit(solution)/shard_map/ppermute | solution.py:110
  651.4 26.9 %collective-permute-start.95 = (bf16[256,1024]{1,0:T(8,128)(2,1)}, bf16[256,1024]{1,0:T(8,128)(2,1)}, u32[]{:S(2)}, u32[]{:S(2)}) collective-permute-start(bf16[256,1024]{1,0:T(8,128)(2,1)} %fusion.49), channel_id=1, source_target_pairs={{0,16},{16,0},{1,17},{17,1},{2,18},{18,2},{3,19},{19,3},{4,20},{20... | collective-permute-start | bytes 1572872 | tf_op jit(solution)/shard_map/ppermute | solution.py:327
  660.6 24.7 %collective-permute-start.94 = (bf16[2,256,1024]{2,1,0:T(8,128)(2,1)}, bf16[2,256,1024]{2,1,0:T(8,128)(2,1)}, u32[]{:S(2)}, u32[]{:S(2)}) collective-permute-start(bf16[2,256,1024]{2,1,0:T(8,128)(2,1)} %pad_maximum_fusion.9), channel_id=1, source_target_pairs={{0,8},{8,0},{1,9},{9,1},{2,10},{10,2},{3,11},{11,3},{4,12},{12,4},... | collective-permute-start | bytes 3145736 | tf_op jit(solution)/shard_map/ppermute | solution.py:327
  (132 other events, 1446.8 us)

commit v5 on v4

--- a/solution.py
+++ b/solution.py
@@ -1280,6 +1280,8 @@
         beside=[half_low],
     )
     both_low = Cell(all_four(half_low.value, far_low[0].value))
+    attn_total = Cell(jnp.concatenate([attn_in.total(), attn_out.total()], axis=1))
+    bind(both_low, attn_total)
     if pairs:
         came += begin(conv_chips.send(), beside=[both_low])
     low, sums, *matrices = ffn_backward_out(
@@ -1288,7 +1290,7 @@
     first_out = ring_of(0, matrices[0])
     low = Cell(low)
     bind(low, *came)
-    attn_part = ring_of(1, jnp.concatenate([attn_in.total(), attn_out.total()], axis=1))
+    attn_part = ring_of(1, attn_total.value)
     conv_sends = conv_chips.send() if pairs else []
     came = begin(hop_together(second_in.ring, attn_part, first_out), conv_sends, beside=[low])
     mine, away, *matrices = ffn_backward_in(low.value, first, [], kept_first, False)

time: 709 us -> 711 us (level)
    unnamed x166 -> x172, local copies, waits for them, and re-layouts: 14.6 us -> 16.9 us
  transfers between devices with their start and end apart: 100 -> 100, of which waited for: 48 -> 49; matrix products, arithmetic and copies ran while one was open for 14% -> 14% of each run, Pallas kernels for 13% -> 13%
where the time goes in v5:
time: 711 us; the launch traced here: 701 us
  waiting for transfers between devices  262 us (37%)
  Pallas kernels  166 us (23%)
  starting transfers between devices  121 us (17%)
  other arithmetic  81.5 us (11%)
  local copies, waits for them, and re-layouts  36.3 us (5%)
  matrix products  30.3 us (4%)
    ppermute x75, waiting for transfers between devices, start(): came.append(Cell(lax.ppermute(value, axis, pairs)))  216 us
    ppermute x75, starting transfers between devices, start(): came.append(Cell(lax.ppermute(value, axis, pairs)))  84 us
    pallas_call x6, Pallas kernels, panel_call(): pl.pallas_call(functools.partial(kernel, count), out_shape=outs, in_specs...  52.7 us
    pallas_call x4, Pallas kernels, ffn_backward_call(): pl.pallas_call(functools.partial(kernel, count, halves, bias, (outer, way...  42.8 us
    pallas_call x10, Pallas kernels, hop_together(): pl.pallas_call(functools.partial(hop_kernel, tuple(plan), (len(inputs), l...  36.2 us
    ppermute x10, starting transfers between devices, swap_cores(): return lax.ppermute(values, 'c', SWAP)  19.7 us
    all_to_all x1, waiting for transfers between devices, on_device(): lax.all_to_all(outgoing, 'f', split_axis=0, concat_axis=0, tiled=True)  19.1 us
    pallas_call x2, Pallas kernels, ffn_forward_call(): pl.pallas_call(functools.partial(ffn_forward_kernel, count, halves), out_...  19 us
  transfers between devices with their start and end apart: 100, of which 49 were waited for; matrix products, arithmetic and copies ran while one was open for 14% of the time, Pallas kernels for 13%

profile of v5, /device:TPU:1, one launch (start us, length us, event | category | flops | bytes accessed | tf_op | source)
XLA Modules:
  0.0 700.9 jit_solution(11121509514426153044)
XLA Ops:
  15.8 7.5 %collective-permute-done.refs_1_ = bf16[2,128,1024]{2,1,0:T(8,128)(2,1)S(1)} collective-permute-done((bf16[2,128,1024]{2,1,0:T(8,128)(2,1)S(1)}, bf16[2,128,1024]{2,1,0:T(8,128)(2,1)S(1)}, u32[]{:S(2)}, u32[]{:S(2)}) %collective-permute-start) | collective-permute-done | bytes 524320 | tf_op jit(solution)/shard_map/ppermute | solution.py:110
  31.9 8.3 %convert_element_type.214 = bf16[3,1024,1024]{2,1,0:T(8,128)(2,1)} convert(f32[3,1024,1024]{2,1,0:T(8,128)} %param.21) | non-fusion elementwise | flops 3145728 | bytes 18874368 | tf_op jit(solution)/shard_map/convert_element_type | solution.py:999
  40.2 8.2 %convert_element_type.215 = bf16[3,1024,1024]{2,1,0:T(8,128)(2,1)} convert(f32[3,1024,1024]{2,1,0:T(8,128)} %param.22) | non-fusion elementwise | flops 3145728 | bytes 18874368 | tf_op jit(solution)/shard_map/convert_element_type | solution.py:1000
  52.8 8.8 %collective-permute-done.7.refs_3_ = bf16[2,128,1024]{2,1,0:T(8,128)(2,1)S(1)} collective-permute-done((bf16[2,128,1024]{2,1,0:T(8,128)(2,1)}, bf16[2,128,1024]{2,1,0:T(8,128)(2,1)S(1)}, u32[]{:S(2)}, u32[]{:S(2)}) %collective-permute-start.7) | collective-permute-done | bytes 524320 | tf_op jit(solution)/shard_map/ppermute | solution.py:110
  65.5 7.3 %collective-permute-done.11.refs_1_ = bf16[2,128,1024]{2,1,0:T(8,128)(2,1)S(1)} collective-permute-done((bf16[2,128,1024]{2,1,0:T(8,128)(2,1)S(1)}, bf16[2,128,1024]{2,1,0:T(8,128)(2,1)S(1)}, u32[]{:S(2)}, u32[]{:S(2)}) %collective-permute-start.11) | collective-permute-done | bytes 524320 | tf_op jit(solution)/shard_map/ppermute | solution.py:110
  75.4 8.8 %collective-permute-done.9.refs_5_ = bf16[2,128,1024]{2,1,0:T(8,128)(2,1)} collective-permute-done((bf16[2,128,1024]{2,1,0:T(8,128)(2,1)S(1)}, bf16[2,128,1024]{2,1,0:T(8,128)(2,1)}, u32[]{:S(2)}, u32[]{:S(2)}) %collective-permute-start.9) | collective-permute-done | bytes 524320 | tf_op jit(solution)/shard_map/ppermute | solution.py:110
  90.9 5.8 collective-permute-done.13.refs_7_
  96.8 9.5 %ffn_forward.2 = (f32[1,1024,1024]{2,1,0:T(8,128)}, bf16[1,1024,1024]{2,1,0:T(8,128)(2,1)}, f32[512,1024]{1,0:T(8,128)}, bf16[512,1024]{1,0:T(8,128)(2,1)}) custom-call(s32[9]{0:T(128)} %concatenate.74.meta, bf16[1024,1024]{1,0:T(8,128)(2,1)} %pad_maximum_fusion.4.normed, f32[1,1,1024]{2,1,0:T(1,128)} %get-tuple-element.283.bias, ...), custom_call_target="tpu_custom_call" | custom-call | flops 4294967296 | bytes 27262976 | tf_op jit(solution)/shard_map/ffn_forward/pallas_call | solution.py:416
  106.3 5.7 collective-permute-start.14
  112.0 4.4 collective-permute-done.18.refs_3_
  121.5 5.4 collective-permute-done.25.refs_4_
  132.7 13.0 %collective-permute-done.21.refs_6_ = bf16[7,128,512]{2,1,0:T(8,128)(2,1)S(1)} collective-permute-done((bf16[7,128,512]{2,1,0:T(8,128)(2,1)}, bf16[7,128,512]{2,1,0:T(8,128)(2,1)S(1)}, u32[]{:S(2)}, u32[]{:S(2)}) %collective-permute-start.21) | collective-permute-done | bytes 917536 | tf_op jit(solution)/shard_map/ppermute | solution.py:110
  151.0 6.6 collective-permute-done.29.refs_5_
  157.7 9.8 %collective-permute-done.28 = bf16[256,1024]{1,0:T(8,128)(2,1)S(1)} collective-permute-done((bf16[256,1024]{1,0:T(8,128)(2,1)S(1)}, bf16[256,1024]{1,0:T(8,128)(2,1)S(1)}, u32[]{:S(2)}, u32[]{:S(2)}) %collective-permute-start.28) | collective-permute-done | bytes 524320 | tf_op jit(solution)/shard_map/ppermute | solution.py:110
  168.7 10.5 %collective-permute-start.36 = (bf16[7,128,512]{2,1,0:T(8,128)(2,1)S(1)}, bf16[7,128,512]{2,1,0:T(8,128)(2,1)}, u32[]{:S(2)}, u32[]{:S(2)}) collective-permute-start(bf16[7,128,512]{2,1,0:T(8,128)(2,1)S(1)} %collective-permute-done.21.refs_6_), channel_id=1, source_target_pairs={{0,8},{8,0},{1,9},{9,1},{2,10},{10,2},{3,11},{11,3},{4,12},{12,4},... | collective-permute-start | bytes 2752520 | tf_op jit(solution)/shard_map/ppermute | solution.py:110
  180.0 8.1 %collective-permute-start.37 = (bf16[7,128,512]{2,1,0:T(8,128)(2,1)}, bf16[7,128,512]{2,1,0:T(8,128)(2,1)}, u32[]{:S(2)}, u32[]{:S(2)}) collective-permute-start(bf16[7,128,512]{2,1,0:T(8,128)(2,1)} %collective-permute-done.34.refs_7_), channel_id=1, source_target_pairs={{0,8},{8,0},{1,9},{9,1},{2,10},{10,2},{3,11},{11,3},{4,12},{12,4},... | collective-permute-start | bytes 2752520 | tf_op jit(solution)/shard_map/ppermute | solution.py:110
  193.7 9.4 %attention_forward.1 = (f32[256,1024]{1,0:T(8,128)}, bf16[256,1024]{1,0:T(8,128)(2,1)}, bf16[256,1024]{1,0:T(8,128)(2,1)}, bf16[256,1024]{1,0:T(8,128)(2,1)}, bf...) custom-call(s32[10]{0:T(128)} %concatenate.71.meta, f32[256,1024]{1,0:T(8,128)} %multiply_add_fusion.3.stream, ...), custom_call_target="tpu_custom_call" | custom-call | flops 2147483648 | bytes 16777216 | tf_op jit(solution)/shard_map/attention_forward/pallas_call | solution.py:906
  203.2 10.0 %collective-permute-done.38.refs_15_ = bf16[2,128,1024]{2,1,0:T(8,128)(2,1)} collective-permute-done((bf16[2,128,1024]{2,1,0:T(8,128)(2,1)}, bf16[2,128,1024]{2,1,0:T(8,128)(2,1)}, u32[]{:S(2)}, u32[]{:S(2)}) %collective-permute-start.38) | collective-permute-done | bytes 524320 | tf_op jit(solution)/shard_map/ppermute | solution.py:110
  213.2 8.1 %conv_forward.1 = (f32[256,1024]{1,0:T(8,128)}, bf16[256,1024]{1,0:T(8,128)(2,1)}, f32[2,256,1024]{2,1,0:T(8,128)}, bf16[256,1024]{1,0:T(8,128)(2,1)}, bf16[256,1024]{1,0:T(8,128)(2,1)}) custom-call(s32[10]{0:T(128)} %concatenate.71.meta, f32[256,1024]{1,0:T(8,128)} %get-tuple-element.320.stream, f32[34,1024]{1,0:T(8,128)} %rows.15, ...), custom_call_target="tpu_custom_call" | custom-call | flops 1610612736 | bytes 14680064 | tf_op jit(solution)/shard_map/conv_forward/pallas_call | solution.py:906
  225.0 9.5 %ffn_forward.3 = (f32[2,512,1024]{2,1,0:T(8,128)}, bf16[2,512,1024]{2,1,0:T(8,128)(2,1)}, f32[256,1024]{1,0:T(8,128)}, bf16[256,1024]{1,0:T(8,128)(2,1)}) custom-call(s32[9]{0:T(128)} %concatenate.74.meta, bf16[512,1024]{1,0:T(8,128)(2,1)} %copy-done.52, f32[2,1,1024]{2,1,0:T(1,128)} %broadcast_in_dim.25.bias, ...), custom_call_target="tpu_custom_call" | custom-call | flops 4294967296 | bytes 17825792 | tf_op jit(solution)/shard_map/ffn_forward/pallas_call | solution.py:416
  237.4 4.6 turn.1
  246.2 12.7 %ffn_out_backward.2 = (bf16[2,512,1024]{2,1,0:T(8,128)(2,1)}, f32[34,1024]{1,0:T(8,128)}, bf16[2,2,2,1024,256]{4,3,2,1,0:T(8,128)(2,1)}) custom-call(s32[11]{0:T(128)} %concatenate.79.meta, f32[2,512,1024]{2,1,0:T(8,128)} %get-tuple-element.342.hidden, bf16[2,512,1024]{2,1,0:T(8,128)(2,1)} %get-tuple-element.343.active, ...), custom_call_target="tpu_custom_call" | custom-call | flops 4294967296 | bytes 16777216 | tf_op jit(solution)/shard_map/ffn_out_backward/pallas_call | solution.py:509
  263.6 9.5 %ffn_in_backward.2 = (f32[256,1024]{1,0:T(8,128)}, bf16[256,1024]{1,0:T(8,128)(2,1)}, bf16[2,2,1024,256]{3,2,1,0:T(8,128)(2,1)}, bf16[2,1024,256]{2,1,0:T(8,128)(2,1)}, bf16[2,1024,256]{2,1,0:T(8,128)(2,1)}) custom-call(s32[11]{0:T(128)} %concatenate.79.meta, bf16[512,1024]{1,0:T(8,128)(2,1)} %copy-done.52, bf16[2,512,1024]{2,1,0:T(8,128)(2,1)} %get-tuple-element.350.low, ...), custom_call_target="tpu_custom_call" | custom-call | flops 4294967296 | bytes 16777216 | tf_op jit(solution)/shard_map/ffn_in_backward/pallas_call | solution.py:509
  288.6 8.8 %conv_out_backward.1 = (bf16[2,256,1024]{2,1,0:T(8,128)(2,1)}, bf16[2,1,1024,256]{3,2,1,0:T(8,128)(2,1)}, bf16[2,1,1024,256]{3,2,1,0:T(8,128)(2,1)}, f32[34,1024]{1,0:T(8,128)}) custom-call(s32[10]{0:T(128)} %concatenate.71.meta, f32[256,1024]{1,0:T(8,128)} %get-tuple-element.367.grad, f32[2,256,1024]{2,1,0:T(8,128)} %get-tuple-element.368.wide, ...), custom_call_target="tpu_custom_call" | custom-call | flops 1073741824 | bytes 10485760 | tf_op jit(solution)/shard_map/conv_out_backward/pallas_call | solution.py:906
  297.5 6.4 collective-permute-done.48
  312.1 7.1 %conv_in_backward.1 = (f32[256,1024]{1,0:T(8,128)}, bf16[2,2,1024,256]{3,2,1,0:T(8,128)(2,1)}, bf16[2,2,1024,256]{3,2,1,0:T(8,128)(2,1)}, f32[34,1024]{1,0:T(8,128)}) custom-call(s32[10]{0:T(128)} %concatenate.71.meta, f32[256,1024]{1,0:T(8,128)} %get-tuple-element.367.grad, f32[256,1024]{1,0:T(8,128)} %get-tuple-element.320.stream, ...), custom_call_target="tpu_custom_call" | custom-call | flops 2147483648 | bytes 12582912 | tf_op jit(solution)/shard_map/conv_in_backward/pallas_call | solution.py:906
  319.2 9.7 %attention_heads_backward.1 = (bf16[3,256,1024]{2,1,0:T(8,128)(2,1)}, bf16[2,1,1024,256]{3,2,1,0:T(8,128)(2,1)}, bf16[2,1,1024,256]{3,2,1,0:T(8,128)(2,1)}, f32[34,1024]{1,0:T(8,128)}) custom-call(s32[10]{0:T(128)} %concatenate.71.meta, f32[256,1024]{1,0:T(8,128)} %get-tuple-element.386.grad, bf16[256,1024]{1,0:T(8,128)(2,1)} %get-tuple-element.387.queries, ...), custom_call_target="tpu_custom_call" | custom-call | flops 1610612736 | bytes 10485760 | tf_op jit(solution)/shard_map/attention_heads_backward/pallas_call | solution.py:906
  340.8 9.4 %attention_in_backward.1 = (f32[256,1024]{1,0:T(8,128)}, bf16[2,3,1024,256]{3,2,1,0:T(8,128)(2,1)}, bf16[2,3,1024,256]{3,2,1,0:T(8,128)(2,1)}, f32[34,1024]{1,0:T(8,128)}, bf16[256,1024]{1,0:T(8,128)(2,1)}) custom-call(s32[10]{0:T(128)} %concatenate.71.meta, f32[256,1024]{1,0:T(8,128)} %get-tuple-element.386.grad, f32[256,1024]{1,0:T(8,128)} %multiply_add_fusion.3.stream, ...), custom_call_target="tpu_custom_call" | custom-call | flops 3221225472 | bytes 14680064 | tf_op jit(solution)/shard_map/attention_in_backward/pallas_call | solution.py:906
  350.3 7.6 %collective-permute-done.53.refs_1_ = bf16[12,128,256]{2,1,0:T(8,128)(2,1)S(1)} collective-permute-done((bf16[12,128,256]{2,1,0:T(8,128)(2,1)}, bf16[12,128,256]{2,1,0:T(8,128)(2,1)S(1)}, u32[]{:S(2)}, u32[]{:S(2)}) %collective-permute-start.53) | collective-permute-done | bytes 786464 | tf_op jit(solution)/shard_map/ppermute | solution.py:110
  365.6 11.1 %collective-permute-done.57 = bf16[256,1024]{1,0:T(8,128)(2,1)S(1)} collective-permute-done((bf16[256,1024]{1,0:T(8,128)(2,1)S(1)}, bf16[256,1024]{1,0:T(8,128)(2,1)S(1)}, u32[]{:S(2)}, u32[]{:S(2)}) %collective-permute-start.57) | collective-permute-done | bytes 524320 | tf_op jit(solution)/shard_map/ppermute | solution.py:110
  390.6 11.3 %ffn_out_backward.3 = (bf16[1,1024,1024]{2,1,0:T(8,128)(2,1)}, f32[34,1024]{1,0:T(8,128)}, bf16[2,2,1,1024,256]{4,3,2,1,0:T(8,128)(2,1)}) custom-call(s32[11]{0:T(128)} %concatenate.79.meta, f32[1,1024,1024]{2,1,0:T(8,128)} %get-tuple-element.425.hidden, bf16[1,1024,1024]{2,1,0:T(8,128)(2,1)} %get-tuple-element.426.active, ...), custom_call_target="tpu_custom_call" | custom-call | flops 4294967296 | bytes 25165824 | tf_op jit(solution)/shard_map/ffn_out_backward/pallas_call | solution.py:509
  410.3 9.4 %ffn_in_backward.3 = (f32[512,1024]{1,0:T(8,128)}, bf16[512,1024]{1,0:T(8,128)(2,1)}, bf16[2,2,1,1024,256]{4,3,2,1,0:T(8,128)(2,1)}) custom-call(s32[11]{0:T(128)} %concatenate.79.meta, bf16[1024,1024]{1,0:T(8,128)(2,1)} %pad_maximum_fusion.4.normed, bf16[1,1024,1024]{2,1,0:T(8,128)(2,1)} %get-tuple-element.444.low, bf16[2,128,1024]{2,1,0:T(8,128)(2,1)} %copy-done.41, ...), custom_call_target="tpu_custom_call" | custom-call | flops 4294967296 | bytes 25165824 | tf_op jit(solution)/shard_map/ffn_in_backward/pallas_call | solution.py:509
  419.7 10.5 %collective-permute-done.63.refs_5_ = bf16[16,128,256]{2,1,0:T(8,128)(2,1)} collective-permute-done((bf16[16,128,256]{2,1,0:T(8,128)(2,1)}, bf16[16,128,256]{2,1,0:T(8,128)(2,1)}, u32[]{:S(2)}, u32[]{:S(2)}) %collective-permute-start.63) | collective-permute-done | bytes 1048608 | tf_op jit(solution)/shard_map/ppermute | solution.py:110
  434.0 5.1 hop.16
  450.0 22.3 %collective-permute-done.66.refs_4_ = bf16[19,128,256]{2,1,0:T(8,128)(2,1)} collective-permute-done((bf16[19,128,256]{2,1,0:T(8,128)(2,1)}, bf16[19,128,256]{2,1,0:T(8,128)(2,1)}, u32[]{:S(2)}, u32[]{:S(2)}) %collective-permute-start.66) | collective-permute-done | bytes 1245216 | tf_op jit(solution)/shard_map/ppermute | solution.py:110
  472.4 4.5 collective-permute-done.67.refs_5_
  477.9 4.9 hop.17
  490.9 20.4 %collective-permute-done.71.refs_4_ = bf16[19,128,256]{2,1,0:T(8,128)(2,1)S(1)} collective-permute-done((bf16[19,128,256]{2,1,0:T(8,128)(2,1)}, bf16[19,128,256]{2,1,0:T(8,128)(2,1)S(1)}, u32[]{:S(2)}, u32[]{:S(2)}) %collective-permute-start.71) | collective-permute-done | bytes 1245216 | tf_op jit(solution)/shard_map/ppermute | solution.py:110
  524.3 9.4 %collective-permute-done.75.refs_3_ = bf16[11,128,256]{2,1,0:T(8,128)(2,1)S(1)} collective-permute-done((bf16[11,128,256]{2,1,0:T(8,128)(2,1)}, bf16[11,128,256]{2,1,0:T(8,128)(2,1)S(1)}, u32[]{:S(2)}, u32[]{:S(2)}) %collective-permute-start.75) | collective-permute-done | bytes 720928 | tf_op jit(solution)/shard_map/ppermute | solution.py:110
  533.7 4.5 collective-permute-done.76.refs_4_
  555.5 6.7 collective-permute-done.80
  572.2 5.0 all-to-all-start
  579.2 5.5 collective-permute-done.83
  587.3 7.3 %collective-permute-done.84 = f32[34,1024]{1,0:T(8,128)S(1)} collective-permute-done((f32[34,1024]{1,0:T(8,128)S(1)}, f32[34,1024]{1,0:T(8,128)S(1)}, u32[]{:S(2)}, u32[]{:S(2)}) %collective-permute-start.84) | collective-permute-done | bytes 139296 | tf_op jit(solution)/shard_map/ppermute | solution.py:110
  594.6 19.1 %all-to-all-done = bf16[8,3,128,256]{3,2,1,0:T(8,128)(2,1)} async-done(((bf16[8,3,128,256]{3,2,1,0:T(8,128)(2,1)}), bf16[8,3,128,256]{3,2,1,0:T(8,128)(2,1)}, u32[]{:S(2)}, u32[]{:S(2)}) %all-to-all-start) | async-done | bytes 1572896 | tf_op jit(solution)/shard_map/all_to_all | solution.py:1374
  629.9 5.5 collective-permute-done.91
  638.1 4.3 fusion.43
  655.0 4.8 collective-permute-done.93
  (493 shorter events, 285.2 us)
Async XLA Ops:
  28.4 22.8 %collective-permute-start.4 = (bf16[7,128,512]{2,1,0:T(8,128)(2,1)S(1)}, bf16[7,128,512]{2,1,0:T(8,128)(2,1)S(1)}, u32[]{:S(2)}, u32[]{:S(2)}) collective-permute-start(bf16[7,128,512]{2,1,0:T(8,128)(2,1)S(1)} %constant_dynamic-slice_fusion.3.refs_0_), channel_id=1, source_target_pairs={{0,2},{2,4},{4,6},{6,7},{7,5},{5,3},{3,1},{1,0},{8,10},{10,12},{12... | collective-permute-start | bytes 2752520 | tf_op jit(solution)/shard_map/ppermute | solution.py:110
  29.8 21.7 %collective-permute-start.5 = (bf16[7,128,512]{2,1,0:T(8,128)(2,1)S(1)}, bf16[7,128,512]{2,1,0:T(8,128)(2,1)S(1)}, u32[]{:S(2)}, u32[]{:S(2)}) collective-permute-start(bf16[7,128,512]{2,1,0:T(8,128)(2,1)S(1)} %constant_dynamic-slice_fusion.3.refs_0_), channel_id=1, source_target_pairs={{2,0},{4,2},{6,4},{7,6},{5,7},{3,5},{1,3},{0,1},{10,8},{12,10},{14... | collective-permute-start | bytes 2752520 | tf_op jit(solution)/shard_map/ppermute | solution.py:110
  29.9 21.6 %collective-permute-start.6 = (bf16[7,128,512]{2,1,0:T(8,128)(2,1)S(1)}, bf16[7,128,512]{2,1,0:T(8,128)(2,1)S(1)}, u32[]{:S(2)}, u32[]{:S(2)}) collective-permute-start(bf16[7,128,512]{2,1,0:T(8,128)(2,1)S(1)} %constant_dynamic-slice_fusion.3.refs_0_), channel_id=1, source_target_pairs={{0,8},{8,0},{1,9},{9,1},{2,10},{10,2},{3,11},{11,3},{4,12},{12,4},... | collective-permute-start | bytes 2752520 | tf_op jit(solution)/shard_map/ppermute | solution.py:110
  30.5 31.2 %collective-permute-start.7 = (bf16[2,128,1024]{2,1,0:T(8,128)(2,1)}, bf16[2,128,1024]{2,1,0:T(8,128)(2,1)S(1)}, u32[]{:S(2)}, u32[]{:S(2)}) collective-permute-start(bf16[2,128,1024]{2,1,0:T(8,128)(2,1)} %copy-done.61), channel_id=1, source_target_pairs={{0,2},{2,4},{4,6},{6,7},{7,5},{5,3},{3,1},{1,0},{8,10},{10,12},{12... | collective-permute-start | bytes 1572872 | tf_op jit(solution)/shard_map/ppermute | solution.py:110
  31.8 30.9 %collective-permute-start.8 = (bf16[2,128,1024]{2,1,0:T(8,128)(2,1)}, bf16[2,128,1024]{2,1,0:T(8,128)(2,1)S(1)}, u32[]{:S(2)}, u32[]{:S(2)}) collective-permute-start(bf16[2,128,1024]{2,1,0:T(8,128)(2,1)} %collective-permute-done.1.refs_2_), channel_id=1, source_target_pairs={{2,0},{4,2},{6,4},{7,6},{5,7},{3,5},{1,3},{0,1},{10,8},{12,10},{14... | collective-permute-start | bytes 1572872 | tf_op jit(solution)/shard_map/ppermute | solution.py:110
  51.5 21.4 %collective-permute-start.11 = (bf16[2,128,1024]{2,1,0:T(8,128)(2,1)S(1)}, bf16[2,128,1024]{2,1,0:T(8,128)(2,1)S(1)}, u32[]{:S(2)}, u32[]{:S(2)}) collective-permute-start(bf16[2,128,1024]{2,1,0:T(8,128)(2,1)S(1)} %copy-done.42), channel_id=1, source_target_pairs={{0,2},{2,4},{4,6},{6,7},{7,5},{5,3},{3,1},{1,0},{8,10},{10,12},{12... | collective-permute-start | bytes 1572872 | tf_op jit(solution)/shard_map/ppermute | solution.py:110
  63.0 23.6 %collective-permute-start.17 = (bf16[7,128,512]{2,1,0:T(8,128)(2,1)S(1)}, bf16[7,128,512]{2,1,0:T(8,128)(2,1)S(1)}, u32[]{:S(2)}, u32[]{:S(2)}) collective-permute-start(bf16[7,128,512]{2,1,0:T(8,128)(2,1)S(1)} %collective-permute-done.5.refs_2_), channel_id=1, source_target_pairs={{0,8},{8,0},{1,9},{9,1},{2,10},{10,2},{3,11},{11,3},{4,12},{12,4},... | collective-permute-start | bytes 2752520 | tf_op jit(solution)/shard_map/ppermute | solution.py:110
  64.4 22.2 %collective-permute-start.16 = (bf16[7,128,512]{2,1,0:T(8,128)(2,1)S(1)}, bf16[7,128,512]{2,1,0:T(8,128)(2,1)S(1)}, u32[]{:S(2)}, u32[]{:S(2)}) collective-permute-start(bf16[7,128,512]{2,1,0:T(8,128)(2,1)S(1)} %collective-permute-done.4.refs_1_), channel_id=1, source_target_pairs={{0,8},{8,0},{1,9},{9,1},{2,10},{10,2},{3,11},{11,3},{4,12},{12,4},... | collective-permute-start | bytes 2752520 | tf_op jit(solution)/shard_map/ppermute | solution.py:110
  64.4 19.8 %collective-permute-start.9 = (bf16[2,128,1024]{2,1,0:T(8,128)(2,1)S(1)}, bf16[2,128,1024]{2,1,0:T(8,128)(2,1)}, u32[]{:S(2)}, u32[]{:S(2)}) collective-permute-start(bf16[2,128,1024]{2,1,0:T(8,128)(2,1)S(1)} %collective-permute-done.7.refs_3_), channel_id=1, source_target_pairs={{0,2},{2,4},{4,6},{6,7},{7,5},{5,3},{3,1},{1,0},{8,10},{10,12},{12... | collective-permute-start | bytes 1572872 | tf_op jit(solution)/shard_map/ppermute | solution.py:110
  86.6 25.4 %collective-permute-start.20 = (bf16[7,128,512]{2,1,0:T(8,128)(2,1)S(1)}, bf16[7,128,512]{2,1,0:T(8,128)(2,1)}, u32[]{:S(2)}, u32[]{:S(2)}) collective-permute-start(bf16[7,128,512]{2,1,0:T(8,128)(2,1)S(1)} %collective-permute-done.5.refs_2_), channel_id=1, source_target_pairs={{2,0},{4,2},{6,4},{7,6},{5,7},{3,5},{1,3},{0,1},{10,8},{12,10},{14... | collective-permute-start | bytes 2752520 | tf_op jit(solution)/shard_map/ppermute | solution.py:110
  87.8 28.7 %collective-permute-start.18 = (bf16[7,128,512]{2,1,0:T(8,128)(2,1)S(1)}, bf16[7,128,512]{2,1,0:T(8,128)(2,1)}, u32[]{:S(2)}, u32[]{:S(2)}) collective-permute-start(bf16[7,128,512]{2,1,0:T(8,128)(2,1)S(1)} %collective-permute-done.4.refs_1_), channel_id=1, source_target_pairs={{0,2},{2,4},{4,6},{6,7},{7,5},{5,3},{3,1},{1,0},{8,10},{10,12},{12... | collective-permute-start | bytes 2752520 | tf_op jit(solution)/shard_map/ppermute | solution.py:110
  89.7 22.3 %collective-permute-start.22 = (bf16[2,128,1024]{2,1,0:T(8,128)(2,1)}, bf16[2,128,1024]{2,1,0:T(8,128)(2,1)S(1)}, u32[]{:S(2)}, u32[]{:S(2)}) collective-permute-start(bf16[2,128,1024]{2,1,0:T(8,128)(2,1)} %copy-done.68), channel_id=1, source_target_pairs={{0,16},{16,0},{1,17},{17,1},{2,18},{18,2},{3,19},{19,3},{4,20},{20... | collective-permute-start | bytes 1572872 | tf_op jit(solution)/shard_map/ppermute | solution.py:110
  106.3 22.0 %collective-permute-start.14 = (bf16[512,1024]{1,0:T(8,128)(2,1)}, bf16[512,1024]{1,0:T(8,128)(2,1)S(1)}, u32[]{:S(2)}, u32[]{:S(2)}) collective-permute-start(bf16[512,1024]{1,0:T(8,128)(2,1)} %get-tuple-element.286), channel_id=1, source_target_pairs={{0,8},{8,0},{1,9},{9,1},{2,10},{10,2},{3,11},{11,3},{4,12},{12,4},... | collective-permute-start | bytes 3145736 | tf_op jit(solution)/shard_map/ppermute | solution.py:321
  117.9 14.8 %collective-permute-start.27 = (bf16[7,128,512]{2,1,0:T(8,128)(2,1)}, bf16[7,128,512]{2,1,0:T(8,128)(2,1)S(1)}, u32[]{:S(2)}, u32[]{:S(2)}) collective-permute-start(bf16[7,128,512]{2,1,0:T(8,128)(2,1)} %collective-permute-done.20.refs_4_), channel_id=1, source_target_pairs={{0,8},{8,0},{1,9},{9,1},{2,10},{10,2},{3,11},{11,3},{4,12},{12,4},... | collective-permute-start | bytes 2752520 | tf_op jit(solution)/shard_map/ppermute | solution.py:110
  126.9 18.9 %collective-permute-start.21 = (bf16[7,128,512]{2,1,0:T(8,128)(2,1)}, bf16[7,128,512]{2,1,0:T(8,128)(2,1)S(1)}, u32[]{:S(2)}, u32[]{:S(2)}) collective-permute-start(bf16[7,128,512]{2,1,0:T(8,128)(2,1)} %collective-permute-done.20.refs_4_), channel_id=1, source_target_pairs={{2,0},{4,2},{6,4},{7,6},{5,7},{3,5},{1,3},{0,1},{10,8},{12,10},{14... | collective-permute-start | bytes 2752520 | tf_op jit(solution)/shard_map/ppermute | solution.py:110
  128.1 18.6 %collective-permute-start.19 = (bf16[7,128,512]{2,1,0:T(8,128)(2,1)}, bf16[7,128,512]{2,1,0:T(8,128)(2,1)}, u32[]{:S(2)}, u32[]{:S(2)}) collective-permute-start(bf16[7,128,512]{2,1,0:T(8,128)(2,1)} %collective-permute-done.18.refs_3_), channel_id=1, source_target_pairs={{0,2},{2,4},{4,6},{6,7},{7,5},{5,3},{3,1},{1,0},{8,10},{10,12},{12... | collective-permute-start | bytes 2752520 | tf_op jit(solution)/shard_map/ppermute | solution.py:110
  128.3 18.4 %collective-permute-start.24 = (bf16[2,128,1024]{2,1,0:T(8,128)(2,1)S(1)}, bf16[2,128,1024]{2,1,0:T(8,128)(2,1)S(1)}, u32[]{:S(2)}, u32[]{:S(2)}) collective-permute-start(bf16[2,128,1024]{2,1,0:T(8,128)(2,1)S(1)} %collective-permute-done.23.refs_3_), channel_id=1, source_target_pairs={{0,16},{16,0},{1,17},{17,1},{2,18},{18,2},{3,19},{19,3},{4,20},{20... | collective-permute-start | bytes 1572872 | tf_op jit(solution)/shard_map/ppermute | solution.py:110
  149.5 18.0 %collective-permute-start.28 = (bf16[256,1024]{1,0:T(8,128)(2,1)S(1)}, bf16[256,1024]{1,0:T(8,128)(2,1)S(1)}, u32[]{:S(2)}, u32[]{:S(2)}) collective-permute-start(bf16[256,1024]{1,0:T(8,128)(2,1)S(1)} %slice.314), channel_id=1, source_target_pairs={{0,16},{16,0},{1,17},{17,1},{2,18},{18,2},{3,19},{19,3},{4,20},{20... | collective-permute-start | bytes 1572872 | tf_op jit(solution)/shard_map/ppermute | solution.py:110
  149.7 29.5 %collective-permute-start.34 = (bf16[7,128,512]{2,1,0:T(8,128)(2,1)S(1)}, bf16[7,128,512]{2,1,0:T(8,128)(2,1)}, u32[]{:S(2)}, u32[]{:S(2)}) collective-permute-start(bf16[7,128,512]{2,1,0:T(8,128)(2,1)S(1)} %collective-permute-done.21.refs_6_), channel_id=1, source_target_pairs={{2,0},{4,2},{6,4},{7,6},{5,7},{3,5},{1,3},{0,1},{10,8},{12,10},{14... | collective-permute-start | bytes 2752520 | tf_op jit(solution)/shard_map/ppermute | solution.py:110
  168.7 25.0 %collective-permute-start.36 = (bf16[7,128,512]{2,1,0:T(8,128)(2,1)S(1)}, bf16[7,128,512]{2,1,0:T(8,128)(2,1)}, u32[]{:S(2)}, u32[]{:S(2)}) collective-permute-start(bf16[7,128,512]{2,1,0:T(8,128)(2,1)S(1)} %collective-permute-done.21.refs_6_), channel_id=1, source_target_pairs={{0,8},{8,0},{1,9},{9,1},{2,10},{10,2},{3,11},{11,3},{4,12},{12,4},... | collective-permute-start | bytes 2752520 | tf_op jit(solution)/shard_map/ppermute | solution.py:110
  179.2 14.5 %collective-permute-start.35 = (bf16[7,128,512]{2,1,0:T(8,128)(2,1)}, bf16[7,128,512]{2,1,0:T(8,128)(2,1)}, u32[]{:S(2)}, u32[]{:S(2)}) collective-permute-start(bf16[7,128,512]{2,1,0:T(8,128)(2,1)} %collective-permute-done.19.refs_5_), channel_id=1, source_target_pairs={{0,8},{8,0},{1,9},{9,1},{2,10},{10,2},{3,11},{11,3},{4,12},{12,4},... | collective-permute-start | bytes 2752520 | tf_op jit(solution)/shard_map/ppermute | solution.py:110
  188.1 15.1 %collective-permute-start.39 = (bf16[2,128,1024]{2,1,0:T(8,128)(2,1)}, bf16[2,128,1024]{2,1,0:T(8,128)(2,1)}, u32[]{:S(2)}, u32[]{:S(2)}) collective-permute-start(bf16[2,128,1024]{2,1,0:T(8,128)(2,1)} %collective-permute-done.29.refs_5_), channel_id=1, source_target_pairs={{0,16},{16,0},{1,17},{17,1},{2,18},{18,2},{3,19},{19,3},{4,20},{20... | collective-permute-start | bytes 1572872 | tf_op jit(solution)/shard_map/ppermute | solution.py:110
  188.1 25.1 %collective-permute-start.38 = (bf16[2,128,1024]{2,1,0:T(8,128)(2,1)}, bf16[2,128,1024]{2,1,0:T(8,128)(2,1)}, u32[]{:S(2)}, u32[]{:S(2)}) collective-permute-start(bf16[2,128,1024]{2,1,0:T(8,128)(2,1)} %collective-permute-done.32.refs_7_), channel_id=1, source_target_pairs={{0,16},{16,0},{1,17},{17,1},{2,18},{18,2},{3,19},{19,3},{4,20},{20... | collective-permute-start | bytes 1572872 | tf_op jit(solution)/shard_map/ppermute | solution.py:110
  280.1 23.8 %collective-permute-start.48 = (bf16[2,1024,256]{2,1,0:T(8,128)(2,1)S(1)}, bf16[2,1024,256]{2,1,0:T(8,128)(2,1)S(1)}, u32[]{:S(2)}, u32[]{:S(2)}) collective-permute-start(bf16[2,1024,256]{2,1,0:T(8,128)(2,1)S(1)} %copy-done.59), channel_id=1, source_target_pairs={{0,16},{16,0},{1,17},{17,1},{2,18},{18,2},{3,19},{19,3},{4,20},{20... | collective-permute-start | bytes 3145736 | tf_op jit(solution)/shard_map/ppermute | solution.py:110
  281.4 16.1 %collective-permute-start.46 = (bf16[8,128,256]{2,1,0:T(8,128)(2,1)}, bf16[8,128,256]{2,1,0:T(8,128)(2,1)S(1)}, u32[]{:S(2)}, u32[]{:S(2)}) collective-permute-start(bf16[8,128,256]{2,1,0:T(8,128)(2,1)} %get-tuple-element.372), channel_id=1, source_target_pairs={{0,2},{2,4},{4,6},{6,7},{7,5},{5,3},{3,1},{1,0},{8,10},{10,12},{12... | collective-permute-start | bytes 1572872 | tf_op jit(solution)/shard_map/ppermute | solution.py:110
  282.7 14.8 %collective-permute-start.47 = (bf16[8,128,256]{2,1,0:T(8,128)(2,1)}, bf16[8,128,256]{2,1,0:T(8,128)(2,1)S(1)}, u32[]{:S(2)}, u32[]{:S(2)}) collective-permute-start(bf16[8,128,256]{2,1,0:T(8,128)(2,1)} %get-tuple-element.373), channel_id=1, source_target_pairs={{2,0},{4,2},{6,4},{7,6},{5,7},{3,5},{1,3},{0,1},{10,8},{12,10},{14... | collective-permute-start | bytes 1572872 | tf_op jit(solution)/shard_map/ppermute | solution.py:110
  307.4 22.9 %collective-permute-start.51 = (bf16[2,1024,256]{2,1,0:T(8,128)(2,1)S(1)}, bf16[2,1024,256]{2,1,0:T(8,128)(2,1)S(1)}, u32[]{:S(2)}, u32[]{:S(2)}) collective-permute-start(bf16[2,1024,256]{2,1,0:T(8,128)(2,1)S(1)} %copy-done.57), channel_id=1, source_target_pairs={{0,16},{16,0},{1,17},{17,1},{2,18},{18,2},{3,19},{19,3},{4,20},{20... | collective-permute-start | bytes 3145736 | tf_op jit(solution)/shard_map/ppermute | solution.py:110
  307.5 22.8 %collective-permute-start.52 = (bf16[2,1,1024,256]{3,2,1,0:T(8,128)(2,1)}, bf16[2,1,1024,256]{3,2,1,0:T(8,128)(2,1)S(1)}, u32[]{:S(2)}, u32[]{:S(2)}) collective-permute-start(bf16[2,1,1024,256]{3,2,1,0:T(8,128)(2,1)} %get-tuple-element.396), channel_id=1, source_target_pairs={{0,8},{8,0},{1,9},{9,1},{2,10},{10,2},{3,11},{11,3},{4,12},{12,4},... | collective-permute-start | bytes 3145736 | tf_op jit(solution)/shard_map/ppermute | solution.py:110
  309.6 19.3 %collective-permute-start.49 = (bf16[8,128,256]{2,1,0:T(8,128)(2,1)}, bf16[8,128,256]{2,1,0:T(8,128)(2,1)S(1)}, u32[]{:S(2)}, u32[]{:S(2)}) collective-permute-start(bf16[8,128,256]{2,1,0:T(8,128)(2,1)} %get-tuple-element.393), channel_id=1, source_target_pairs={{0,2},{2,4},{4,6},{6,7},{7,5},{5,3},{3,1},{1,0},{8,10},{10,12},{12... | collective-permute-start | bytes 1572872 | tf_op jit(solution)/shard_map/ppermute | solution.py:110
  310.3 18.6 %collective-permute-start.50 = (bf16[8,128,256]{2,1,0:T(8,128)(2,1)}, bf16[8,128,256]{2,1,0:T(8,128)(2,1)S(1)}, u32[]{:S(2)}, u32[]{:S(2)}) collective-permute-start(bf16[8,128,256]{2,1,0:T(8,128)(2,1)} %get-tuple-element.394), channel_id=1, source_target_pairs={{2,0},{4,2},{6,4},{7,6},{5,7},{3,5},{1,3},{0,1},{10,8},{12,10},{14... | collective-permute-start | bytes 1572872 | tf_op jit(solution)/shard_map/ppermute | solution.py:110
  335.4 22.5 %collective-permute-start.55 = (bf16[2,2,1024,256]{3,2,1,0:T(8,128)(2,1)}, bf16[2,2,1024,256]{3,2,1,0:T(8,128)(2,1)S(1)}, u32[]{:S(2)}, u32[]{:S(2)}) collective-permute-start(bf16[2,2,1024,256]{3,2,1,0:T(8,128)(2,1)} %get-tuple-element.410), channel_id=1, source_target_pairs={{0,8},{8,0},{1,9},{9,1},{2,10},{10,2},{3,11},{11,3},{4,12},{12,4},... | collective-permute-start | bytes 6291464 | tf_op jit(solution)/shard_map/ppermute | solution.py:110
  338.3 19.6 %collective-permute-start.56 = (bf16[2,1,1024,256]{3,2,1,0:T(8,128)(2,1)S(1)}, bf16[2,1,1024,256]{3,2,1,0:T(8,128)(2,1)S(1)}, u32[]{:S(2)}, u32[]{:S(2)}) collective-permute-start(bf16[2,1,1024,256]{3,2,1,0:T(8,128)(2,1)S(1)} %copy-done.58), channel_id=1, source_target_pairs={{0,8},{8,0},{1,9},{9,1},{2,10},{10,2},{3,11},{11,3},{4,12},{12,4},... | collective-permute-start | bytes 3145736 | tf_op jit(solution)/shard_map/ppermute | solution.py:110
  338.4 19.5 %collective-permute-start.53 = (bf16[12,128,256]{2,1,0:T(8,128)(2,1)}, bf16[12,128,256]{2,1,0:T(8,128)(2,1)S(1)}, u32[]{:S(2)}, u32[]{:S(2)}) collective-permute-start(bf16[12,128,256]{2,1,0:T(8,128)(2,1)} %get-tuple-element.408), channel_id=1, source_target_pairs={{0,2},{2,4},{4,6},{6,7},{7,5},{5,3},{3,1},{1,0},{8,10},{10,12},{12... | collective-permute-start | bytes 2359304 | tf_op jit(solution)/shard_map/ppermute | solution.py:110
  362.2 19.4 %collective-permute-start.59 = (bf16[2,3,1024,256]{3,2,1,0:T(8,128)(2,1)}, bf16[2,3,1024,256]{3,2,1,0:T(8,128)(2,1)}, u32[]{:S(2)}, u32[]{:S(2)}) collective-permute-start(bf16[2,3,1024,256]{3,2,1,0:T(8,128)(2,1)} %get-tuple-element.421), channel_id=1, source_target_pairs={{0,8},{8,0},{1,9},{9,1},{2,10},{10,2},{3,11},{11,3},{4,12},{12,4},... | collective-permute-start | bytes 9437192 | tf_op jit(solution)/shard_map/ppermute | solution.py:110
  406.6 23.5 %collective-permute-start.63 = (bf16[16,128,256]{2,1,0:T(8,128)(2,1)}, bf16[16,128,256]{2,1,0:T(8,128)(2,1)}, u32[]{:S(2)}, u32[]{:S(2)}) collective-permute-start(bf16[16,128,256]{2,1,0:T(8,128)(2,1)} %get-tuple-element.447), channel_id=1, source_target_pairs={{0,2},{2,4},{4,6},{6,7},{7,5},{5,3},{3,1},{1,0},{8,10},{10,12},{12... | collective-permute-start | bytes 3145736 | tf_op jit(solution)/shard_map/ppermute | solution.py:110
  406.7 23.7 %collective-permute-start.64 = (bf16[16,128,256]{2,1,0:T(8,128)(2,1)}, bf16[16,128,256]{2,1,0:T(8,128)(2,1)}, u32[]{:S(2)}, u32[]{:S(2)}) collective-permute-start(bf16[16,128,256]{2,1,0:T(8,128)(2,1)} %get-tuple-element.448), channel_id=1, source_target_pairs={{2,0},{4,2},{6,4},{7,6},{5,7},{3,5},{1,3},{0,1},{10,8},{12,10},{14... | collective-permute-start | bytes 3145736 | tf_op jit(solution)/shard_map/ppermute | solution.py:110
  408.3 23.0 %collective-permute-start.65 = (bf16[2,1024,256]{2,1,0:T(8,128)(2,1)}, bf16[2,1024,256]{2,1,0:T(8,128)(2,1)}, u32[]{:S(2)}, u32[]{:S(2)}) collective-permute-start(bf16[2,1024,256]{2,1,0:T(8,128)(2,1)} %slice_bitcast_fusion), channel_id=1, source_target_pairs={{0,16},{16,0},{1,17},{17,1},{2,18},{18,2},{3,19},{19,3},{4,20},{20... | collective-permute-start | bytes 3145736 | tf_op jit(solution)/shard_map/ppermute | solution.py:110
  442.1 34.8 %collective-permute-start.67 = (bf16[23,128,256]{2,1,0:T(8,128)(2,1)}, bf16[23,128,256]{2,1,0:T(8,128)(2,1)S(1)}, u32[]{:S(2)}, u32[]{:S(2)}) collective-permute-start(bf16[23,128,256]{2,1,0:T(8,128)(2,1)} %get-tuple-element.460), channel_id=1, source_target_pairs={{2,0},{4,2},{6,4},{7,6},{5,7},{3,5},{1,3},{0,1},{10,8},{12,10},{14... | collective-permute-start | bytes 4521992 | tf_op jit(solution)/shard_map/ppermute | solution.py:110
  443.4 28.9 %collective-permute-start.66 = (bf16[19,128,256]{2,1,0:T(8,128)(2,1)}, bf16[19,128,256]{2,1,0:T(8,128)(2,1)}, u32[]{:S(2)}, u32[]{:S(2)}) collective-permute-start(bf16[19,128,256]{2,1,0:T(8,128)(2,1)} %get-tuple-element.459), channel_id=1, source_target_pairs={{0,2},{2,4},{4,6},{6,7},{7,5},{5,3},{3,1},{1,0},{8,10},{10,12},{12... | collective-permute-start | bytes 3735560 | tf_op jit(solution)/shard_map/ppermute | solution.py:110
  446.6 30.2 %collective-permute-start.69 = (bf16[256,1024]{1,0:T(8,128)(2,1)}, bf16[256,1024]{1,0:T(8,128)(2,1)}, u32[]{:S(2)}, u32[]{:S(2)}) collective-permute-start(bf16[256,1024]{1,0:T(8,128)(2,1)} %slice.313), channel_id=1, source_target_pairs={{0,16},{16,0},{1,17},{17,1},{2,18},{18,2},{3,19},{19,3},{4,20},{20... | collective-permute-start | bytes 1572872 | tf_op jit(solution)/shard_map/ppermute | solution.py:110
  482.9 28.4 %collective-permute-start.71 = (bf16[19,128,256]{2,1,0:T(8,128)(2,1)}, bf16[19,128,256]{2,1,0:T(8,128)(2,1)S(1)}, u32[]{:S(2)}, u32[]{:S(2)}) collective-permute-start(bf16[19,128,256]{2,1,0:T(8,128)(2,1)} %get-tuple-element.475), channel_id=1, source_target_pairs={{0,2},{2,4},{4,6},{6,7},{7,5},{5,3},{3,1},{1,0},{8,10},{10,12},{12... | collective-permute-start | bytes 3735560 | tf_op jit(solution)/shard_map/ppermute | solution.py:110
  483.0 28.3 %collective-permute-start.72 = (bf16[19,128,256]{2,1,0:T(8,128)(2,1)}, bf16[19,128,256]{2,1,0:T(8,128)(2,1)}, u32[]{:S(2)}, u32[]{:S(2)}) collective-permute-start(bf16[19,128,256]{2,1,0:T(8,128)(2,1)} %get-tuple-element.476), channel_id=1, source_target_pairs={{2,0},{4,2},{6,4},{7,6},{5,7},{3,5},{1,3},{0,1},{10,8},{12,10},{14... | collective-permute-start | bytes 3735560 | tf_op jit(solution)/shard_map/ppermute | solution.py:110
  516.3 21.9 %collective-permute-start.76 = (bf16[15,128,256]{2,1,0:T(8,128)(2,1)}, bf16[15,128,256]{2,1,0:T(8,128)(2,1)S(1)}, u32[]{:S(2)}, u32[]{:S(2)}) collective-permute-start(bf16[15,128,256]{2,1,0:T(8,128)(2,1)} %get-tuple-element.482), channel_id=1, source_target_pairs={{2,0},{4,2},{6,4},{7,6},{5,7},{3,5},{1,3},{0,1},{10,8},{12,10},{14... | collective-permute-start | bytes 2949128 | tf_op jit(solution)/shard_map/ppermute | solution.py:110
  517.7 15.9 %collective-permute-start.75 = (bf16[11,128,256]{2,1,0:T(8,128)(2,1)}, bf16[11,128,256]{2,1,0:T(8,128)(2,1)S(1)}, u32[]{:S(2)}, u32[]{:S(2)}) collective-permute-start(bf16[11,128,256]{2,1,0:T(8,128)(2,1)} %get-tuple-element.481), channel_id=1, source_target_pairs={{0,2},{2,4},{4,6},{6,7},{7,5},{5,3},{3,1},{1,0},{8,10},{10,12},{12... | collective-permute-start | bytes 2162696 | tf_op jit(solution)/shard_map/ppermute | solution.py:110
  572.2 41.5 %all-to-all-start = ((bf16[8,3,128,256]{3,2,1,0:T(8,128)(2,1)}), bf16[8,3,128,256]{3,2,1,0:T(8,128)(2,1)}, u32[]{:S(2)}, u32[]{:S(2)}) async-start(bf16[8,3,128,256]{3,2,1,0:T(8,128)(2,1)} %bitcast.369), calls=%async_computation | async-start | bytes 3145728 | tf_op jit(solution)/shard_map/all_to_all | solution.py:1374
  624.7 20.2 %collective-permute-start.86 = (f32[34,1024]{1,0:T(8,128)S(1)}, f32[34,1024]{1,0:T(8,128)S(1)}, u32[]{:S(2)}, u32[]{:S(2)}) collective-permute-start(f32[34,1024]{1,0:T(8,128)S(1)} %add.722), channel_id=1, source_target_pairs={{0,4},{1,5},{2,6},{3,7},{4,0},{5,1},{6,2},{7,3},{8,12},{9,13},{10,... | collective-permute-start | bytes 417800 | tf_op jit(solution)/shard_map/ppermute | solution.py:110
  652.9 26.9 %collective-permute-start.95 = (bf16[256,1024]{1,0:T(8,128)(2,1)}, bf16[256,1024]{1,0:T(8,128)(2,1)}, u32[]{:S(2)}, u32[]{:S(2)}) collective-permute-start(bf16[256,1024]{1,0:T(8,128)(2,1)} %fusion.49), channel_id=1, source_target_pairs={{0,16},{16,0},{1,17},{17,1},{2,18},{18,2},{3,19},{19,3},{4,20},{20... | collective-permute-start | bytes 1572872 | tf_op jit(solution)/shard_map/ppermute | solution.py:327
  662.1 24.7 %collective-permute-start.94 = (bf16[2,256,1024]{2,1,0:T(8,128)(2,1)}, bf16[2,256,1024]{2,1,0:T(8,128)(2,1)}, u32[]{:S(2)}, u32[]{:S(2)}) collective-permute-start(bf16[2,256,1024]{2,1,0:T(8,128)(2,1)} %pad_maximum_fusion.9), channel_id=1, source_target_pairs={{0,8},{8,0},{1,9},{9,1},{2,10},{10,2},{3,11},{11,3},{4,12},{12,4},... | collective-permute-start | bytes 3145736 | tf_op jit(solution)/shard_map/ppermute | solution.py:327
  (135 other events, 1439.3 us)
